TPU v7x, 256 devices: a whole 4x4x8 slice. The times are simulated.
256 devices in a mesh: front: 16 (over z, x_hi), row: 4 (over y), col: 4 (over x_lo, core).
Axes of the slice: x: 4 (x_hi: 2, x_lo: 2; x = x_hi * 2 + x_lo), y: 4, z: 8, core: 2. Of those that a mesh axis runs over, the one named last changes fastest.
Arguments:
- front_matrix: bfloat16 [16, 6144, 6144], P('front', 'row', 'col'), may hold values from -32 to 32, as said below
- kept_child: bfloat16 [16, 2048, 2048], P('front', 'row', 'col'), may hold values from -32 to 32, as said below
- passed_child: bfloat16 [16, 2048, 2048], P('front', 'row', 'col'), may hold values from -32 to 32, as said below
- child_map: int32 [16, 2, 16], P('front'), may hold values from 0 to 47, as said below
- pivots: int32 [16, 2, 4], P('front'), may hold values from 0 to 47, as said below
- pivot_inverse: bfloat16 [16, 2, 512, 512], P('front'), may hold values from -0.03125 to 0.03125, as said below
Outputs:
- updated: bfloat16 [16, 6144, 6144], P('front', 'row', 'col')
Inputs may be any that keep to these rules, and one draw needn't show every extreme that they name: `front_matrix`: symmetric in its last two dimensions. `kept_child`: symmetric in its last two dimensions. `passed_child`: symmetric in its last two dimensions. `pivot_inverse`: symmetric in its last two dimensions. `child_map`: within each front and map the entries differ; child block a maps to a parent block p with p // (48 // 4) == a // (16 // 4). `pivots`: entry j of each step lies in block-column range [j * 48 // 4, (j + 1) * 48 // 4); no block is a pivot block twice within a front.
All inputs are finite; a program needn't handle non-finite values.
Results may differ from a plain program's by a relative error of at most 0.0067.
Values may be sent and summed in bfloat16 or wider, within the bound.
No kernel may reach another device: no remote copies, remote signals or barrier semaphores. Data moves between devices by JAX's collectives and lax.ppermute only.
A program may use at most 128 MiB of HBM per device.

v0:
```python
import jax
import jax.numpy as jnp
from jax import lax
from jax.sharding import PartitionSpec as P

BLK = 128
P_SIZE = 512
STEPS = 2


def from_partner(block, axis, bit):
    count = lax.axis_size(axis)
    route = []
    for low in range(count):
        high = low | 1 << bit
        if high != low and high < count:
            route += [(low, high), (high, low)]
    return lax.ppermute(block, axis, route)


def extend_add(child, row_map, col_map, blocks_here):
    child_blocks = row_map.shape[0]
    targets = jnp.arange(blocks_here, dtype=jnp.int32)
    row_pick = (row_map[:, None] == targets[None, :]).astype(jnp.bfloat16)
    col_pick = (col_map[:, None] == targets[None, :]).astype(jnp.bfloat16)
    pieces = child.reshape(child_blocks, BLK, child_blocks, BLK)
    partial_rows = jnp.einsum(
        "ap,aibj->pibj", row_pick, pieces, preferred_element_type=jnp.float32
    ).astype(jnp.bfloat16)
    placed = jnp.einsum("pibj,bq->piqj", partial_rows, col_pick, preferred_element_type=jnp.float32)
    return placed.reshape(blocks_here * BLK, blocks_here * BLK)


def local_map(mapping, shard, child_blocks, blocks_here):
    return (
        lax.dynamic_slice_in_dim(mapping, shard * child_blocks, child_blocks) - shard * blocks_here
    )


def body(front_matrix, kept_child, passed_child, child_map, pivots, pivot_inverse):
    row_id = lax.axis_index("row")
    col_id = lax.axis_index("col")
    width_cols = lax.axis_size("col")
    span = front_matrix.shape[1]
    blocks_here = span // BLK
    child_blocks = kept_child.shape[1] // BLK
    arrived = from_partner(passed_child, "front", 0)
    parent_maps = child_map[0]
    current = front_matrix[0].astype(jnp.float32)
    for which, child in ((0, kept_child[0]), (1, arrived[0])):
        row_map = local_map(parent_maps[which], row_id, child_blocks, blocks_here)
        col_map = local_map(parent_maps[which], col_id, child_blocks, blocks_here)
        current = current + extend_add(child, row_map, col_map, blocks_here)
    within_piece = None
    for section in range(STEPS):
        local_block = (
            lax.dynamic_index_in_dim(pivots[0, section], col_id, keepdims=False)
            - col_id * blocks_here
        )
        column_piece = lax.dynamic_slice_in_dim(current, local_block * BLK, BLK, 1).astype(
            jnp.bfloat16
        )
        gathered = lax.all_gather(column_piece[None], ("row", "col"), axis=0, tiled=True)
        own_rows = lax.dynamic_slice_in_dim(gathered, row_id * width_cols, width_cols, 0)
        opposite = lax.dynamic_slice_in_dim(gathered, col_id * width_cols, width_cols, 0)
        inverse_now = pivot_inverse[0, section].reshape(width_cols, BLK, P_SIZE)
        multipliers = jnp.einsum(
            "jik,jkl->il", own_rows, inverse_now, preferred_element_type=jnp.float32
        ).astype(jnp.bfloat16)
        pattern = "ijk,jmk->im"
        stacked = multipliers.reshape(span, width_cols, BLK)
        within_piece = None
        current = current - jnp.einsum(
            pattern, stacked, opposite, preferred_element_type=jnp.float32
        )
    return current.astype(jnp.bfloat16)[None]


def solution(mesh):
    in_specs = (
        P("front", "row", "col"),
        P("front", "row", "col"),
        P("front", "row", "col"),
        P("front", None, None),
        P("front", None, None),
        P("front", None, None, None),
    )
    out_specs = P("front", "row", "col")
    return jax.shard_map(body, mesh=mesh, in_specs=in_specs, out_specs=out_specs, check_vma=False)
```

profile of v0, /device:TPU:1, one launch (start us, length us, event | category | flops | bytes accessed | tf_op | source)
XLA Modules:
  0.0 174.8 jit_solution(3811665563908067030)
XLA Ops:
  6.5 3.6 %collective-permute-start = (bf16[1,512,512]{2,1,0:T(8,128)(2,1)}, bf16[1,512,512]{2,1,0:T(8,128)(2,1)S(1)}, u32[]{:S(2)}, u32[]{:S(2)}) collective-permute-start(bf16[1,512,512]{2,1,0:T(8,128)(2,1)} %param.8), channel_id=1, source_target_pairs={{0,16},{16,0},{32,48},{48,32},{64,80},{80,64},{96,112},{112,96},{1... | collective-permute-start | bytes 1572872 | tf_op jit(solution)/shard_map/ppermute | solution.py:18
  10.1 0.8 fusion.40
  11.0 1.2 reshape_squeeze.12
  12.2 0.8 fusion.39
  13.0 0.6 constant_dynamic-slice_fusion
  14.2 0.9 fusion.12
  15.1 5.6 %fusion.4 = f32[12,12,128,128]{3,0,2,1:T(8,128)} fusion(bf16[12,128,4,128]{3,0,2,1:T(8,128)(2,1)S(1)} %fusion.12, s32[4]{0:T(128)S(1)} %get-tuple-element.11), kind=kOutput, calls=%fused_computation.12 | convolution fusion | flops 18874416 | bytes 11010064 | tf_op jit(solution)/shard_map/pibj,bq->piqj/dot_general | solution.py:30
  20.8 0.2 collective-permute-done
  21.0 0.1 reshape_squeeze.13
  21.1 0.9 fusion.10
  22.1 7.0 %fusion.5 = f32[12,12,128,128]{3,0,2,1:T(8,128)} fusion(bf16[12,128,4,128]{3,0,2,1:T(8,128)(2,1)S(1)} %fusion.10, s32[4]{0:T(128)S(1)} %get-tuple-element.13), kind=kOutput, calls=%fused_computation.13 | convolution fusion | flops 18874416 | bytes 11010064 | tf_op jit(solution)/shard_map/pibj,bq->piqj/dot_general | solution.py:30
  29.1 1.9 %copy-done.1 = f32[12,12,128,128]{3,0,2,1:T(8,128)S(1)} copy-done((f32[12,12,128,128]{3,0,2,1:T(8,128)S(1)}, f32[12,12,128,128]{3,0,2,1:T(8,128)}, u32[]{:S(2)}) %copy-start.1) | copy-done | bytes 9437208
  30.9 14.0 %bitcast_add_fusion = f32[1536,1536]{1,0:T(8,128)S(1)} fusion(f32[192,8,12,128]{3,2,1,0:T(8,128)} %bitcast.74, f32[192,8,12,128]{3,2,1,0:T(8,128)S(1)} %bitcast.73, bf16[1,1536,1536]{2,1,0:T(8,128)(2,1)} %param.6), kind=kLoop, calls=%fused_computation | loop fusion | flops 7077888 | bytes 33030144 | tf_op jit(solution)/shard_map/add | solution.py:53
  44.9 3.6 %copy-done = f32[1536,1536]{1,0:T(8,128)} copy-done((f32[1536,1536]{1,0:T(8,128)}, f32[1536,1536]{1,0:T(8,128)S(1)}, u32[]{:S(2)}) %copy-start) | copy-done | bytes 9437208
  48.6 0.8 dynamic-slice_convert_fusion.1
  49.4 0.2 all-gather.7.cloned.1.call-start
  50.4 49.1 %all-gather.5.cloned.1.call-done = bf16[24576,128]{1,0:T(8,128)(2,1)} async-done(((bf16[1536,128]{1,0:T(8,128)(2,1)}), bf16[24576,128]{1,0:T(8,128)(2,1)}) %all-gather.5.cloned.1.call-update) | async-done | bytes 6291472 | tf_op jit(solution)/shard_map/all_gather | solution.py:63
  99.5 2.4 %fusion.2 = bf16[1536,512]{0,1:T(8,128)(2,1)S(1)} fusion(bf16[4,128,512]{2,1,0:T(8,128)(2,1)S(1)} %bitcast.77, bf16[16,1536,128]{2,1,0:T(8,128)(2,1)} %bitcast.78, s32[]{:T(128)S(6)} %select_n.24), kind=kOutput, calls=%fused_computation.10 | convolution fusion | flops 806092800 | bytes 3670020 | tf_op jit(solution)/shard_map/jik,jkl->il/dot_general | solution.py:67
  102.0 5.8 %bitcast_subtract_fusion.1 = f32[1536,1536]{1,0:T(8,128)S(1)} fusion(f32[1536,1536]{1,0:T(8,128)} %copy-done, bf16[1536,4,128]{0,2,1:T(8,128)(2,1)S(1)} %bitcast.75, bf16[16,1536,128]{2,1,0:T(8,128)(2,1)} %bitcast.79, s32[]{:T(128)S(6)} %select_n.23), kind=kOutput, calls=%fused_computation.4 | convolution fusion | flops 2418278400 | bytes 22020100 | tf_op jit(solution)/shard_map/ijk,jmk->im/dot_general | solution.py:73
  107.8 3.6 %copy-done.2 = f32[1536,1536]{1,0:T(8,128)} copy-done((f32[1536,1536]{1,0:T(8,128)}, f32[1536,1536]{1,0:T(8,128)S(1)}, u32[]{:S(2)}) %copy-start.2) | copy-done | bytes 9437208
  111.4 0.8 dynamic-slice_convert_fusion
  112.3 45.9 %all-gather.7.cloned.1.call-done = bf16[24576,128]{1,0:T(8,128)(2,1)} async-done(((bf16[1536,128]{1,0:T(8,128)(2,1)}), bf16[24576,128]{1,0:T(8,128)(2,1)}) %all-gather.7.cloned.1.call-update) | async-done | bytes 6291472 | tf_op jit(solution)/shard_map/all_gather | solution.py:63
  158.3 2.4 %fusion.3 = bf16[1536,512]{0,1:T(8,128)(2,1)S(1)} fusion(bf16[4,128,512]{2,1,0:T(8,128)(2,1)S(1)} %bitcast.76, bf16[16,1536,128]{2,1,0:T(8,128)(2,1)} %bitcast.80, s32[]{:T(128)S(6)} %select_n.24), kind=kOutput, calls=%fused_computation.11 | convolution fusion | flops 806092800 | bytes 3670020 | tf_op jit(solution)/shard_map/jik,jkl->il/dot_general | solution.py:67
  160.7 7.2 %fusion.1 = bf16[1,1536,1536]{2,1,0:T(8,128)(2,1)} fusion(f32[1536,1536]{1,0:T(8,128)} %copy-done.2, bf16[1536,4,128]{0,2,1:T(8,128)(2,1)S(1)} %bitcast.82, bf16[16,1536,128]{2,1,0:T(8,128)(2,1)} %bitcast.81, s32[]{:T(128)S(6)} %select_n.23), kind=kOutput, calls=%fused_computation.5 | convolution fusion | flops 2420637696 | bytes 17301508 | tf_op jit(solution)/shard_map/ijk,jmk->im/dot_general | solution.py:73
  (11 shorter events, 0.3 us)
Async XLA Ops:
  6.5 93.0 %all-gather.5.cloned.1.call-start = ((), (), s32[]{:S(2)}) async-start(), calls=%async_computation | async-start | bytes 6684672 | tf_op jit(solution)/shard_map/all_gather | solution.py:63
  6.5 14.5 %collective-permute-start = (bf16[1,512,512]{2,1,0:T(8,128)(2,1)}, bf16[1,512,512]{2,1,0:T(8,128)(2,1)S(1)}, u32[]{:S(2)}, u32[]{:S(2)}) collective-permute-start(bf16[1,512,512]{2,1,0:T(8,128)(2,1)} %param.8), channel_id=1, source_target_pairs={{0,16},{16,0},{32,48},{48,32},{64,80},{80,64},{96,112},{112,96},{1... | collective-permute-start | bytes 1572872 | tf_op jit(solution)/shard_map/ppermute | solution.py:18
  22.1 8.9 %copy-start.1 = (f32[12,12,128,128]{3,0,2,1:T(8,128)S(1)}, f32[12,12,128,128]{3,0,2,1:T(8,128)}, u32[]{:S(2)}) copy-start(f32[12,12,128,128]{3,0,2,1:T(8,128)} %fusion.4) | copy-start | bytes 28311556
  30.9 19.4 %copy-start.3 = (bf16[1,2,512,512]{3,2,1,0:T(8,128)(2,1)S(1)}, bf16[1,2,512,512]{3,2,1,0:T(8,128)(2,1)}, u32[]{:S(2)}) copy-start(bf16[1,2,512,512]{3,2,1,0:T(8,128)(2,1)} %param.11) | copy-start | bytes 3145732
  44.9 3.7 %copy-start = (f32[1536,1536]{1,0:T(8,128)}, f32[1536,1536]{1,0:T(8,128)S(1)}, u32[]{:S(2)}) copy-start(f32[1536,1536]{1,0:T(8,128)S(1)} %bitcast_add_fusion) | copy-start | bytes 28311556
  49.4 108.8 %all-gather.7.cloned.1.call-start = ((), (), s32[]{:S(2)}) async-start(), calls=%async_computation.1 | async-start | bytes 6684672 | tf_op jit(solution)/shard_map/all_gather | solution.py:63
  107.8 3.7 %copy-start.2 = (f32[1536,1536]{1,0:T(8,128)}, f32[1536,1536]{1,0:T(8,128)S(1)}, u32[]{:S(2)}) copy-start(f32[1536,1536]{1,0:T(8,128)S(1)} %bitcast_subtract_fusion.1) | copy-start | bytes 28311556
Sparse Core Ops, SparseCore 0:
  49.6 49.9 all-gather.4
  112.4 45.7 all-gather.6
where the time goes:
time: 175 us
  waiting for transfers between devices  95.3 us (54%)
  matrix products  32.4 us (19%)
  between operations  14.8 us (8%)
  local copies, waits for them, and re-layouts  14.3 us (8%)
  other arithmetic  14.1 us (8%)
  starting transfers between devices  3.8 us (2%)
    all_gather x2, waiting for transfers between devices, body(): lax.all_gather(column_piece[None], ('row', 'col'), axis=0, tiled=True)  95 us
    add x1, other arithmetic, body(): current = current + extend_add(child, row_map, col_map, blocks_here)  14 us
    dot_general x2, matrix products, body(): jnp.einsum(pattern, stacked, opposite, preferred_element_type=jnp.float32)  13.1 us
    dot_general x2, matrix products, extend_add(): jnp.einsum('pibj,bq->piqj', partial_rows, col_pick, preferred_element_typ...  12.6 us
    unnamed x8, local copies, waits for them, and re-layouts  9.16 us
    dot_general x2, matrix products, body(): jnp.einsum('jik,jkl->il', own_rows, inverse_now, preferred_element_type=j...  4.86 us
    ppermute x1, starting transfers between devices, from_partner(): return lax.ppermute(block, axis, route)  3.57 us
  transfers between devices with their start and end apart: 3, of which 3 were waited for; matrix products, arithmetic and copies ran while one was open for 6% of the time, Pallas kernels for 0%

commit v1 on v0

v1 whole, which is shorter than its diff:
```python
import jax
import jax.numpy as jnp
from jax import lax
from jax.experimental import pallas as pl
from jax.experimental.pallas import tpu as pltpu
from jax.sharding import PartitionSpec as P

BLK = 128
PAIR = 2 * BLK
P_SIZE = 512
F32 = jnp.float32
BF16 = jnp.bfloat16
VMEM = pl.BlockSpec(memory_space=pltpu.VMEM)
HBM = pl.BlockSpec(memory_space=pltpu.HBM)
MIB = 1 << 20
SMALL = pl.CostEstimate(flops=1000, bytes_accessed=1000, transcendentals=0)


def shift(x, axis, step):
    n = lax.axis_size(axis)
    return lax.ppermute(x, axis, [(i, (i + step) % n) for i in range(n)])


def flip(x, axis, bit):
    n = lax.axis_size(axis)
    return lax.ppermute(x, axis, [(i, i ^ bit) for i in range(n)])


def at(block, size=BLK):
    return pl.ds(pl.multiple_of(block * size, size), size)


def places():
    return lax.axis_index("row"), lax.axis_index("col")


def dot(a, b):
    return jnp.dot(a, b, preferred_element_type=F32)


def dot_t(a, b):
    return lax.dot_general(a, b, (((1,), (1,)), ((), ())), preferred_element_type=F32)


def out(*shape, dtype=BF16):
    return jax.ShapeDtypeStruct(shape, dtype)


def params(mib):
    return pltpu.CompilerParams(vmem_limit_bytes=mib * MIB)


def add_rows(acc, child, which, s, map_s, piv_s, row, col, here, kids):
    for k in range(kids):

        @pl.when(map_s[0, which, row * kids + k] == piv_s[0, s, row])
        def _():
            for a in range(kids):
                t = map_s[0, which, col * kids + a] - col * here
                acc[s, :, at(t)] += child[0, k * BLK : (k + 1) * BLK, a * BLK : (a + 1) * BLK].astype(F32)


def add_cols(acc, child, which, s, map_s, piv_s, row, col, here, kids):
    for k in range(kids):

        @pl.when(map_s[0, which, col * kids + k] == piv_s[0, s, col])
        def _():
            for a in range(kids):
                t = map_s[0, which, row * kids + a] - row * here
                acc[s, at(t), :] += child[0, a * BLK : (a + 1) * BLK, k * BLK : (k + 1) * BLK].astype(F32)


def scalars(map_ref, piv_ref, map_s, piv_s, sem):
    first = pltpu.make_async_copy(map_ref, map_s, sem.at[0])
    second = pltpu.make_async_copy(piv_ref, piv_s, sem.at[1])
    first.start()
    second.start()
    first.wait()
    second.wait()


def each_block(map_s, col, here, kids, visit):
    place = jnp.int32(0)
    for t in range(here):
        hit = jnp.bool_(False)
        for a in range(kids):
            hit = hit | (map_s[0, 1, col * kids + a] - col * here == t)

        @pl.when(jnp.logical_not(hit))
        def _():
            visit(t, place)

        place = place + jnp.where(hit, 0, 1)


def early_kernel(map_ref, piv_ref, front, kept, rows_out, map_s, piv_s, rows_in, kid, sem):
    row, col = places()
    here = front.shape[1] // BLK
    kids = kept.shape[1] // BLK
    child = pltpu.make_async_copy(kept, kid, sem.at[2])
    child.start()
    scalars(map_ref, piv_ref, map_s, piv_s, sem)
    copies = []
    for s in range(2):
        pr = piv_s[0, s, row] - row * here
        copies.append(pltpu.make_async_copy(front.at[0, at(pr), :], rows_in.at[s], sem.at[s]))
    for c in copies:
        c.start()
    for c in copies:
        c.wait()
    child.wait()
    for s in range(2):
        for k in range(kids):

            @pl.when(map_s[0, 0, row * kids + k] == piv_s[0, s, row])
            def _():
                for a in range(kids):
                    t = at(map_s[0, 0, col * kids + a] - col * here)
                    piece = kid[0, k * BLK : (k + 1) * BLK, a * BLK : (a + 1) * BLK].astype(F32)
                    rows_in[s, :, t] = (rows_in[s, :, t].astype(F32) + piece).astype(BF16)

    def visit(t, place):
        for s in range(2):
            rows_out[s * BLK : (s + 1) * BLK, at(place)] = rows_in[s, :, t * BLK : (t + 1) * BLK]

    each_block(map_s, col, here, kids, visit)


def early(child_map, pivots, front, kept):
    span = front.shape[1]
    return pl.pallas_call(
        early_kernel,
        out_shape=out(PAIR, span - kept.shape[1]),
        in_specs=[HBM] * 4,
        out_specs=VMEM,
        scratch_shapes=[
            pltpu.SMEM(child_map.shape, jnp.int32),
            pltpu.SMEM(pivots.shape, jnp.int32),
            pltpu.VMEM((2, BLK, span), BF16),
            pltpu.VMEM(kept.shape, BF16),
            pltpu.SemaphoreType.DMA((3,)),
        ],
        compiler_params=params(57),
        cost_estimate=SMALL,
        name="early",
    )(child_map, pivots, front, kept)


def prepare_kernel(
    map_ref, piv_ref, front, kept, rows_out, cols32, map_s, piv_s, rows_in, cols_in, rows32, sem
):
    row, col = places()
    here = front.shape[1] // BLK
    kids = kept.shape[1] // BLK
    scalars(map_ref, piv_ref, map_s, piv_s, sem)
    copies = []
    for s in range(2):
        pr = piv_s[0, s, row] - row * here
        pc = piv_s[0, s, col] - col * here
        copies.append(pltpu.make_async_copy(front.at[0, at(pr), :], rows_in.at[s], sem.at[2 * s]))
        copies.append(pltpu.make_async_copy(front.at[0, :, at(pc)], cols_in.at[s], sem.at[2 * s + 1]))
    for c in copies:
        c.start()
    for c in copies:
        c.wait()
    rows32[...] = rows_in[...].astype(F32)
    cols32[...] = cols_in[...].astype(F32)
    for s in range(2):
        add_rows(rows32, kept, 0, s, map_s, piv_s, row, col, here, kids)
        add_cols(cols32, kept, 0, s, map_s, piv_s, row, col, here, kids)
        for a in range(kids):
            t = map_s[0, 1, col * kids + a] - col * here
            rows_out[s, :, a * BLK : (a + 1) * BLK] = rows32[s, :, at(t)]


def prepare(child_map, pivots, front, kept):
    span = front.shape[1]
    return pl.pallas_call(
        prepare_kernel,
        out_shape=(out(2, BLK, kept.shape[1], dtype=F32), out(2, span, BLK, dtype=F32)),
        in_specs=[HBM, HBM, HBM, VMEM],
        out_specs=(VMEM, VMEM),
        scratch_shapes=[
            pltpu.SMEM(child_map.shape, jnp.int32),
            pltpu.SMEM(pivots.shape, jnp.int32),
            pltpu.VMEM((2, BLK, span), BF16),
            pltpu.VMEM((2, span, BLK), BF16),
            pltpu.VMEM((2, BLK, span), F32),
            pltpu.SemaphoreType.DMA((4,)),
        ],
        compiler_params=params(12),
        cost_estimate=SMALL,
        name="prepare",
    )(child_map, pivots, front, kept)


def extract_kernel(map_s, piv_s, rows32, cols32, arrived, rows_out, top, bottom, cross):
    row, col = places()
    half = top.shape[0]
    halves = half // BLK
    here = 2 * halves
    kids = arrived.shape[1] // BLK
    for s in range(2):
        own = slice(s * BLK, (s + 1) * BLK)
        rows_out[own, : kids * BLK] = rows32[s].astype(BF16)
        top[:, own] = cols32[s, :half].astype(BF16)
        bottom[:, own] = cols32[s, half:].astype(BF16)
        for k in range(kids):

            @pl.when(map_s[0, 1, row * kids + k] == piv_s[0, s, row])
            def _():
                piece = arrived[0, k * BLK : (k + 1) * BLK, :].astype(F32)
                rows_out[own, : kids * BLK] = (rows32[s] + piece).astype(BF16)

            @pl.when(map_s[0, 1, col * kids + k] == piv_s[0, s, col])
            def _():
                for a in range(kids):
                    t = map_s[0, 1, row * kids + a] - row * here
                    piece = arrived[0, a * BLK : (a + 1) * BLK, k * BLK : (k + 1) * BLK].astype(F32)
                    total = (cols32[s, at(t), :] + piece).astype(BF16)

                    @pl.when(t < halves)
                    def _():
                        top[at(t), own] = total

                    @pl.when(t >= halves)
                    def _():
                        bottom[at(t - halves), own] = total

    t = piv_s[0, 1, row] - row * here
    rows_out[BLK:, kids * BLK :] = jnp.zeros((BLK, BLK), BF16)

    @pl.when(t < halves)
    def _():
        rows_out[:BLK, kids * BLK :] = top[at(t), :BLK]
        cross[...] = top[at(t), :BLK]

    @pl.when(t >= halves)
    def _():
        rows_out[:BLK, kids * BLK :] = bottom[at(t - halves), :BLK]
        cross[...] = bottom[at(t - halves), :BLK]


def extract(child_map, pivots, rows32, cols32, arrived):
    half = cols32.shape[1] // 2
    return pl.pallas_call(
        extract_kernel,
        out_shape=(out(PAIR, arrived.shape[1] + BLK), out(half, PAIR), out(half, PAIR), out(BLK, BLK)),
        in_specs=[pl.BlockSpec(memory_space=pltpu.SMEM)] * 2 + [VMEM] * 3,
        out_specs=(VMEM,) * 4,
        compiler_params=params(8),
        cost_estimate=SMALL,
        name="extract",
    )(child_map, pivots, rows32, cols32, arrived)


def base_kernel(map_ref, front, kept, arrived, base, map_s, sem):
    row, col = places()
    step = pl.program_id(0)
    here = front.shape[2] // BLK
    deep = front.shape[1] // BLK
    kids = kept.shape[1] // BLK
    width = front.shape[1]
    load = pltpu.make_async_copy(map_ref, map_s, sem.at[0])
    load.start()
    load.wait()
    mine = pl.ds(pl.multiple_of(step * width, width), width)
    base[mine, :] = front[0].astype(F32)
    for which, child in ((0, kept), (1, arrived)):
        for k in range(kids):
            t = map_s[0, which, row * kids + k] - row * here - step * deep

            @pl.when((t >= 0) & (t < deep))
            def _():
                for a in range(kids):
                    u = map_s[0, which, col * kids + a] - col * here
                    piece = child[0, k * BLK : (k + 1) * BLK, a * BLK : (a + 1) * BLK]
                    base[at(t + step * deep), at(u)] += piece.astype(F32)


def make_base(child_map, front, kept, arrived):
    span = front.shape[1]
    steps = 4
    return pl.pallas_call(
        base_kernel,
        grid=(steps,),
        out_shape=out(span, span, dtype=F32),
        in_specs=[HBM, pl.BlockSpec((1, span // steps, span), lambda i: (0, i, 0)), VMEM, VMEM],
        out_specs=VMEM,
        scratch_shapes=[pltpu.SMEM(child_map.shape, jnp.int32), pltpu.SemaphoreType.DMA((1,))],
        compiler_params=params(16),
        cost_estimate=SMALL,
        name="base",
    )(child_map, front, kept, arrived)


def weights_kernel(x0, x1, x2, x3, inverse, w, x, k, ki):
    row, col = places()
    for q, xq in enumerate((x0, x1, x2, x3)):
        j = lax.bitwise_xor(col, q)
        for d in range(4):
            x[at(lax.rem(row + d, 4)), at(j)] = xq[d]
    k[...] = dot_t(inverse[0, 0], x[...]).astype(BF16)
    ki[...] = dot(k[...], inverse[0, 1]).astype(BF16)
    both = (inverse[0, 0].astype(F32) + dot_t(ki[...], k[...])).astype(BF16)
    flat = dot_t(inverse[0, 1], k[...]).astype(BF16)
    for i in range(4):
        for j in range(4):
            a, b = slice(i * BLK, (i + 1) * BLK), slice(j * BLK, (j + 1) * BLK)
            upper, lower = slice(i * PAIR, i * PAIR + BLK), slice(i * PAIR + BLK, (i + 1) * PAIR)
            left, right = slice(j * PAIR, j * PAIR + BLK), slice(j * PAIR + BLK, (j + 1) * PAIR)
            w[upper, left] = both[a, b]
            w[upper, right] = -ki[a, b]
            w[lower, left] = -flat[a, b]
            w[lower, right] = inverse[0, 1, a, b]


def weights(crosses, inverse):
    return pl.pallas_call(
        weights_kernel,
        out_shape=out(2 * P_SIZE, 2 * P_SIZE),
        in_specs=[VMEM] * 5,
        out_specs=VMEM,
        scratch_shapes=[pltpu.VMEM((P_SIZE, P_SIZE), BF16)] * 3,
        compiler_params=params(12),
        cost_estimate=SMALL,
        name="weights",
    )(*crosses, inverse)


def gather_kernel(w, u0, u1, u3, a0, a1, a3, acc):
    row, _ = places()
    split = u0.shape[1]
    js = [lax.rem(row + d, 4) for d in (0, 1, 3)]

    def chunk(pieces, n, offset):
        here = at(n, PAIR)
        total = dot(w[:, at(js[0], PAIR)], pieces[0][:, here])
        total += dot(w[:, at(js[1], PAIR)], pieces[1][:, here])
        total += dot(w[:, at(js[2], PAIR)], pieces[2][:, here])
        acc[:, at(n + offset, PAIR)] = total

    @pl.loop(0, split // PAIR)
    def _(n):
        chunk((u0, u1, u3), n, 0)

    @pl.loop(0, acc.shape[1] // PAIR - split // PAIR)
    def _(n):
        chunk((a0, a1, a3), n, split // PAIR)


def gather(w, us, as_, span):
    return pl.pallas_call(
        gather_kernel,
        out_shape=out(2 * P_SIZE, span, dtype=F32),
        in_specs=[VMEM] * 7,
        out_specs=VMEM,
        compiler_params=params(12),
        cost_estimate=SMALL,
        name="gather",
    )(w, *us, *as_)


def finish_kernel(map_ref, w, acc, f1, f2, v, map_s, order, far, sem):
    row, col = places()
    span = acc.shape[1]
    here = span // BLK
    kids = map_s.shape[2] // 4
    load = pltpu.make_async_copy(map_ref, map_s, sem.at[0])
    load.start()
    far[:BLK, :] = f1[...]
    far[BLK:, :] = f2[...]
    load.wait()

    def visit(t, place):
        order[place] = t

    each_block(map_s, col, here, kids, visit)
    for a in range(kids):
        order[here - kids + a] = map_s[0, 1, col * kids + a] - col * here
    mine = at(lax.rem(row + 2, 4), PAIR)

    @pl.loop(0, span // PAIR)
    def _(n):
        chunk = at(n, PAIR)
        total = (acc[:, chunk] + dot(w[:, mine], far[:, chunk])).astype(BF16)
        v[:, at(order[2 * n])] = total[:, :BLK]
        v[:, at(order[2 * n + 1])] = total[:, BLK:]


def finish(child_map, w, acc, f1, f2):
    return pl.pallas_call(
        finish_kernel,
        out_shape=out(*acc.shape),
        in_specs=[HBM] + [VMEM] * 4,
        out_specs=VMEM,
        scratch_shapes=[
            pltpu.SMEM(child_map.shape, jnp.int32),
            pltpu.SMEM((acc.shape[1] // BLK,), jnp.int32),
            pltpu.VMEM((PAIR, acc.shape[1]), BF16),
            pltpu.SemaphoreType.DMA((1,)),
        ],
        compiler_params=params(8),
        cost_estimate=SMALL,
        name="finish",
    )(child_map, w, acc, f1, f2)


def update_kernel(half, c0, c1, c2, c3, v, base, updated, panel, done, sem):
    _, col = places()
    depth = c0.shape[0]
    width = done.shape[2]
    rows = pl.ds(half * depth, depth)
    for q, c in enumerate((c0, c1, c2, c3)):
        panel[:, at(lax.bitwise_xor(col, q), PAIR)] = c[...]

    def store(n):
        return pltpu.make_async_copy(done.at[n], updated.at[0, rows, at(n, width)], sem.at[n])

    chunks = done.shape[0]

    @pl.loop(0, chunks)
    def _(n):
        here = at(n, width)
        done[n] = (base[rows, here] - dot(panel[...], v[:, here])).astype(BF16)
        store(n).start()

    @pl.loop(0, chunks)
    def _(n):
        store(n).wait()


def update(half, pieces, v, base, *rest):
    span = base.shape[0]
    width = 2 * PAIR

    def kernel(*refs):
        update_kernel(half, *refs[:6], *refs[6 + len(rest) :])

    return pl.pallas_call(
        kernel,
        out_shape=out(1, span, span),
        in_specs=[VMEM] * 6 + [HBM] * len(rest),
        out_specs=HBM,
        input_output_aliases={6: 0} if rest else {},
        scratch_shapes=[
            pltpu.VMEM((span // 2, 4 * PAIR), BF16),
            pltpu.VMEM((span // width, span // 2, width), BF16),
            pltpu.SemaphoreType.DMA((span // width,)),
        ],
        compiler_params=params(12),
        cost_estimate=SMALL,
        name="update",
    )(*pieces, v, base, *rest)


def body(front_matrix, kept_child, passed_child, child_map, pivots, pivot_inverse):
    hold = lax.optimization_barrier
    span = front_matrix.shape[1]
    kid = kept_child.shape[1]
    arrived = flip(passed_child, "front", 1)
    u = early(child_map, pivots, front_matrix, kept_child)
    un, up = shift(u, "row", -1), shift(u, "row", 1)
    rows32, cols32 = prepare(child_map, pivots, front_matrix, kept_child)
    arrived, _, rows32, cols32 = hold((arrived, u, rows32, cols32))
    a, top, bottom, cross = extract(child_map, pivots, rows32, cols32, arrived)
    tfar, tnear = flip(top, "col", 2), flip(top, "col", 1)
    an, ap = shift(a, "row", -1), shift(a, "row", 1)
    cross2 = shift(cross, "row", 2)
    base = make_base(child_map, front_matrix, kept_child, arrived)
    un, up, an, ap, cross2, base, tfar, tnear = hold((un, up, an, ap, cross2, base, tfar, tnear))
    crosses = jnp.stack([cross, an[:BLK, kid:], cross2, ap[:BLK, kid:]])
    xfar, xnear = flip(crosses, "col", 2), flip(crosses, "col", 1)
    f1 = shift(jnp.concatenate([up[:BLK], ap[:BLK, :kid]], axis=1), "row", 1)
    f2 = shift(jnp.concatenate([un[BLK:], an[BLK:, :kid]], axis=1), "row", -1)
    tcorner = flip(tfar, "col", 1)
    xfar, xnear, tcorner, bottom = hold((xfar, xnear, tcorner, bottom))
    xcorner = flip(xfar, "col", 1)
    bfar, bnear = flip(bottom, "col", 2), flip(bottom, "col", 1)
    w = weights((crosses, xnear, xfar, xcorner), pivot_inverse)
    acc = gather(w, (u, un, up), (a, an, ap), span)
    acc, f1, f2 = hold((acc, f1, f2))
    v = finish(child_map, w, acc, f1, f2)
    v, bfar, bnear = hold((v, bfar, bnear))
    bcorner = flip(bfar, "col", 1)
    upper = update(0, (top, tnear, tfar, tcorner), v, base)
    upper, bcorner = hold((upper, bcorner))
    return update(1, (bottom, bnear, bfar, bcorner), v, base, upper)


def solution(mesh):
    in_specs = (
        P("front", "row", "col"),
        P("front", "row", "col"),
        P("front", "row", "col"),
        P("front", None, None),
        P("front", None, None),
        P("front", None, None, None),
    )
    out_specs = P("front", "row", "col")
    return jax.shard_map(body, mesh=mesh, in_specs=in_specs, out_specs=out_specs, check_vma=False)
```

time: 175 us -> 59.8 us (0.34)
  waiting for transfers between devices: 95.3 us -> 10.6 us
  matrix products: 32.4 us -> 0 us
  Pallas kernels: 0 us -> 25.2 us
  starting transfers between devices: 3.8 us -> 23.3 us
  between operations: 14.8 us -> 0.39 us
  local copies, waits for them, and re-layouts: 14.3 us -> 0.09 us
  other arithmetic: 14.1 us -> 0.08 us
    all_gather x2 -> x0, waiting for transfers between devices: 95 us -> none  [body(): lax.all_gather(column_piece[None], ('row', 'col'), axis=0, tiled=True)]
    dot_general x8 -> x0, matrix products: 32.4 us -> none  [the longest x2 13.1 us: body(): jnp.einsum(pattern, stacked, opposite, preferred_element_type=jnp.float32)]
    pallas_call x0 -> x9, Pallas kernels: none -> 25.2 us  [the longest x2 8.27 us: update(): pl.pallas_call(kernel, out_shape=out(1, span, span), in_specs=[VMEM] * 6...]
    ppermute x1 -> x17, starting transfers between devices: 3.57 us -> 23.3 us  [the longest x10 14.5 us: flip(): return lax.ppermute(x, axis, [(i, i ^ bit) for i in range(n)])]
    add x1 -> x0, other arithmetic: 14 us -> none  [body(): current = current + extend_add(child, row_map, col_map, blocks_here)]
    ppermute x1 -> x17, waiting for transfers between devices: 0.24 us -> 10.6 us  [the longest x7 5.59 us: shift(): return lax.ppermute(x, axis, [(i, (i + step) % n) for i in range(n)])]
    unnamed x8 -> x12, local copies, waits for them, and re-layouts: 9.16 us -> 0.03 us
  transfers between devices with their start and end apart: 3 -> 17, of which waited for: 3 -> 5; matrix products, arithmetic and copies ran while one was open for 6% -> 0% of each run, Pallas kernels for 0% -> 35%
where the time goes in v1:
time: 59.8 us; the launch traced here: 59.6 us
  Pallas kernels  25.2 us (42%)
  starting transfers between devices  23.3 us (39%)
  waiting for transfers between devices  10.6 us (18%)
    ppermute x10, starting transfers between devices, flip(): return lax.ppermute(x, axis, [(i, i ^ bit) for i in range(n)])  14.5 us
    ppermute x7, starting transfers between devices, shift(): return lax.ppermute(x, axis, [(i, (i + step) % n) for i in range(n)])  8.77 us
    pallas_call x2, Pallas kernels, update(): pl.pallas_call(kernel, out_shape=out(1, span, span), in_specs=[VMEM] * 6...  8.27 us
    ppermute x7, waiting for transfers between devices, shift(): return lax.ppermute(x, axis, [(i, (i + step) % n) for i in range(n)])  5.59 us
    ppermute x10, waiting for transfers between devices, flip(): return lax.ppermute(x, axis, [(i, i ^ bit) for i in range(n)])  5 us
    pallas_call x1, Pallas kernels, gather(): pl.pallas_call(gather_kernel, out_shape=out(2 * P_SIZE, span, dtype=F32),...  3.55 us
    pallas_call x1, Pallas kernels, make_base(): pl.pallas_call(base_kernel, grid=(steps,), out_shape=out(span, span, dtyp...  3.54 us
    pallas_call x1, Pallas kernels, early(): pl.pallas_call(early_kernel, out_shape=out(PAIR, span - kept.shape[1]), i...  3.09 us
  transfers between devices with their start and end apart: 17, of which 5 were waited for; matrix products, arithmetic and copies ran while one was open for 0% of the time, Pallas kernels for 35%

profile of v1, /device:TPU:1, one launch (start us, length us, event | category | flops | bytes accessed | tf_op | source)
XLA Modules:
  0.0 59.6 jit_solution(11832451899531628939)
XLA Ops:
  0.0 3.7 %collective-permute-start = (bf16[1,512,512]{2,1,0:T(8,128)(2,1)}, bf16[1,512,512]{2,1,0:T(8,128)(2,1)S(1)}, u32[]{:S(2)}, u32[]{:S(2)}) collective-permute-start(bf16[1,512,512]{2,1,0:T(8,128)(2,1)} %param.8), channel_id=1, source_target_pairs={{0,16},{16,0},{32,48},{48,32},{64,80},{80,64},{96,112},{112,96},{1... | collective-permute-start | bytes 1572872 | tf_op jit(solution)/shard_map/ppermute | solution.py:26
  3.7 3.1 %early.1.u0 = bf16[256,1024]{1,0:T(8,128)(2,1)} custom-call(s32[1,2,16]{2,1,0:T(2,128)} %map_ref.7, s32[1,2,4]{2,1,0:T(2,128)} %piv_s.1, bf16[1,1536,1536]{2,1,0:T(8,128)(2,1)} %front.5, bf16[1,512,512]{2,1,0:T(8,128)(2,1)} %kept.5), custom_call_target="tpu_custom_call" | custom-call | flops 1000 | bytes 1000 | tf_op jit(solution)/shard_map/early/pallas_call | solution.py:131
  6.8 2.7 %collective-permute-start.1 = (bf16[256,1024]{1,0:T(8,128)(2,1)}, bf16[256,1024]{1,0:T(8,128)(2,1)S(1)}, u32[]{:S(2)}, u32[]{:S(2)}) collective-permute-start(bf16[256,1024]{1,0:T(8,128)(2,1)} %early.1.u0), channel_id=1, source_target_pairs={{0,12},{4,0},{8,4},{12,8},{1,13},{5,1},{9,5},{13,9},{2,14},{6,2},{... | collective-permute-start | bytes 1572872 | tf_op jit(solution)/shard_map/ppermute | solution.py:21
  9.6 1.6 %prepare.1 = (f32[2,128,512]{2,1,0:T(8,128)S(1)}, f32[2,1536,128]{2,1,0:T(8,128)S(1)}) custom-call(s32[1,2,16]{2,1,0:T(2,128)S(1)} %copy-done.4, s32[1,2,4]{2,1,0:T(2,128)S(1)} %copy-done.5, bf16[1,1536,1536]{2,1,0:T(8,128)(2,1)S(1)} %copy-done, bf16[1,512,512]{2,1,0:T(8,128)(2,1)S(1)} %copy-done.1), custom_call_target="tpu_custom_call" | custom-call | flops 1000 | bytes 1000 | tf_op jit(solution)/shard_map/prepare/pallas_call | solution.py:178
  11.1 3.4 %collective-permute-done.arrived = bf16[1,512,512]{2,1,0:T(8,128)(2,1)S(1)} collective-permute-done((bf16[1,512,512]{2,1,0:T(8,128)(2,1)}, bf16[1,512,512]{2,1,0:T(8,128)(2,1)S(1)}, u32[]{:S(2)}, u32[]{:S(2)}) %collective-permute-start) | collective-permute-done | bytes 524320 | tf_op jit(solution)/shard_map/ppermute | solution.py:26
  15.4 2.2 %collective-permute-start.6 = (bf16[768,256]{1,0:T(8,128)(2,1)S(1)}, bf16[768,256]{1,0:T(8,128)(2,1)S(1)}, u32[]{:S(2)}, u32[]{:S(2)}) collective-permute-start(bf16[768,256]{1,0:T(8,128)(2,1)S(1)} %get-tuple-element.41.refs_0_), channel_id=1, source_target_pairs={{0,2},{1,3},{2,0},{3,1},{4,6},{5,7},{6,4},{7,5},{8,10},{9,11},{10,... | collective-permute-start | bytes 1179656 | tf_op jit(solution)/shard_map/ppermute | solution.py:26
  17.7 1.8 %collective-permute-start.7 = (bf16[768,256]{1,0:T(8,128)(2,1)S(1)}, bf16[768,256]{1,0:T(8,128)(2,1)S(1)}, u32[]{:S(2)}, u32[]{:S(2)}) collective-permute-start(bf16[768,256]{1,0:T(8,128)(2,1)S(1)} %get-tuple-element.41.refs_0_), channel_id=1, source_target_pairs={{0,1},{1,0},{2,3},{3,2},{4,5},{5,4},{6,7},{7,6},{8,9},{9,8},{10,11... | collective-permute-start | bytes 1179656 | tf_op jit(solution)/shard_map/ppermute | solution.py:26
  19.4 2.8 %collective-permute-start.3 = (bf16[256,640]{1,0:T(8,128)(2,1)S(1)}, bf16[256,640]{1,0:T(8,128)(2,1)S(1)}, u32[]{:S(2)}, u32[]{:S(2)}) collective-permute-start(bf16[256,640]{1,0:T(8,128)(2,1)S(1)} %get-tuple-element.40.a0), channel_id=1, source_target_pairs={{0,12},{4,0},{8,4},{12,8},{1,13},{5,1},{9,5},{13,9},{2,14},{6,2},{... | collective-permute-start | bytes 983048 | tf_op jit(solution)/shard_map/ppermute | solution.py:21
  22.2 0.9 %collective-permute-done.2.u3 = bf16[256,1024]{1,0:T(8,128)(2,1)S(1)} collective-permute-done((bf16[256,1024]{1,0:T(8,128)(2,1)}, bf16[256,1024]{1,0:T(8,128)(2,1)S(1)}, u32[]{:S(2)}, u32[]{:S(2)}) %collective-permute-start.2) | collective-permute-done | bytes 524320 | tf_op jit(solution)/shard_map/ppermute | solution.py:21
  23.1 1.5 %collective-permute-start.5 = (bf16[128,128]{1,0:T(8,128)(2,1)S(1)}, bf16[128,128]{1,0:T(8,128)(2,1)S(1)}, u32[]{:S(2)}, u32[]{:S(2)}) collective-permute-start(bf16[128,128]{1,0:T(8,128)(2,1)S(1)} %get-tuple-element.39), channel_id=1, source_target_pairs={{0,8},{4,12},{8,0},{12,4},{1,9},{5,13},{9,1},{13,5},{2,10},{6,14},... | collective-permute-start | bytes 98312 | tf_op jit(solution)/shard_map/ppermute | solution.py:21
  24.6 3.5 %base.1.refs_5_ = f32[1536,1536]{1,0:T(8,128)S(1)} custom-call(s32[1,2,16]{2,1,0:T(2,128)S(1)} %copy-done.4, bf16[1,1536,1536]{2,1,0:T(8,128)(2,1)S(1)} %copy-done, bf16[1,512,512]{2,1,0:T(8,128)(2,1)S(1)} %copy-done.1, bf16[1,512,512]{2,1,0:T(8,128)(2,1)S(1)} %collective-permute-done.arrived), custom_call_target="tpu_custom_call" | custom-call | flops 1000 | bytes 1000 | tf_op jit(solution)/shard_map/base/pallas_call | solution.py:284
  28.2 2.7 %collective-permute-done.5 = bf16[128,128]{1,0:T(8,128)(2,1)S(1)} collective-permute-done((bf16[128,128]{1,0:T(8,128)(2,1)S(1)}, bf16[128,128]{1,0:T(8,128)(2,1)S(1)}, u32[]{:S(2)}, u32[]{:S(2)}) %collective-permute-start.5) | collective-permute-done | bytes 32800 | tf_op jit(solution)/shard_map/ppermute | solution.py:21
  30.9 1.9 %collective-permute-done.4.a3 = bf16[256,640]{1,0:T(8,128)(2,1)S(1)} collective-permute-done((bf16[256,640]{1,0:T(8,128)(2,1)S(1)}, bf16[256,640]{1,0:T(8,128)(2,1)S(1)}, u32[]{:S(2)}, u32[]{:S(2)}) %collective-permute-start.4) | collective-permute-done | bytes 327712 | tf_op jit(solution)/shard_map/ppermute | solution.py:21
  33.2 1.7 %collective-permute-start.9 = (bf16[4,128,128]{2,1,0:T(8,128)(2,1)S(1)}, bf16[4,128,128]{2,1,0:T(8,128)(2,1)S(1)}, u32[]{:S(2)}, u32[]{:S(2)}) collective-permute-start(bf16[4,128,128]{2,1,0:T(8,128)(2,1)S(1)} %pad_maximum_fusion.2.x0), channel_id=1, source_target_pairs={{0,1},{1,0},{2,3},{3,2},{4,5},{5,4},{6,7},{7,6},{8,9},{9,8},{10,11... | collective-permute-start | bytes 393224 | tf_op jit(solution)/shard_map/ppermute | solution.py:26
  35.2 1.7 %collective-permute-start.12 = (bf16[128,1536]{1,0:T(8,128)(2,1)S(1)}, bf16[128,1536]{1,0:T(8,128)(2,1)S(1)}, u32[]{:S(2)}, u32[]{:S(2)}) collective-permute-start(bf16[128,1536]{1,0:T(8,128)(2,1)S(1)} %pad_maximum_fusion), channel_id=1, source_target_pairs={{0,4},{4,8},{8,12},{12,0},{1,5},{5,9},{9,13},{13,1},{2,6},{6,10},{... | collective-permute-start | bytes 1179656 | tf_op jit(solution)/shard_map/ppermute | solution.py:21
  37.0 1.3 %collective-permute-start.14 = (bf16[768,256]{1,0:T(8,128)(2,1)S(1)}, bf16[768,256]{1,0:T(8,128)(2,1)S(1)}, u32[]{:S(2)}, u32[]{:S(2)}) collective-permute-start(bf16[768,256]{1,0:T(8,128)(2,1)S(1)} %get-tuple-element.47.refs_0_), channel_id=1, source_target_pairs={{0,2},{1,3},{2,0},{3,1},{4,6},{5,7},{6,4},{7,5},{8,10},{9,11},{10,... | collective-permute-start | bytes 1179656 | tf_op jit(solution)/shard_map/ppermute | solution.py:26
  38.3 1.6 %collective-permute-start.15 = (bf16[768,256]{1,0:T(8,128)(2,1)S(1)}, bf16[768,256]{1,0:T(8,128)(2,1)S(1)}, u32[]{:S(2)}, u32[]{:S(2)}) collective-permute-start(bf16[768,256]{1,0:T(8,128)(2,1)S(1)} %get-tuple-element.47.refs_0_), channel_id=1, source_target_pairs={{0,1},{1,0},{2,3},{3,2},{4,5},{5,4},{6,7},{7,6},{8,9},{9,8},{10,11... | collective-permute-start | bytes 1179656 | tf_op jit(solution)/shard_map/ppermute | solution.py:26
  39.9 1.5 %collective-permute-done.11.x3 = bf16[4,128,128]{2,1,0:T(8,128)(2,1)S(1)} collective-permute-done((bf16[4,128,128]{2,1,0:T(8,128)(2,1)S(1)}, bf16[4,128,128]{2,1,0:T(8,128)(2,1)S(1)}, u32[]{:S(2)}, u32[]{:S(2)}) %collective-permute-start.11) | collective-permute-done | bytes 131104 | tf_op jit(solution)/shard_map/ppermute | solution.py:26
  41.5 1.5 %weights.1.w = bf16[1024,1024]{1,0:T(8,128)(2,1)S(1)} custom-call(bf16[4,128,128]{2,1,0:T(8,128)(2,1)S(1)} %pad_maximum_fusion.2.x0, bf16[4,128,128]{2,1,0:T(8,128)(2,1)S(1)} %collective-permute-done.9.x1, bf16[4,128,128]{2,1,0:T(8,128)(2,1)S(1)} %collective-permute-done.8.x2, bf16[4,128,128]{2,1,0:T(8,128)(2,1)S(1)} %collective-permute-done.11.x3, ...), custom_call_target="tpu_custom_call" | custom-call | flops 1000 | bytes 1000 | tf_op jit(solution)/shard_map/weights/pallas_call | solution.py:319
  43.0 3.5 %gather.1.acc = f32[1024,1536]{1,0:T(8,128)S(1)} custom-call(bf16[1024,1024]{1,0:T(8,128)(2,1)S(1)} %weights.1.w, bf16[256,1024]{1,0:T(8,128)(2,1)S(1)} %copy-done.2, bf16[256,1024]{1,0:T(8,128)(2,1)S(1)} %collective-permute-done.1.u1, bf16[256,1024]{1,0:T(8,128)(2,1)S(1)} %collective-permute-done.2.u3, bf16[256,640]{1,0:T(8,128)(2,1)S(1)} %get-tuple-element.40.a0, ...), custom_call_target="tpu_custom_call" | custom-call | flops 1000 | bytes 1000 | tf_op jit(solution)/shard_map/gather/pallas_call | solution.py:353
  46.6 2.8 %finish.1.refs_4_ = bf16[1024,1536]{1,0:T(8,128)(2,1)S(1)} custom-call(s32[1,2,16]{2,1,0:T(2,128)S(1)} %copy-done.4, bf16[1024,1024]{1,0:T(8,128)(2,1)S(1)} %weights.1.w, f32[1024,1536]{1,0:T(8,128)S(1)} %gather.1.acc, bf16[128,1536]{1,0:T(8,128)(2,1)S(1)} %collective-permute-done.12.f1, bf16[128,1536]{1,0:T(8,128)(2,1)S(1)} %collective-permute-done.13.f2), custom_call_target="tpu_custom_call" | custom-call | flops 1000 | bytes 1000 | tf_op jit(solution)/shard_map/finish/pallas_call | solution.py:392
  49.5 1.7 %collective-permute-start.16 = (bf16[768,256]{1,0:T(8,128)(2,1)S(1)}, bf16[768,256]{1,0:T(8,128)(2,1)S(1)}, u32[]{:S(2)}, u32[]{:S(2)}) collective-permute-start(bf16[768,256]{1,0:T(8,128)(2,1)S(1)} %collective-permute-done.14.refs_2_), channel_id=1, source_target_pairs={{0,1},{1,0},{2,3},{3,2},{4,5},{5,4},{6,7},{7,6},{8,9},{9,8},{10,11... | collective-permute-start | bytes 1179656 | tf_op jit(solution)/shard_map/ppermute | solution.py:26
  51.2 4.1 %update.2.refs_6_ = bf16[1,1536,1536]{2,1,0:T(8,128)(2,1)} custom-call(bf16[768,256]{1,0:T(8,128)(2,1)S(1)} %get-tuple-element.41.refs_0_, bf16[768,256]{1,0:T(8,128)(2,1)S(1)} %collective-permute-done.7.refs_1_, bf16[768,256]{1,0:T(8,128)(2,1)S(1)} %collective-permute-done.6.refs_2_, bf16[768,256]{1,0:T(8,128)(2,1)S(1)} %collective-permute-done.10.refs_3_, ...), custom_call_target="tpu_custom_call" | custom-call | flops 1000 | bytes 1000 | tf_op jit(solution)/shard_map/update/pallas_call | solution.py:440
  55.3 4.1 %update.3 = bf16[1,1536,1536]{2,1,0:T(8,128)(2,1)} custom-call(bf16[768,256]{1,0:T(8,128)(2,1)S(1)} %get-tuple-element.47.refs_0_, bf16[768,256]{1,0:T(8,128)(2,1)S(1)} %collective-permute-done.15.refs_1_, bf16[768,256]{1,0:T(8,128)(2,1)S(1)} %collective-permute-done.14.refs_2_, ...), custom_call_target="tpu_custom_call", output_to_operand_aliasing={{}: (6, {})} | custom-call | flops 1000 | bytes 1000 | tf_op jit(solution)/shard_map/update/pallas_call | solution.py:440
  (39 shorter events, 1.6 us)
Async XLA Ops:
  0.0 9.5 %copy-start.5 = (s32[1,2,4]{2,1,0:T(2,128)S(1)}, s32[1,2,4]{2,1,0:T(2,128)}, u32[]{:S(2)}) copy-start(s32[1,2,4]{2,1,0:T(2,128)} %piv_s.1) | copy-start | bytes 100
  0.0 9.5 %copy-start = (bf16[1,1536,1536]{2,1,0:T(8,128)(2,1)S(1)}, bf16[1,1536,1536]{2,1,0:T(8,128)(2,1)}, u32[]{:S(2)}) copy-start(bf16[1,1536,1536]{2,1,0:T(8,128)(2,1)} %front.5) | copy-start | bytes 14155780
  0.0 9.5 %copy-start.1 = (bf16[1,512,512]{2,1,0:T(8,128)(2,1)S(1)}, bf16[1,512,512]{2,1,0:T(8,128)(2,1)}, u32[]{:S(2)}) copy-start(bf16[1,512,512]{2,1,0:T(8,128)(2,1)} %kept.5) | copy-start | bytes 1572868
  0.0 9.5 %copy-start.4 = (s32[1,2,16]{2,1,0:T(2,128)S(1)}, s32[1,2,16]{2,1,0:T(2,128)}, u32[]{:S(2)}) copy-start(s32[1,2,16]{2,1,0:T(2,128)} %map_ref.7) | copy-start | bytes 388
  0.0 14.6 %collective-permute-start = (bf16[1,512,512]{2,1,0:T(8,128)(2,1)}, bf16[1,512,512]{2,1,0:T(8,128)(2,1)S(1)}, u32[]{:S(2)}, u32[]{:S(2)}) collective-permute-start(bf16[1,512,512]{2,1,0:T(8,128)(2,1)} %param.8), channel_id=1, source_target_pairs={{0,16},{16,0},{32,48},{48,32},{64,80},{80,64},{96,112},{112,96},{1... | collective-permute-start | bytes 1572872 | tf_op jit(solution)/shard_map/ppermute | solution.py:26
  6.8 15.4 %collective-permute-start.1 = (bf16[256,1024]{1,0:T(8,128)(2,1)}, bf16[256,1024]{1,0:T(8,128)(2,1)S(1)}, u32[]{:S(2)}, u32[]{:S(2)}) collective-permute-start(bf16[256,1024]{1,0:T(8,128)(2,1)} %early.1.u0), channel_id=1, source_target_pairs={{0,12},{4,0},{8,4},{12,8},{1,13},{5,1},{9,5},{13,9},{2,14},{6,2},{... | collective-permute-start | bytes 1572872 | tf_op jit(solution)/shard_map/ppermute | solution.py:21
  9.5 13.6 %collective-permute-start.2 = (bf16[256,1024]{1,0:T(8,128)(2,1)}, bf16[256,1024]{1,0:T(8,128)(2,1)S(1)}, u32[]{:S(2)}, u32[]{:S(2)}) collective-permute-start(bf16[256,1024]{1,0:T(8,128)(2,1)} %early.1.u0), channel_id=1, source_target_pairs={{0,4},{4,8},{8,12},{12,0},{1,5},{5,9},{9,13},{13,1},{2,6},{6,10},{... | collective-permute-start | bytes 1572872 | tf_op jit(solution)/shard_map/ppermute | solution.py:21
  15.4 17.3 %collective-permute-start.6 = (bf16[768,256]{1,0:T(8,128)(2,1)S(1)}, bf16[768,256]{1,0:T(8,128)(2,1)S(1)}, u32[]{:S(2)}, u32[]{:S(2)}) collective-permute-start(bf16[768,256]{1,0:T(8,128)(2,1)S(1)} %get-tuple-element.41.refs_0_), channel_id=1, source_target_pairs={{0,2},{1,3},{2,0},{3,1},{4,6},{5,7},{6,4},{7,5},{8,10},{9,11},{10,... | collective-permute-start | bytes 1179656 | tf_op jit(solution)/shard_map/ppermute | solution.py:26
  17.7 15.1 %collective-permute-start.7 = (bf16[768,256]{1,0:T(8,128)(2,1)S(1)}, bf16[768,256]{1,0:T(8,128)(2,1)S(1)}, u32[]{:S(2)}, u32[]{:S(2)}) collective-permute-start(bf16[768,256]{1,0:T(8,128)(2,1)S(1)} %get-tuple-element.41.refs_0_), channel_id=1, source_target_pairs={{0,1},{1,0},{2,3},{3,2},{4,5},{5,4},{6,7},{7,6},{8,9},{9,8},{10,11... | collective-permute-start | bytes 1179656 | tf_op jit(solution)/shard_map/ppermute | solution.py:26
  19.4 11.5 %collective-permute-start.3 = (bf16[256,640]{1,0:T(8,128)(2,1)S(1)}, bf16[256,640]{1,0:T(8,128)(2,1)S(1)}, u32[]{:S(2)}, u32[]{:S(2)}) collective-permute-start(bf16[256,640]{1,0:T(8,128)(2,1)S(1)} %get-tuple-element.40.a0), channel_id=1, source_target_pairs={{0,12},{4,0},{8,4},{12,8},{1,13},{5,1},{9,5},{13,9},{2,14},{6,2},{... | collective-permute-start | bytes 983048 | tf_op jit(solution)/shard_map/ppermute | solution.py:21
  22.2 10.6 %collective-permute-start.4 = (bf16[256,640]{1,0:T(8,128)(2,1)S(1)}, bf16[256,640]{1,0:T(8,128)(2,1)S(1)}, u32[]{:S(2)}, u32[]{:S(2)}) collective-permute-start(bf16[256,640]{1,0:T(8,128)(2,1)S(1)} %get-tuple-element.40.a0), channel_id=1, source_target_pairs={{0,4},{4,8},{8,12},{12,0},{1,5},{5,9},{9,13},{13,1},{2,6},{6,10},{... | collective-permute-start | bytes 983048 | tf_op jit(solution)/shard_map/ppermute | solution.py:21
  23.1 18.3 %copy-start.3 = (bf16[1,2,512,512]{3,2,1,0:T(8,128)(2,1)S(1)}, bf16[1,2,512,512]{3,2,1,0:T(8,128)(2,1)}, u32[]{:S(2)}) copy-start(bf16[1,2,512,512]{3,2,1,0:T(8,128)(2,1)} %inverse.1) | copy-start | bytes 3145732
  23.1 7.8 %collective-permute-start.5 = (bf16[128,128]{1,0:T(8,128)(2,1)S(1)}, bf16[128,128]{1,0:T(8,128)(2,1)S(1)}, u32[]{:S(2)}, u32[]{:S(2)}) collective-permute-start(bf16[128,128]{1,0:T(8,128)(2,1)S(1)} %get-tuple-element.39), channel_id=1, source_target_pairs={{0,8},{4,12},{8,0},{12,4},{1,9},{5,13},{9,1},{13,5},{2,10},{6,14},... | collective-permute-start | bytes 98312 | tf_op jit(solution)/shard_map/ppermute | solution.py:21
  28.2 14.8 %copy-start.2 = (bf16[256,1024]{1,0:T(8,128)(2,1)S(1)}, bf16[256,1024]{1,0:T(8,128)(2,1)}, u32[]{:S(2)}) copy-start(bf16[256,1024]{1,0:T(8,128)(2,1)} %early.1.u0) | copy-start | bytes 1572868
  32.9 4.1 %collective-permute-start.8 = (bf16[4,128,128]{2,1,0:T(8,128)(2,1)S(1)}, bf16[4,128,128]{2,1,0:T(8,128)(2,1)S(1)}, u32[]{:S(2)}, u32[]{:S(2)}) collective-permute-start(bf16[4,128,128]{2,1,0:T(8,128)(2,1)S(1)} %pad_maximum_fusion.2.x0), channel_id=1, source_target_pairs={{0,2},{1,3},{2,0},{3,1},{4,6},{5,7},{6,4},{7,5},{8,10},{9,11},{10,... | collective-permute-start | bytes 393224 | tf_op jit(solution)/shard_map/ppermute | solution.py:26
  33.2 3.8 %collective-permute-start.9 = (bf16[4,128,128]{2,1,0:T(8,128)(2,1)S(1)}, bf16[4,128,128]{2,1,0:T(8,128)(2,1)S(1)}, u32[]{:S(2)}, u32[]{:S(2)}) collective-permute-start(bf16[4,128,128]{2,1,0:T(8,128)(2,1)S(1)} %pad_maximum_fusion.2.x0), channel_id=1, source_target_pairs={{0,1},{1,0},{2,3},{3,2},{4,5},{5,4},{6,7},{7,6},{8,9},{9,8},{10,11... | collective-permute-start | bytes 393224 | tf_op jit(solution)/shard_map/ppermute | solution.py:26
  35.0 2.0 %collective-permute-start.10 = (bf16[768,256]{1,0:T(8,128)(2,1)S(1)}, bf16[768,256]{1,0:T(8,128)(2,1)S(1)}, u32[]{:S(2)}, u32[]{:S(2)}) collective-permute-start(bf16[768,256]{1,0:T(8,128)(2,1)S(1)} %collective-permute-done.6.refs_2_), channel_id=1, source_target_pairs={{0,1},{1,0},{2,3},{3,2},{4,5},{5,4},{6,7},{7,6},{8,9},{9,8},{10,11... | collective-permute-start | bytes 1179656 | tf_op jit(solution)/shard_map/ppermute | solution.py:26
  35.1 11.5 %collective-permute-start.13 = (bf16[128,1536]{1,0:T(8,128)(2,1)S(1)}, bf16[128,1536]{1,0:T(8,128)(2,1)S(1)}, u32[]{:S(2)}, u32[]{:S(2)}) collective-permute-start(bf16[128,1536]{1,0:T(8,128)(2,1)S(1)} %pad_maximum_fusion.1), channel_id=1, source_target_pairs={{0,12},{4,0},{8,4},{12,8},{1,13},{5,1},{9,5},{13,9},{2,14},{6,2},{... | collective-permute-start | bytes 1179656 | tf_op jit(solution)/shard_map/ppermute | solution.py:21
  35.2 11.4 %collective-permute-start.12 = (bf16[128,1536]{1,0:T(8,128)(2,1)S(1)}, bf16[128,1536]{1,0:T(8,128)(2,1)S(1)}, u32[]{:S(2)}, u32[]{:S(2)}) collective-permute-start(bf16[128,1536]{1,0:T(8,128)(2,1)S(1)} %pad_maximum_fusion), channel_id=1, source_target_pairs={{0,4},{4,8},{8,12},{12,0},{1,5},{5,9},{9,13},{13,1},{2,6},{6,10},{... | collective-permute-start | bytes 1179656 | tf_op jit(solution)/shard_map/ppermute | solution.py:21
  37.0 12.5 %collective-permute-start.14 = (bf16[768,256]{1,0:T(8,128)(2,1)S(1)}, bf16[768,256]{1,0:T(8,128)(2,1)S(1)}, u32[]{:S(2)}, u32[]{:S(2)}) collective-permute-start(bf16[768,256]{1,0:T(8,128)(2,1)S(1)} %get-tuple-element.47.refs_0_), channel_id=1, source_target_pairs={{0,2},{1,3},{2,0},{3,1},{4,6},{5,7},{6,4},{7,5},{8,10},{9,11},{10,... | collective-permute-start | bytes 1179656 | tf_op jit(solution)/shard_map/ppermute | solution.py:26
  38.3 11.2 %collective-permute-start.15 = (bf16[768,256]{1,0:T(8,128)(2,1)S(1)}, bf16[768,256]{1,0:T(8,128)(2,1)S(1)}, u32[]{:S(2)}, u32[]{:S(2)}) collective-permute-start(bf16[768,256]{1,0:T(8,128)(2,1)S(1)} %get-tuple-element.47.refs_0_), channel_id=1, source_target_pairs={{0,1},{1,0},{2,3},{3,2},{4,5},{5,4},{6,7},{7,6},{8,9},{9,8},{10,11... | collective-permute-start | bytes 1179656 | tf_op jit(solution)/shard_map/ppermute | solution.py:26
  39.9 1.5 %collective-permute-start.11 = (bf16[4,128,128]{2,1,0:T(8,128)(2,1)S(1)}, bf16[4,128,128]{2,1,0:T(8,128)(2,1)S(1)}, u32[]{:S(2)}, u32[]{:S(2)}) collective-permute-start(bf16[4,128,128]{2,1,0:T(8,128)(2,1)S(1)} %collective-permute-done.8.x2), channel_id=1, source_target_pairs={{0,1},{1,0},{2,3},{3,2},{4,5},{5,4},{6,7},{7,6},{8,9},{9,8},{10,11... | collective-permute-start | bytes 393224 | tf_op jit(solution)/shard_map/ppermute | solution.py:26
  49.5 5.9 %collective-permute-start.16 = (bf16[768,256]{1,0:T(8,128)(2,1)S(1)}, bf16[768,256]{1,0:T(8,128)(2,1)S(1)}, u32[]{:S(2)}, u32[]{:S(2)}) collective-permute-start(bf16[768,256]{1,0:T(8,128)(2,1)S(1)} %collective-permute-done.14.refs_2_), channel_id=1, source_target_pairs={{0,1},{1,0},{2,3},{3,2},{4,5},{5,4},{6,7},{7,6},{8,9},{9,8},{10,11... | collective-permute-start | bytes 1179656 | tf_op jit(solution)/shard_map/ppermute | solution.py:26

commit v2 on v1

v2 whole, which is shorter than its diff:
```python
import jax
import jax.numpy as jnp
from jax import lax
from jax.experimental import pallas as pl
from jax.experimental.pallas import tpu as pltpu
from jax.sharding import PartitionSpec as P

BLK = 128
PAIR = 2 * BLK
TILE = 512
P_SIZE = 512
F32 = jnp.float32
BF16 = jnp.bfloat16
VMEM = pl.BlockSpec(memory_space=pltpu.VMEM)
HBM = pl.BlockSpec(memory_space=pltpu.HBM)
SMEM = pl.BlockSpec(memory_space=pltpu.SMEM)
MIB = 1 << 20
SMALL = pl.CostEstimate(flops=1000, bytes_accessed=1000, transcendentals=0)


def shift(x, axis, step):
    n = lax.axis_size(axis)
    return lax.ppermute(x, axis, [(i, (i + step) % n) for i in range(n)])


def flip(x, axis, bit):
    n = lax.axis_size(axis)
    return lax.ppermute(x, axis, [(i, i ^ bit) for i in range(n)])


def at(block, size=BLK):
    return pl.ds(pl.multiple_of(block * size, size), size)


def places():
    return lax.axis_index("row"), lax.axis_index("col")


def dot(a, b):
    return jnp.dot(a, b, preferred_element_type=F32)


def dot_t(a, b):
    return lax.dot_general(a, b, (((1,), (1,)), ((), ())), preferred_element_type=F32)


def out(*shape, dtype=BF16):
    return jax.ShapeDtypeStruct(shape, dtype)


def params(mib):
    return pltpu.CompilerParams(vmem_limit_bytes=mib * MIB)


def add_rows(acc, child, which, s, map_s, piv_s, row, col, here, kids):
    for k in range(kids):

        @pl.when(map_s[0, which, row * kids + k] == piv_s[0, s, row])
        def _():
            for a in range(kids):
                t = map_s[0, which, col * kids + a] - col * here
                acc[s, :, at(t)] += child[0, k * BLK : (k + 1) * BLK, a * BLK : (a + 1) * BLK].astype(F32)


def add_cols(acc, child, which, s, map_s, piv_s, row, col, here, kids):
    for k in range(kids):

        @pl.when(map_s[0, which, col * kids + k] == piv_s[0, s, col])
        def _():
            for a in range(kids):
                t = map_s[0, which, row * kids + a] - row * here
                acc[s, at(t), :] += child[0, a * BLK : (a + 1) * BLK, k * BLK : (k + 1) * BLK].astype(F32)


def scalars(map_ref, piv_ref, map_s, piv_s, sem):
    first = pltpu.make_async_copy(map_ref, map_s, sem.at[0])
    second = pltpu.make_async_copy(piv_ref, piv_s, sem.at[1])
    first.start()
    second.start()
    first.wait()
    second.wait()


def each_block(map_s, col, here, kids, visit):
    place = jnp.int32(0)
    for t in range(here):
        hit = jnp.bool_(False)
        for a in range(kids):
            hit = hit | (map_s[0, 1, col * kids + a] - col * here == t)

        @pl.when(jnp.logical_not(hit))
        def _():
            visit(t, place)

        place = place + jnp.where(hit, 0, 1)


def early_kernel(map_ref, piv_ref, front, kept, rows_out, map_s, piv_s, rows_in, kid, sem):
    row, col = places()
    here = front.shape[1] // BLK
    kids = kept.shape[1] // BLK
    child = pltpu.make_async_copy(kept, kid, sem.at[2])
    child.start()
    scalars(map_ref, piv_ref, map_s, piv_s, sem)
    copies = []
    for s in range(2):
        pr = piv_s[0, s, row] - row * here
        copies.append(pltpu.make_async_copy(front.at[0, at(pr), :], rows_in.at[s], sem.at[s]))
    for c in copies:
        c.start()
    for c in copies:
        c.wait()
    child.wait()
    for s in range(2):
        for k in range(kids):

            @pl.when(map_s[0, 0, row * kids + k] == piv_s[0, s, row])
            def _():
                for a in range(kids):
                    t = at(map_s[0, 0, col * kids + a] - col * here)
                    piece = kid[0, k * BLK : (k + 1) * BLK, a * BLK : (a + 1) * BLK].astype(F32)
                    rows_in[s, :, t] = (rows_in[s, :, t].astype(F32) + piece).astype(BF16)

    def visit(t, place):
        for s in range(2):
            rows_out[s * BLK : (s + 1) * BLK, at(place)] = rows_in[s, :, t * BLK : (t + 1) * BLK]

    each_block(map_s, col, here, kids, visit)


def early(child_map, pivots, front, kept):
    span = front.shape[1]
    return pl.pallas_call(
        early_kernel,
        out_shape=out(PAIR, span - kept.shape[1]),
        in_specs=[HBM] * 4,
        out_specs=VMEM,
        scratch_shapes=[
            pltpu.SMEM(child_map.shape, jnp.int32),
            pltpu.SMEM(pivots.shape, jnp.int32),
            pltpu.VMEM((2, BLK, span), BF16),
            pltpu.VMEM(kept.shape, BF16),
            pltpu.SemaphoreType.DMA((3,)),
        ],
        compiler_params=params(57),
        cost_estimate=SMALL,
        name="early",
    )(child_map, pivots, front, kept)


def prepare_kernel(
    map_ref, piv_ref, front, kept, rows_out, cols32, map_s, piv_s, rows_in, cols_in, rows32, sem
):
    row, col = places()
    here = front.shape[1] // BLK
    kids = kept.shape[1] // BLK
    scalars(map_ref, piv_ref, map_s, piv_s, sem)
    copies = []
    for s in range(2):
        pr = piv_s[0, s, row] - row * here
        pc = piv_s[0, s, col] - col * here
        copies.append(pltpu.make_async_copy(front.at[0, at(pr), :], rows_in.at[s], sem.at[2 * s]))
        copies.append(pltpu.make_async_copy(front.at[0, :, at(pc)], cols_in.at[s], sem.at[2 * s + 1]))
    for c in copies:
        c.start()
    for c in copies:
        c.wait()
    rows32[...] = rows_in[...].astype(F32)
    cols32[...] = cols_in[...].astype(F32)
    for s in range(2):
        add_rows(rows32, kept, 0, s, map_s, piv_s, row, col, here, kids)
        add_cols(cols32, kept, 0, s, map_s, piv_s, row, col, here, kids)
        for a in range(kids):
            t = map_s[0, 1, col * kids + a] - col * here
            rows_out[s, :, a * BLK : (a + 1) * BLK] = rows32[s, :, at(t)]


def prepare(child_map, pivots, front, kept):
    span = front.shape[1]
    return pl.pallas_call(
        prepare_kernel,
        out_shape=(out(2, BLK, kept.shape[1], dtype=F32), out(2, span, BLK, dtype=F32)),
        in_specs=[HBM, HBM, HBM, VMEM],
        out_specs=(VMEM, VMEM),
        scratch_shapes=[
            pltpu.SMEM(child_map.shape, jnp.int32),
            pltpu.SMEM(pivots.shape, jnp.int32),
            pltpu.VMEM((2, BLK, span), BF16),
            pltpu.VMEM((2, span, BLK), BF16),
            pltpu.VMEM((2, BLK, span), F32),
            pltpu.SemaphoreType.DMA((4,)),
        ],
        compiler_params=params(12),
        cost_estimate=SMALL,
        name="prepare",
    )(child_map, pivots, front, kept)


def extract_kernel(map_s, piv_s, rows32, cols32, arrived, rows_out, top, bottom, cross, cols):
    row, col = places()
    here = cols.shape[0] // BLK
    kids = arrived.shape[1] // BLK
    for s in range(2):
        own = slice(s * BLK, (s + 1) * BLK)
        rows_out[own, : kids * BLK] = rows32[s].astype(BF16)
        cols[:, own] = cols32[s].astype(BF16)
        for k in range(kids):

            @pl.when(map_s[0, 1, row * kids + k] == piv_s[0, s, row])
            def _():
                piece = arrived[0, k * BLK : (k + 1) * BLK, :].astype(F32)
                rows_out[own, : kids * BLK] = (rows32[s] + piece).astype(BF16)

            @pl.when(map_s[0, 1, col * kids + k] == piv_s[0, s, col])
            def _():
                for a in range(kids):
                    t = map_s[0, 1, row * kids + a] - row * here
                    piece = arrived[0, a * BLK : (a + 1) * BLK, k * BLK : (k + 1) * BLK].astype(F32)
                    cols[at(t), own] = (cols32[s, at(t), :] + piece).astype(BF16)

    top[...] = cols[: top.shape[0], :]
    bottom[...] = cols[top.shape[0] :, :]
    block = cols[at(piv_s[0, 1, row] - row * here), :BLK]
    rows_out[:BLK, kids * BLK :] = block
    rows_out[BLK:, kids * BLK :] = jnp.zeros((BLK, BLK), BF16)
    cross[...] = block


def extract(child_map, pivots, rows32, cols32, arrived):
    span = cols32.shape[1]
    return pl.pallas_call(
        extract_kernel,
        out_shape=(
            out(PAIR, arrived.shape[1] + BLK),
            out(span - TILE, PAIR),
            out(TILE, PAIR),
            out(BLK, BLK),
        ),
        in_specs=[SMEM] * 2 + [VMEM] * 3,
        out_specs=(VMEM,) * 4,
        scratch_shapes=[pltpu.VMEM((span, PAIR), BF16)],
        compiler_params=params(8),
        cost_estimate=SMALL,
        name="extract",
    )(child_map, pivots, rows32, cols32, arrived)


def add_blocks(base, child, which, map_s, first, deep):
    row, col = places()
    here = base.shape[1] // BLK
    kids = child.shape[1] // BLK
    for k in range(kids):
        t = map_s[0, which, row * kids + k] - row * here

        @pl.when((t >= first) & (t < first + deep))
        def _():
            for a in range(kids):
                u = map_s[0, which, col * kids + a] - col * here
                piece = child[0, k * BLK : (k + 1) * BLK, a * BLK : (a + 1) * BLK]
                base[at(t), at(u)] += piece.astype(F32)


def make_base(child_map, front, kept):
    span = front.shape[1]
    steps = 4
    width = span // steps

    def kernel(map_s, front, kept, base):
        step = pl.program_id(0)
        base[at(step, width), :] = front[0].astype(F32)
        add_blocks(base, kept, 0, map_s, step * (width // BLK), width // BLK)

    return pl.pallas_call(
        kernel,
        grid=(steps,),
        out_shape=out(span, span, dtype=F32),
        in_specs=[SMEM, pl.BlockSpec((1, width, span), lambda i: (0, i, 0)), VMEM],
        out_specs=VMEM,
        compiler_params=params(14),
        cost_estimate=SMALL,
        name="base",
    )(child_map, front, kept)


def add_child(child_map, base, arrived):
    def kernel(map_s, _, arrived, base):
        add_blocks(base, arrived, 1, map_s, 0, base.shape[0] // BLK)

    return pl.pallas_call(
        kernel,
        out_shape=out(*base.shape, dtype=F32),
        in_specs=[SMEM, VMEM, VMEM],
        out_specs=VMEM,
        input_output_aliases={1: 0},
        compiler_params=params(4),
        cost_estimate=SMALL,
        name="add_child",
    )(child_map, base, arrived)


def stage(us, as_):
    split = us[0].shape[1]
    kid = as_[0].shape[1] - BLK

    def kernel(u0, u1, u2, a0, a1, a2, panel, onward):
        _, col = places()
        even = lax.rem(col, 2) == 0
        for n, (u, a) in enumerate(((u0, a0), (u1, a1), (u2, a2))):
            panel[n * PAIR : (n + 1) * PAIR, :split] = u[...]
            panel[n * PAIR : (n + 1) * PAIR, split:] = a[:, :kid]

        @pl.when(even)
        def _():
            onward[:, :split] = u2[...]
            onward[:, split:] = a2[:, :kid]

        @pl.when(jnp.logical_not(even))
        def _():
            onward[:, :split] = u1[...]
            onward[:, split:] = a1[:, :kid]

    return pl.pallas_call(
        kernel,
        out_shape=(out(2 * P_SIZE, split + kid), out(PAIR, split + kid)),
        in_specs=[VMEM] * 6,
        out_specs=(VMEM, VMEM),
        compiler_params=params(4),
        cost_estimate=SMALL,
        name="stage",
    )(*us, *as_)


def hand_on(x):
    rows, cols = lax.axis_size("row"), lax.axis_size("col")
    route = []
    for r in range(rows):
        for c in range(cols):
            to = (r + 1) % rows if c % 2 == 0 else (r - 1) % rows
            route.append((r * cols + c, to * cols + c))
    return lax.ppermute(x, ("row", "col"), route)


def begin(pieces, corners, inverse):
    span = pieces[0].shape[0]

    def kernel(c0, c1, c2, k0, k1, inverse, first, second):
        _, col = places()
        js = [lax.bitwise_xor(col, q) for q in range(4)]
        for n, corner in enumerate((k0, k1)):
            rows = slice(n * TILE, (n + 1) * TILE)
            total = dot(corner[:, :BLK], inverse[0, 0, at(js[3]), :])
            second[rows, at(js[3])] = corner[:, BLK:]
            for q, c in enumerate((c0, c1, c2)):
                total += dot(c[rows, :BLK], inverse[0, 0, at(js[q]), :])
                second[rows, at(js[q])] = c[rows, BLK:]
            first[rows, :] = total

    return pl.pallas_call(
        kernel,
        out_shape=(out(span, P_SIZE, dtype=F32), out(span, P_SIZE)),
        in_specs=[VMEM] * 6,
        out_specs=(VMEM, VMEM),
        compiler_params=params(6),
        cost_estimate=SMALL,
        name="begin",
    )(*pieces, *corners, inverse)


def ring_places(row):
    found = []
    for j in range(4):
        d = lax.rem(j - row + 4, 4)
        found.append(jnp.where(d < 2, d, 5 - d))
    return found


def eliminate(mult, rows, m1, i2, x, k, inverse, place):
    p2 = (i2.astype(F32) - dot_t(m1.astype(BF16), x[...])).astype(BF16)
    m2 = dot(p2, inverse[0, 1]).astype(BF16)
    n1 = (m1 - dot_t(m2, k[...])).astype(BF16)
    for j in range(4):
        b = slice(j * BLK, (j + 1) * BLK)
        mult[rows, at(2 * place[j])] = n1[:, b]
        mult[rows, at(2 * place[j] + 1)] = m2[:, b]


def multiply_top(crosses, first, second, inverse):
    span = first.shape[0]

    def kernel(x0, x1, x2, x3, x4, first, second, inverse, mult, x, k):
        row, col = places()
        for q, xq in enumerate((x0, x1, x2, (x3, x4))):
            j = lax.bitwise_xor(col, q)
            for d in range(4):
                x[at(lax.rem(row + d, 4)), at(j)] = xq[d // 2][d % 2] if q == 3 else xq[d]
        k[...] = dot_t(inverse[0, 0], x[...]).astype(BF16)
        place = ring_places(row)
        for r in range(0, span, TILE):
            rows = slice(r, r + TILE)
            eliminate(mult, rows, first[rows, :], second[rows, :], x, k, inverse, place)

    return pl.pallas_call(
        kernel,
        out_shape=(out(span, 2 * P_SIZE), out(P_SIZE, P_SIZE), out(P_SIZE, P_SIZE)),
        in_specs=[VMEM] * 8,
        out_specs=(VMEM,) * 3,
        compiler_params=params(8),
        cost_estimate=SMALL,
        name="multiply_top",
    )(*crosses, first, second, inverse)


def multiply_bottom(pieces, corners, x, k, inverse):
    span = pieces[0].shape[0]

    def kernel(c0, c1, c2, k0, k1, x, k, inverse, mult, p1, i2):
        row, col = places()
        for q, c in enumerate((c0, c1, c2)):
            j = lax.bitwise_xor(col, q)
            p1[:, at(j)] = c[:, :BLK]
            i2[:, at(j)] = c[:, BLK:]
        j = lax.bitwise_xor(col, 3)
        for n, corner in enumerate((k0, k1)):
            rows = slice(n * PAIR, (n + 1) * PAIR)
            p1[rows, at(j)] = corner[:, :BLK]
            i2[rows, at(j)] = corner[:, BLK:]
        m1 = dot(p1[...], inverse[0, 0])
        eliminate(mult, slice(0, span), m1, i2[...], x, k, inverse, ring_places(row))

    return pl.pallas_call(
        kernel,
        out_shape=out(span, 2 * P_SIZE),
        in_specs=[VMEM] * 8,
        out_specs=VMEM,
        scratch_shapes=[pltpu.VMEM((span, P_SIZE), BF16)] * 2,
        compiler_params=params(8),
        cost_estimate=SMALL,
        name="multiply_bottom",
    )(*pieces, *corners, x, k, inverse)


def update(child_map, mults, panel, far, base):
    span = base.shape[0]
    kids = child_map.shape[2] // 4
    blocks = span // BLK

    def kernel(map_s, top, bottom, _, far, base, updated, panel, order, done, sem):
        _, col = places()
        panel[3 * PAIR :, :] = far[...]

        def visit(t, place):
            order[place] = t

        each_block(map_s, col, blocks, kids, visit)
        for a in range(kids):
            order[blocks - kids + a] = map_s[0, 1, col * kids + a] - col * blocks

        def store(n):
            return pltpu.make_async_copy(done.at[n], updated.at[0, :, at(order[n])], sem.at[n])

        for n in range(0, blocks, TILE // BLK):
            for r in range(0, span, TILE):
                rows = slice(r, r + TILE)
                first = top.shape[0]
                part_of = top[rows, :] if r < first else bottom[r - first : r - first + TILE, :]
                total = dot(part_of, panel[:, n * BLK : n * BLK + TILE])
                for m in range(TILE // BLK):
                    part = total[:, m * BLK : (m + 1) * BLK]
                    done[n + m, rows, :] = (base[rows, at(order[n + m])] - part).astype(BF16)
            for m in range(TILE // BLK):
                store(n + m).start()
        for n in range(blocks):
            store(n).wait()

    return pl.pallas_call(
        kernel,
        out_shape=(out(1, span, span), out(*panel.shape)),
        in_specs=[SMEM] + [VMEM] * 5,
        out_specs=(HBM, VMEM),
        input_output_aliases={3: 1},
        scratch_shapes=[
            pltpu.SMEM((blocks,), jnp.int32),
            pltpu.VMEM((blocks, span, BLK), BF16),
            pltpu.SemaphoreType.DMA((blocks,)),
        ],
        compiler_params=params(14),
        cost_estimate=SMALL,
        name="update",
    )(child_map, *mults, panel, far, base)[0]


def body(front_matrix, kept_child, passed_child, child_map, pivots, pivot_inverse):
    hold = lax.optimization_barrier
    kid = kept_child.shape[1]
    arrived = flip(passed_child, "front", 1)
    u = early(child_map, pivots, front_matrix, kept_child)
    un, up = shift(u, "row", -1), shift(u, "row", 1)
    rows32, cols32 = prepare(child_map, pivots, front_matrix, kept_child)
    base = make_base(child_map, front_matrix, kept_child)
    arrived, _, rows32, cols32, base = hold((arrived, u, rows32, cols32, base))
    a, top, bottom, cross = extract(child_map, pivots, rows32, cols32, arrived)
    tfar, tnear = flip(top, "col", 2), flip(top, "col", 1)
    an, ap = shift(a, "row", -1), shift(a, "row", 1)
    cross2 = shift(cross, "row", 2)
    base = add_child(child_map, base, arrived)
    un, up, an, ap, cross2, base, tfar, tnear, bottom = hold(
        (un, up, an, ap, cross2, base, tfar, tnear, bottom)
    )
    panel, onward = stage((u, un, up), (a, an, ap))
    far = hand_on(onward)
    crosses = jnp.stack([cross, an[:BLK, kid:], cross2, ap[:BLK, kid:]])
    xfar, xnear = flip(crosses, "col", 2), flip(crosses, "col", 1)
    bfar, bnear = flip(bottom, "col", 2), flip(bottom, "col", 1)
    tcorners = [flip(tfar[n : n + TILE], "col", 1) for n in range(0, top.shape[0], TILE)]
    first, second = begin((top, tnear, tfar), tcorners, pivot_inverse)
    xfar, xnear, panel, first, second = hold((xfar, xnear, panel, first, second))
    xcorners = [flip(xfar[n : n + 2], "col", 1) for n in (0, 2)]
    upper, x, k = multiply_top((crosses, xnear, xfar, *xcorners), first, second, pivot_inverse)
    upper, bfar, bnear = hold((upper, bfar, bnear))
    bcorners = [flip(bfar[n : n + PAIR], "col", 1) for n in range(0, bottom.shape[0], PAIR)]
    lower = multiply_bottom((bottom, bnear, bfar), bcorners, x, k, pivot_inverse)
    lower, far = hold((lower, far))
    return update(child_map, (upper, lower), panel, far, base)


def solution(mesh):
    in_specs = (
        P("front", "row", "col"),
        P("front", "row", "col"),
        P("front", "row", "col"),
        P("front", None, None),
        P("front", None, None),
        P("front", None, None, None),
    )
    out_specs = P("front", "row", "col")
    return jax.shard_map(body, mesh=mesh, in_specs=in_specs, out_specs=out_specs, check_vma=False)
```

time: 59.8 us -> 56.8 us (0.950)
  Pallas kernels: 25.2 us -> 21 us
  waiting for transfers between devices: 10.6 us -> 12.3 us
    pallas_call x6 -> x7, Pallas kernels: 19.7 us -> 15.5 us  [the longest x1 7.19 us: update(): pl.pallas_call(kernel, out_shape=(out(1, span, span), out(*panel.shape)),...]
    ppermute x0 -> x1, starting transfers between devices: none -> 2.84 us  [hand_on(): return lax.ppermute(x, ('row', 'col'), route)]
    ppermute x7 -> x5, starting transfers between devices: 8.77 us -> 7.03 us  [shift(): return lax.ppermute(x, axis, [(i, (i + step) % n) for i in range(n)])]
    ppermute x10 -> x13, starting transfers between devices: 14.5 us -> 13 us  [flip(): return lax.ppermute(x, axis, [(i, i ^ bit) for i in range(n)])]
    ppermute x7 -> x5, waiting for transfers between devices: 5.59 us -> 6.89 us  [shift(): return lax.ppermute(x, axis, [(i, (i + step) % n) for i in range(n)])]
    ppermute x10 -> x13, waiting for transfers between devices: 5 us -> 5.44 us  [flip(): return lax.ppermute(x, axis, [(i, i ^ bit) for i in range(n)])]
  transfers between devices with their start and end apart: 17 -> 19, of which waited for: 5 -> 9; matrix products, arithmetic and copies ran while one was open for 0% -> 0% of each run, Pallas kernels for 35% -> 24%
where the time goes in v2:
time: 56.8 us; the launch traced here: 56.6 us
  starting transfers between devices  22.9 us (40%)
  Pallas kernels  21 us (37%)
  waiting for transfers between devices  12.3 us (22%)
    ppermute x13, starting transfers between devices, flip(): return lax.ppermute(x, axis, [(i, i ^ bit) for i in range(n)])  13 us
    pallas_call x1, Pallas kernels, update(): pl.pallas_call(kernel, out_shape=(out(1, span, span), out(*panel.shape)),...  7.19 us
    ppermute x5, starting transfers between devices, shift(): return lax.ppermute(x, axis, [(i, (i + step) % n) for i in range(n)])  7.03 us
    ppermute x5, waiting for transfers between devices, shift(): return lax.ppermute(x, axis, [(i, (i + step) % n) for i in range(n)])  6.89 us
    ppermute x13, waiting for transfers between devices, flip(): return lax.ppermute(x, axis, [(i, i ^ bit) for i in range(n)])  5.44 us
    pallas_call x1, Pallas kernels, early(): pl.pallas_call(early_kernel, out_shape=out(PAIR, span - kept.shape[1]), i...  3.01 us
    ppermute x1, starting transfers between devices, hand_on(): return lax.ppermute(x, ('row', 'col'), route)  2.84 us
    pallas_call x1, Pallas kernels, multiply_top(): pl.pallas_call(kernel, out_shape=(out(span, 2 * P_SIZE), out(P_SIZE, P_SI...  2.78 us
  transfers between devices with their start and end apart: 19, of which 9 were waited for; matrix products, arithmetic and copies ran while one was open for 0% of the time, Pallas kernels for 24%

profile of v2, /device:TPU:1, one launch (start us, length us, event | category | flops | bytes accessed | tf_op | source)
XLA Modules:
  0.0 56.6 jit_solution(3599713263230686464)
XLA Ops:
  0.0 3.7 %collective-permute-start = (bf16[1,512,512]{2,1,0:T(8,128)(2,1)}, bf16[1,512,512]{2,1,0:T(8,128)(2,1)S(1)}, u32[]{:S(2)}, u32[]{:S(2)}) collective-permute-start(bf16[1,512,512]{2,1,0:T(8,128)(2,1)} %param.8), channel_id=1, source_target_pairs={{0,16},{16,0},{32,48},{48,32},{64,80},{80,64},{96,112},{112,96},{1... | collective-permute-start | bytes 1572872 | tf_op jit(solution)/shard_map/ppermute | solution.py:28
  3.7 3.0 %early.1.u0 = bf16[256,1024]{1,0:T(8,128)(2,1)} custom-call(s32[1,2,16]{2,1,0:T(2,128)} %map_s.7, s32[1,2,4]{2,1,0:T(2,128)} %piv_s.1, bf16[1,1536,1536]{2,1,0:T(8,128)(2,1)} %front.5, bf16[1,512,512]{2,1,0:T(8,128)(2,1)} %kept.5), custom_call_target="tpu_custom_call" | custom-call | flops 1000 | bytes 1000 | tf_op jit(solution)/shard_map/early/pallas_call | solution.py:133
  6.7 1.4 %collective-permute-start.2 = (bf16[256,1024]{1,0:T(8,128)(2,1)}, bf16[256,1024]{1,0:T(8,128)(2,1)S(1)}, u32[]{:S(2)}, u32[]{:S(2)}) collective-permute-start(bf16[256,1024]{1,0:T(8,128)(2,1)} %early.1.u0), channel_id=1, source_target_pairs={{0,4},{4,8},{8,12},{12,0},{1,5},{5,9},{9,13},{13,1},{2,6},{6,10},{... | collective-permute-start | bytes 1572872 | tf_op jit(solution)/shard_map/ppermute | solution.py:23
  8.1 1.5 %collective-permute-start.1 = (bf16[256,1024]{1,0:T(8,128)(2,1)}, bf16[256,1024]{1,0:T(8,128)(2,1)S(1)}, u32[]{:S(2)}, u32[]{:S(2)}) collective-permute-start(bf16[256,1024]{1,0:T(8,128)(2,1)} %early.1.u0), channel_id=1, source_target_pairs={{0,12},{4,0},{8,4},{12,8},{1,13},{5,1},{9,5},{13,9},{2,14},{6,2},{... | collective-permute-start | bytes 1572872 | tf_op jit(solution)/shard_map/ppermute | solution.py:23
  9.6 1.5 %prepare.1 = (f32[2,128,512]{2,1,0:T(8,128)S(1)}, f32[2,1536,128]{2,1,0:T(8,128)S(1)}) custom-call(s32[1,2,16]{2,1,0:T(2,128)S(1)} %copy-done.4, s32[1,2,4]{2,1,0:T(2,128)S(1)} %copy-done.5, bf16[1,1536,1536]{2,1,0:T(8,128)(2,1)S(1)} %copy-done, bf16[1,512,512]{2,1,0:T(8,128)(2,1)S(1)} %copy-done.2), custom_call_target="tpu_custom_call" | custom-call | flops 1000 | bytes 1000 | tf_op jit(solution)/shard_map/prepare/pallas_call | solution.py:180
  11.2 1.6 %base.1._ = f32[1536,1536]{1,0:T(8,128)S(1)} custom-call(s32[1,2,16]{2,1,0:T(2,128)S(1)} %copy-done.4, bf16[1,1536,1536]{2,1,0:T(8,128)(2,1)S(1)} %copy-done, bf16[1,512,512]{2,1,0:T(8,128)(2,1)S(1)} %copy-done.2), custom_call_target="tpu_custom_call" | custom-call | flops 1000 | bytes 1000 | tf_op jit(solution)/shard_map/base/pallas_call | solution.py:273
  12.7 1.9 %collective-permute-done.arrived = bf16[1,512,512]{2,1,0:T(8,128)(2,1)S(1)} collective-permute-done((bf16[1,512,512]{2,1,0:T(8,128)(2,1)}, bf16[1,512,512]{2,1,0:T(8,128)(2,1)S(1)}, u32[]{:S(2)}, u32[]{:S(2)}) %collective-permute-start) | collective-permute-done | bytes 524320 | tf_op jit(solution)/shard_map/ppermute | solution.py:28
  14.6 0.9 %extract.1 = (bf16[256,640]{1,0:T(8,128)(2,1)S(1)}, bf16[1024,256]{1,0:T(8,128)(2,1)S(1)}, bf16[512,256]{1,0:T(8,128)(2,1)S(1)}, bf16[128,128]{1,0:T(8,128)(2,1)S(1)}) custom-call(s32[1,2,16]{2,1,0:T(2,128)S(1)} %copy-done.4, s32[1,2,4]{2,1,0:T(2,128)S(1)} %copy-done.5, f32[2,128,512]{2,1,0:T(8,128)S(1)} %get-tuple-element.44.rows32, ...), custom_call_target="tpu_custom_call" | custom-call | flops 1000 | bytes 1000 | tf_op jit(solution)/shard_map/extract/pallas_call | solution.py:231
  15.5 2.2 %collective-permute-start.7 = (bf16[1024,256]{1,0:T(8,128)(2,1)S(1)}, bf16[1024,256]{1,0:T(8,128)(2,1)S(1)}, u32[]{:S(2)}, u32[]{:S(2)}) collective-permute-start(bf16[1024,256]{1,0:T(8,128)(2,1)S(1)} %get-tuple-element.50.c0), channel_id=1, source_target_pairs={{0,1},{1,0},{2,3},{3,2},{4,5},{5,4},{6,7},{7,6},{8,9},{9,8},{10,11... | collective-permute-start | bytes 1572872 | tf_op jit(solution)/shard_map/ppermute | solution.py:28
  17.8 1.5 %collective-permute-start.6 = (bf16[1024,256]{1,0:T(8,128)(2,1)S(1)}, bf16[1024,256]{1,0:T(8,128)(2,1)S(1)}, u32[]{:S(2)}, u32[]{:S(2)}) collective-permute-start(bf16[1024,256]{1,0:T(8,128)(2,1)S(1)} %get-tuple-element.50.c0), channel_id=1, source_target_pairs={{0,2},{1,3},{2,0},{3,1},{4,6},{5,7},{6,4},{7,5},{8,10},{9,11},{10,... | collective-permute-start | bytes 1572872 | tf_op jit(solution)/shard_map/ppermute | solution.py:28
  19.2 1.3 %collective-permute-start.4 = (bf16[256,640]{1,0:T(8,128)(2,1)S(1)}, bf16[256,640]{1,0:T(8,128)(2,1)S(1)}, u32[]{:S(2)}, u32[]{:S(2)}) collective-permute-start(bf16[256,640]{1,0:T(8,128)(2,1)S(1)} %get-tuple-element.48.a0), channel_id=1, source_target_pairs={{0,4},{4,8},{8,12},{12,0},{1,5},{5,9},{9,13},{13,1},{2,6},{6,10},{... | collective-permute-start | bytes 983048 | tf_op jit(solution)/shard_map/ppermute | solution.py:23
  20.8 1.4 %collective-permute-start.3 = (bf16[256,640]{1,0:T(8,128)(2,1)S(1)}, bf16[256,640]{1,0:T(8,128)(2,1)S(1)}, u32[]{:S(2)}, u32[]{:S(2)}) collective-permute-start(bf16[256,640]{1,0:T(8,128)(2,1)S(1)} %get-tuple-element.48.a0), channel_id=1, source_target_pairs={{0,12},{4,0},{8,4},{12,8},{1,13},{5,1},{9,5},{13,9},{2,14},{6,2},{... | collective-permute-start | bytes 983048 | tf_op jit(solution)/shard_map/ppermute | solution.py:23
  22.2 1.4 %collective-permute-start.5 = (bf16[128,128]{1,0:T(8,128)(2,1)S(1)}, bf16[128,128]{1,0:T(8,128)(2,1)S(1)}, u32[]{:S(2)}, u32[]{:S(2)}) collective-permute-start(bf16[128,128]{1,0:T(8,128)(2,1)S(1)} %get-tuple-element.47), channel_id=1, source_target_pairs={{0,8},{4,12},{8,0},{12,4},{1,9},{5,13},{9,1},{13,5},{2,10},{6,14},... | collective-permute-start | bytes 98312 | tf_op jit(solution)/shard_map/ppermute | solution.py:23
  24.4 6.6 %collective-permute-done.5 = bf16[128,128]{1,0:T(8,128)(2,1)S(1)} collective-permute-done((bf16[128,128]{1,0:T(8,128)(2,1)S(1)}, bf16[128,128]{1,0:T(8,128)(2,1)S(1)}, u32[]{:S(2)}, u32[]{:S(2)}) %collective-permute-start.5) | collective-permute-done | bytes 32800 | tf_op jit(solution)/shard_map/ppermute | solution.py:23
  31.3 1.4 %collective-permute-start.11 = (bf16[512,256]{1,0:T(8,128)(2,1)S(1)}, bf16[512,256]{1,0:T(8,128)(2,1)S(1)}, u32[]{:S(2)}, u32[]{:S(2)}) collective-permute-start(bf16[512,256]{1,0:T(8,128)(2,1)S(1)} %get-tuple-element.79), channel_id=1, source_target_pairs={{0,1},{1,0},{2,3},{3,2},{4,5},{5,4},{6,7},{7,6},{8,9},{9,8},{10,11... | collective-permute-start | bytes 786440 | tf_op jit(solution)/shard_map/ppermute | solution.py:28
  33.3 1.0 %collective-permute-start.8 = (bf16[4,128,128]{2,1,0:T(8,128)(2,1)S(1)}, bf16[4,128,128]{2,1,0:T(8,128)(2,1)S(1)}, u32[]{:S(2)}, u32[]{:S(2)}) collective-permute-start(bf16[4,128,128]{2,1,0:T(8,128)(2,1)S(1)} %pad_maximum_fusion.x0), channel_id=1, source_target_pairs={{0,2},{1,3},{2,0},{3,1},{4,6},{5,7},{6,4},{7,5},{8,10},{9,11},{10,... | collective-permute-start | bytes 393224 | tf_op jit(solution)/shard_map/ppermute | solution.py:28
  34.5 2.8 %collective-permute-start.18 = (bf16[256,1536]{1,0:T(8,128)(2,1)S(1)}, bf16[256,1536]{1,0:T(8,128)(2,1)S(1)}, u32[]{:S(2)}, u32[]{:S(2)}) collective-permute-start(bf16[256,1536]{1,0:T(8,128)(2,1)S(1)} %get-tuple-element.73), channel_id=1, source_target_pairs={{0,4},{1,13},{2,6},{3,15},{4,8},{5,1},{6,10},{7,3},{8,12},{9,5},{1... | collective-permute-start | bytes 2359304 | tf_op jit(solution)/shard_map/ppermute | solution.py:340
  37.7 1.4 %begin.1 = (f32[1024,512]{1,0:T(8,128)S(1)}, bf16[1024,512]{1,0:T(8,128)(2,1)S(1)}) custom-call(bf16[1024,256]{1,0:T(8,128)(2,1)S(1)} %get-tuple-element.50.c0, bf16[1024,256]{1,0:T(8,128)(2,1)S(1)} %collective-permute-done.7.c1, bf16[1024,256]{1,0:T(8,128)(2,1)S(1)} %collective-permute-done.6.c2, bf16[512,256]{1,0:T(8,128)(2,1)S(1)} %collective-permute-done.10.k0, ...), custom_call_target="tpu_custom_call" | custom-call | flops 1000 | bytes 1000 | tf_op jit(solution)/shard_map/begin/pallas_call | solution.py:358
  41.2 2.8 %multiply_top.1 = (bf16[1024,1024]{1,0:T(8,128)(2,1)S(1)}, bf16[512,512]{1,0:T(8,128)(2,1)S(1)}, bf16[512,512]{1,0:T(8,128)(2,1)S(1)}) custom-call(bf16[4,128,128]{2,1,0:T(8,128)(2,1)S(1)} %pad_maximum_fusion.x0, bf16[4,128,128]{2,1,0:T(8,128)(2,1)S(1)} %collective-permute-done.9.x1, bf16[4,128,128]{2,1,0:T(8,128)(2,1)S(1)} %collective-permute-done.8.x2, ...), custom_call_target="tpu_custom_call" | custom-call | flops 1000 | bytes 1000 | tf_op jit(solution)/shard_map/multiply_top/pallas_call | solution.py:402
  44.0 1.0 %collective-permute-done.14.c2 = bf16[512,256]{1,0:T(8,128)(2,1)S(1)} collective-permute-done((bf16[512,256]{1,0:T(8,128)(2,1)S(1)}, bf16[512,256]{1,0:T(8,128)(2,1)S(1)}, u32[]{:S(2)}, u32[]{:S(2)}) %collective-permute-start.14) | collective-permute-done | bytes 262176 | tf_op jit(solution)/shard_map/ppermute | solution.py:28
  45.0 1.3 %collective-permute-start.17 = (bf16[256,256]{1,0:T(8,128)(2,1)S(1)}, bf16[256,256]{1,0:T(8,128)(2,1)S(1)}, u32[]{:S(2)}, u32[]{:S(2)}) collective-permute-start(bf16[256,256]{1,0:T(8,128)(2,1)S(1)} %get-tuple-element.81), channel_id=1, source_target_pairs={{0,1},{1,0},{2,3},{3,2},{4,5},{5,4},{6,7},{7,6},{8,9},{9,8},{10,11... | collective-permute-start | bytes 393224 | tf_op jit(solution)/shard_map/ppermute | solution.py:28
  46.4 0.9 %collective-permute-done.17.k1 = bf16[256,256]{1,0:T(8,128)(2,1)S(1)} collective-permute-done((bf16[256,256]{1,0:T(8,128)(2,1)S(1)}, bf16[256,256]{1,0:T(8,128)(2,1)S(1)}, u32[]{:S(2)}, u32[]{:S(2)}) %collective-permute-start.17) | collective-permute-done | bytes 131104 | tf_op jit(solution)/shard_map/ppermute | solution.py:28
  47.6 1.6 %multiply_bottom.1.bottom = bf16[512,1024]{1,0:T(8,128)(2,1)S(1)} custom-call(bf16[512,256]{1,0:T(8,128)(2,1)S(1)} %get-tuple-element.67.c0, bf16[512,256]{1,0:T(8,128)(2,1)S(1)} %collective-permute-done.15.c1, bf16[512,256]{1,0:T(8,128)(2,1)S(1)} %collective-permute-done.14.c2, bf16[256,256]{1,0:T(8,128)(2,1)S(1)} %collective-permute-done.16.k0, ...), custom_call_target="tpu_custom_call" | custom-call | flops 1000 | bytes 1000 | tf_op jit(solution)/shard_map/multiply_bottom/pallas_call | solution.py:430
  49.3 7.2 %update.1 = (bf16[1,1536,1536]{2,1,0:T(8,128)(2,1)}, bf16[1024,1536]{1,0:T(8,128)(2,1)S(1)}) custom-call(s32[1,2,16]{2,1,0:T(2,128)S(1)} %copy-done.4, bf16[1024,1024]{1,0:T(8,128)(2,1)S(1)} %get-tuple-element.68.top, bf16[512,1024]{1,0:T(8,128)(2,1)S(1)} %multiply_bottom.1.bottom, ...), custom_call_target="tpu_custom_call", output_to_operand_aliasing={{1}: (3, {})} | custom-call | flops 1000 | bytes 1000 | tf_op jit(solution)/shard_map/update/pallas_call | solution.py:475
  (41 shorter events, 5.0 us)
Async XLA Ops:
  0.0 9.6 %copy-start.4 = (s32[1,2,16]{2,1,0:T(2,128)S(1)}, s32[1,2,16]{2,1,0:T(2,128)}, u32[]{:S(2)}) copy-start(s32[1,2,16]{2,1,0:T(2,128)} %map_s.7) | copy-start | bytes 388
  0.0 9.6 %copy-start.5 = (s32[1,2,4]{2,1,0:T(2,128)S(1)}, s32[1,2,4]{2,1,0:T(2,128)}, u32[]{:S(2)}) copy-start(s32[1,2,4]{2,1,0:T(2,128)} %piv_s.1) | copy-start | bytes 100
  0.0 9.6 %copy-start.2 = (bf16[1,512,512]{2,1,0:T(8,128)(2,1)S(1)}, bf16[1,512,512]{2,1,0:T(8,128)(2,1)}, u32[]{:S(2)}) copy-start(bf16[1,512,512]{2,1,0:T(8,128)(2,1)} %kept.5) | copy-start | bytes 1572868
  0.0 14.6 %collective-permute-start = (bf16[1,512,512]{2,1,0:T(8,128)(2,1)}, bf16[1,512,512]{2,1,0:T(8,128)(2,1)S(1)}, u32[]{:S(2)}, u32[]{:S(2)}) collective-permute-start(bf16[1,512,512]{2,1,0:T(8,128)(2,1)} %param.8), channel_id=1, source_target_pairs={{0,16},{16,0},{32,48},{48,32},{64,80},{80,64},{96,112},{112,96},{1... | collective-permute-start | bytes 1572872 | tf_op jit(solution)/shard_map/ppermute | solution.py:28
  6.7 14.1 %collective-permute-start.2 = (bf16[256,1024]{1,0:T(8,128)(2,1)}, bf16[256,1024]{1,0:T(8,128)(2,1)S(1)}, u32[]{:S(2)}, u32[]{:S(2)}) collective-permute-start(bf16[256,1024]{1,0:T(8,128)(2,1)} %early.1.u0), channel_id=1, source_target_pairs={{0,4},{4,8},{8,12},{12,0},{1,5},{5,9},{9,13},{13,1},{2,6},{6,10},{... | collective-permute-start | bytes 1572872 | tf_op jit(solution)/shard_map/ppermute | solution.py:23
  8.1 14.1 %collective-permute-start.1 = (bf16[256,1024]{1,0:T(8,128)(2,1)}, bf16[256,1024]{1,0:T(8,128)(2,1)S(1)}, u32[]{:S(2)}, u32[]{:S(2)}) collective-permute-start(bf16[256,1024]{1,0:T(8,128)(2,1)} %early.1.u0), channel_id=1, source_target_pairs={{0,12},{4,0},{8,4},{12,8},{1,13},{5,1},{9,5},{13,9},{2,14},{6,2},{... | collective-permute-start | bytes 1572872 | tf_op jit(solution)/shard_map/ppermute | solution.py:23
  15.5 15.5 %collective-permute-start.7 = (bf16[1024,256]{1,0:T(8,128)(2,1)S(1)}, bf16[1024,256]{1,0:T(8,128)(2,1)S(1)}, u32[]{:S(2)}, u32[]{:S(2)}) collective-permute-start(bf16[1024,256]{1,0:T(8,128)(2,1)S(1)} %get-tuple-element.50.c0), channel_id=1, source_target_pairs={{0,1},{1,0},{2,3},{3,2},{4,5},{5,4},{6,7},{7,6},{8,9},{9,8},{10,11... | collective-permute-start | bytes 1572872 | tf_op jit(solution)/shard_map/ppermute | solution.py:28
  17.8 13.5 %collective-permute-start.6 = (bf16[1024,256]{1,0:T(8,128)(2,1)S(1)}, bf16[1024,256]{1,0:T(8,128)(2,1)S(1)}, u32[]{:S(2)}, u32[]{:S(2)}) collective-permute-start(bf16[1024,256]{1,0:T(8,128)(2,1)S(1)} %get-tuple-element.50.c0), channel_id=1, source_target_pairs={{0,2},{1,3},{2,0},{3,1},{4,6},{5,7},{6,4},{7,5},{8,10},{9,11},{10,... | collective-permute-start | bytes 1572872 | tf_op jit(solution)/shard_map/ppermute | solution.py:28
  19.2 11.8 %collective-permute-start.4 = (bf16[256,640]{1,0:T(8,128)(2,1)S(1)}, bf16[256,640]{1,0:T(8,128)(2,1)S(1)}, u32[]{:S(2)}, u32[]{:S(2)}) collective-permute-start(bf16[256,640]{1,0:T(8,128)(2,1)S(1)} %get-tuple-element.48.a0), channel_id=1, source_target_pairs={{0,4},{4,8},{8,12},{12,0},{1,5},{5,9},{9,13},{13,1},{2,6},{6,10},{... | collective-permute-start | bytes 983048 | tf_op jit(solution)/shard_map/ppermute | solution.py:23
  20.8 10.2 %collective-permute-start.3 = (bf16[256,640]{1,0:T(8,128)(2,1)S(1)}, bf16[256,640]{1,0:T(8,128)(2,1)S(1)}, u32[]{:S(2)}, u32[]{:S(2)}) collective-permute-start(bf16[256,640]{1,0:T(8,128)(2,1)S(1)} %get-tuple-element.48.a0), channel_id=1, source_target_pairs={{0,12},{4,0},{8,4},{12,8},{1,13},{5,1},{9,5},{13,9},{2,14},{6,2},{... | collective-permute-start | bytes 983048 | tf_op jit(solution)/shard_map/ppermute | solution.py:23
  22.2 12.1 %copy-start.3 = (bf16[256,1024]{1,0:T(8,128)(2,1)S(1)}, bf16[256,1024]{1,0:T(8,128)(2,1)}, u32[]{:S(2)}) copy-start(bf16[256,1024]{1,0:T(8,128)(2,1)} %early.1.u0) | copy-start | bytes 1572868
  22.2 8.8 %collective-permute-start.5 = (bf16[128,128]{1,0:T(8,128)(2,1)S(1)}, bf16[128,128]{1,0:T(8,128)(2,1)S(1)}, u32[]{:S(2)}, u32[]{:S(2)}) collective-permute-start(bf16[128,128]{1,0:T(8,128)(2,1)S(1)} %get-tuple-element.47), channel_id=1, source_target_pairs={{0,8},{4,12},{8,0},{12,4},{1,9},{5,13},{9,1},{13,5},{2,10},{6,14},... | collective-permute-start | bytes 98312 | tf_op jit(solution)/shard_map/ppermute | solution.py:23
  24.4 13.3 %copy-start.1 = (bf16[1,2,512,512]{3,2,1,0:T(8,128)(2,1)S(1)}, bf16[1,2,512,512]{3,2,1,0:T(8,128)(2,1)}, u32[]{:S(2)}) copy-start(bf16[1,2,512,512]{3,2,1,0:T(8,128)(2,1)} %inverse.5) | copy-start | bytes 3145732
  31.3 6.1 %collective-permute-start.11 = (bf16[512,256]{1,0:T(8,128)(2,1)S(1)}, bf16[512,256]{1,0:T(8,128)(2,1)S(1)}, u32[]{:S(2)}, u32[]{:S(2)}) collective-permute-start(bf16[512,256]{1,0:T(8,128)(2,1)S(1)} %get-tuple-element.79), channel_id=1, source_target_pairs={{0,1},{1,0},{2,3},{3,2},{4,5},{5,4},{6,7},{7,6},{8,9},{9,8},{10,11... | collective-permute-start | bytes 786440 | tf_op jit(solution)/shard_map/ppermute | solution.py:28
  32.7 4.7 %collective-permute-start.10 = (bf16[512,256]{1,0:T(8,128)(2,1)S(1)}, bf16[512,256]{1,0:T(8,128)(2,1)S(1)}, u32[]{:S(2)}, u32[]{:S(2)}) collective-permute-start(bf16[512,256]{1,0:T(8,128)(2,1)S(1)} %get-tuple-element.80), channel_id=1, source_target_pairs={{0,1},{1,0},{2,3},{3,2},{4,5},{5,4},{6,7},{7,6},{8,9},{9,8},{10,11... | collective-permute-start | bytes 786440 | tf_op jit(solution)/shard_map/ppermute | solution.py:28
  32.8 6.3 %collective-permute-start.9 = (bf16[4,128,128]{2,1,0:T(8,128)(2,1)S(1)}, bf16[4,128,128]{2,1,0:T(8,128)(2,1)S(1)}, u32[]{:S(2)}, u32[]{:S(2)}) collective-permute-start(bf16[4,128,128]{2,1,0:T(8,128)(2,1)S(1)} %pad_maximum_fusion.x0), channel_id=1, source_target_pairs={{0,1},{1,0},{2,3},{3,2},{4,5},{5,4},{6,7},{7,6},{8,9},{9,8},{10,11... | collective-permute-start | bytes 393224 | tf_op jit(solution)/shard_map/ppermute | solution.py:28
  33.3 5.8 %collective-permute-start.8 = (bf16[4,128,128]{2,1,0:T(8,128)(2,1)S(1)}, bf16[4,128,128]{2,1,0:T(8,128)(2,1)S(1)}, u32[]{:S(2)}, u32[]{:S(2)}) collective-permute-start(bf16[4,128,128]{2,1,0:T(8,128)(2,1)S(1)} %pad_maximum_fusion.x0), channel_id=1, source_target_pairs={{0,2},{1,3},{2,0},{3,1},{4,6},{5,7},{6,4},{7,5},{8,10},{9,11},{10,... | collective-permute-start | bytes 393224 | tf_op jit(solution)/shard_map/ppermute | solution.py:28
  34.5 14.7 %collective-permute-start.18 = (bf16[256,1536]{1,0:T(8,128)(2,1)S(1)}, bf16[256,1536]{1,0:T(8,128)(2,1)S(1)}, u32[]{:S(2)}, u32[]{:S(2)}) collective-permute-start(bf16[256,1536]{1,0:T(8,128)(2,1)S(1)} %get-tuple-element.73), channel_id=1, source_target_pairs={{0,4},{1,13},{2,6},{3,15},{4,8},{5,1},{6,10},{7,3},{8,12},{9,5},{1... | collective-permute-start | bytes 2359304 | tf_op jit(solution)/shard_map/ppermute | solution.py:340
  37.4 6.6 %collective-permute-start.15 = (bf16[512,256]{1,0:T(8,128)(2,1)S(1)}, bf16[512,256]{1,0:T(8,128)(2,1)S(1)}, u32[]{:S(2)}, u32[]{:S(2)}) collective-permute-start(bf16[512,256]{1,0:T(8,128)(2,1)S(1)} %get-tuple-element.67.c0), channel_id=1, source_target_pairs={{0,1},{1,0},{2,3},{3,2},{4,5},{5,4},{6,7},{7,6},{8,9},{9,8},{10,11... | collective-permute-start | bytes 786440 | tf_op jit(solution)/shard_map/ppermute | solution.py:28
  37.4 7.6 %collective-permute-start.14 = (bf16[512,256]{1,0:T(8,128)(2,1)S(1)}, bf16[512,256]{1,0:T(8,128)(2,1)S(1)}, u32[]{:S(2)}, u32[]{:S(2)}) collective-permute-start(bf16[512,256]{1,0:T(8,128)(2,1)S(1)} %get-tuple-element.67.c0), channel_id=1, source_target_pairs={{0,2},{1,3},{2,0},{3,1},{4,6},{5,7},{6,4},{7,5},{8,10},{9,11},{10,... | collective-permute-start | bytes 786440 | tf_op jit(solution)/shard_map/ppermute | solution.py:28
  39.1 1.7 %collective-permute-start.13 = (bf16[2,128,128]{2,1,0:T(8,128)(2,1)S(1)}, bf16[2,128,128]{2,1,0:T(8,128)(2,1)S(1)}, u32[]{:S(2)}, u32[]{:S(2)}) collective-permute-start(bf16[2,128,128]{2,1,0:T(8,128)(2,1)S(1)} %get-tuple-element.83), channel_id=1, source_target_pairs={{0,1},{1,0},{2,3},{3,2},{4,5},{5,4},{6,7},{7,6},{8,9},{9,8},{10,11... | collective-permute-start | bytes 196616 | tf_op jit(solution)/shard_map/ppermute | solution.py:28
  39.9 1.3 %collective-permute-start.12 = (bf16[2,128,128]{2,1,0:T(8,128)(2,1)S(1)}, bf16[2,128,128]{2,1,0:T(8,128)(2,1)S(1)}, u32[]{:S(2)}, u32[]{:S(2)}) collective-permute-start(bf16[2,128,128]{2,1,0:T(8,128)(2,1)S(1)} %get-tuple-element.84), channel_id=1, source_target_pairs={{0,1},{1,0},{2,3},{3,2},{4,5},{5,4},{6,7},{7,6},{8,9},{9,8},{10,11... | collective-permute-start | bytes 196616 | tf_op jit(solution)/shard_map/ppermute | solution.py:28
  45.0 2.3 %collective-permute-start.17 = (bf16[256,256]{1,0:T(8,128)(2,1)S(1)}, bf16[256,256]{1,0:T(8,128)(2,1)S(1)}, u32[]{:S(2)}, u32[]{:S(2)}) collective-permute-start(bf16[256,256]{1,0:T(8,128)(2,1)S(1)} %get-tuple-element.81), channel_id=1, source_target_pairs={{0,1},{1,0},{2,3},{3,2},{4,5},{5,4},{6,7},{7,6},{8,9},{9,8},{10,11... | collective-permute-start | bytes 393224 | tf_op jit(solution)/shard_map/ppermute | solution.py:28
  46.3 1.3 %collective-permute-start.16 = (bf16[256,256]{1,0:T(8,128)(2,1)S(1)}, bf16[256,256]{1,0:T(8,128)(2,1)S(1)}, u32[]{:S(2)}, u32[]{:S(2)}) collective-permute-start(bf16[256,256]{1,0:T(8,128)(2,1)S(1)} %get-tuple-element.82), channel_id=1, source_target_pairs={{0,1},{1,0},{2,3},{3,2},{4,5},{5,4},{6,7},{7,6},{8,9},{9,8},{10,11... | collective-permute-start | bytes 393224 | tf_op jit(solution)/shard_map/ppermute | solution.py:28
  (1 other events, 9.6 us)

commit v3 on v2

--- a/solution.py
+++ b/solution.py
@@ -343,11 +343,12 @@
 def begin(pieces, corners, inverse):
     span = pieces[0].shape[0]
 
-    def kernel(c0, c1, c2, k0, k1, inverse, first, second):
+    def kernel(c0, c1, c2, *rest):
+        *corners, inverse, first, second = rest
         _, col = places()
         js = [lax.bitwise_xor(col, q) for q in range(4)]
-        for n, corner in enumerate((k0, k1)):
-            rows = slice(n * TILE, (n + 1) * TILE)
+        for n, corner in enumerate(corners):
+            rows = slice(n * PAIR, (n + 1) * PAIR)
             total = dot(corner[:, :BLK], inverse[0, 0, at(js[3]), :])
             second[rows, at(js[3])] = corner[:, BLK:]
             for q, c in enumerate((c0, c1, c2)):
@@ -358,7 +359,7 @@
     return pl.pallas_call(
         kernel,
         out_shape=(out(span, P_SIZE, dtype=F32), out(span, P_SIZE)),
-        in_specs=[VMEM] * 6,
+        in_specs=[VMEM] * (4 + len(corners)),
         out_specs=(VMEM, VMEM),
         compiler_params=params(6),
         cost_estimate=SMALL,
@@ -458,17 +459,20 @@
         def store(n):
             return pltpu.make_async_copy(done.at[n], updated.at[0, :, at(order[n])], sem.at[n])
 
-        for n in range(0, blocks, TILE // BLK):
+        n = 0
+        while n < blocks:
+            count = TILE // BLK if blocks - n > TILE // BLK else 2
             for r in range(0, span, TILE):
                 rows = slice(r, r + TILE)
                 first = top.shape[0]
                 part_of = top[rows, :] if r < first else bottom[r - first : r - first + TILE, :]
-                total = dot(part_of, panel[:, n * BLK : n * BLK + TILE])
-                for m in range(TILE // BLK):
+                total = dot(part_of, panel[:, n * BLK : (n + count) * BLK])
+                for m in range(count):
                     part = total[:, m * BLK : (m + 1) * BLK]
                     done[n + m, rows, :] = (base[rows, at(order[n + m])] - part).astype(BF16)
-            for m in range(TILE // BLK):
+            for m in range(count):
                 store(n + m).start()
+            n += count
         for n in range(blocks):
             store(n).wait()
 
@@ -511,10 +515,11 @@
     crosses = jnp.stack([cross, an[:BLK, kid:], cross2, ap[:BLK, kid:]])
     xfar, xnear = flip(crosses, "col", 2), flip(crosses, "col", 1)
     bfar, bnear = flip(bottom, "col", 2), flip(bottom, "col", 1)
-    tcorners = [flip(tfar[n : n + TILE], "col", 1) for n in range(0, top.shape[0], TILE)]
+    tcorners = [flip(tfar[n : n + PAIR], "col", 1) for n in range(0, top.shape[0], PAIR)]
+    xfar, xnear, panel = hold((xfar, xnear, panel))
+    xcorners = [flip(xfar[n : n + 2], "col", 1) for n in (0, 2)]
     first, second = begin((top, tnear, tfar), tcorners, pivot_inverse)
-    xfar, xnear, panel, first, second = hold((xfar, xnear, panel, first, second))
-    xcorners = [flip(xfar[n : n + 2], "col", 1) for n in (0, 2)]
+    first, second, xcorners = hold((first, second, xcorners))
     upper, x, k = multiply_top((crosses, xnear, xfar, *xcorners), first, second, pivot_inverse)
     upper, bfar, bnear = hold((upper, bfar, bnear))
     bcorners = [flip(bfar[n : n + PAIR], "col", 1) for n in range(0, bottom.shape[0], PAIR)]

time: 56.8 us -> 56.9 us (level)
  starting transfers between devices: 22.9 us -> 24.1 us
  waiting for transfers between devices: 12.3 us -> 11.3 us
    ppermute x13 -> x15, starting transfers between devices: 13 us -> 14.3 us  [flip(): return lax.ppermute(x, axis, [(i, i ^ bit) for i in range(n)])]
    ppermute x13 -> x15, waiting for transfers between devices: 5.44 us -> 4.38 us  [flip(): return lax.ppermute(x, axis, [(i, i ^ bit) for i in range(n)])]
  transfers between devices with their start and end apart: 19 -> 21, of which waited for: 9 -> 8; matrix products, arithmetic and copies ran while one was open for 0% -> 0% of each run, Pallas kernels for 24% -> 24%
where the time goes in v3:
time: 56.9 us; the launch traced here: 56.8 us
  starting transfers between devices  24.1 us (42%)
  Pallas kernels  21 us (37%)
  waiting for transfers between devices  11.3 us (20%)
    ppermute x15, starting transfers between devices, flip(): return lax.ppermute(x, axis, [(i, i ^ bit) for i in range(n)])  14.3 us
    pallas_call x1, Pallas kernels, update(): pl.pallas_call(kernel, out_shape=(out(1, span, span), out(*panel.shape)),...  7.09 us
    ppermute x5, starting transfers between devices, shift(): return lax.ppermute(x, axis, [(i, (i + step) % n) for i in range(n)])  7.01 us
    ppermute x5, waiting for transfers between devices, shift(): return lax.ppermute(x, axis, [(i, (i + step) % n) for i in range(n)])  6.88 us
    ppermute x15, waiting for transfers between devices, flip(): return lax.ppermute(x, axis, [(i, i ^ bit) for i in range(n)])  4.38 us
    pallas_call x1, Pallas kernels, early(): pl.pallas_call(early_kernel, out_shape=out(PAIR, span - kept.shape[1]), i...  3.01 us
    ppermute x1, starting transfers between devices, hand_on(): return lax.ppermute(x, ('row', 'col'), route)  2.81 us
    pallas_call x1, Pallas kernels, multiply_top(): pl.pallas_call(kernel, out_shape=(out(span, 2 * P_SIZE), out(P_SIZE, P_SI...  2.77 us
  transfers between devices with their start and end apart: 21, of which 8 were waited for; matrix products, arithmetic and copies ran while one was open for 0% of the time, Pallas kernels for 24%

profile of v3, /device:TPU:1, one launch (start us, length us, event | category | flops | bytes accessed | tf_op | source)
XLA Modules:
  0.0 56.8 jit_solution(13129178159994803076)
XLA Ops:
  0.0 3.7 %collective-permute-start = (bf16[1,512,512]{2,1,0:T(8,128)(2,1)}, bf16[1,512,512]{2,1,0:T(8,128)(2,1)S(1)}, u32[]{:S(2)}, u32[]{:S(2)}) collective-permute-start(bf16[1,512,512]{2,1,0:T(8,128)(2,1)} %param.8), channel_id=1, source_target_pairs={{0,16},{16,0},{32,48},{48,32},{64,80},{80,64},{96,112},{112,96},{1... | collective-permute-start | bytes 1572872 | tf_op jit(solution)/shard_map/ppermute | solution.py:28
  3.7 3.0 %early.1.u0 = bf16[256,1024]{1,0:T(8,128)(2,1)} custom-call(s32[1,2,16]{2,1,0:T(2,128)} %map_s.7, s32[1,2,4]{2,1,0:T(2,128)} %piv_s.1, bf16[1,1536,1536]{2,1,0:T(8,128)(2,1)} %front.5, bf16[1,512,512]{2,1,0:T(8,128)(2,1)} %kept.5), custom_call_target="tpu_custom_call" | custom-call | flops 1000 | bytes 1000 | tf_op jit(solution)/shard_map/early/pallas_call | solution.py:133
  6.7 1.5 %collective-permute-start.2 = (bf16[256,1024]{1,0:T(8,128)(2,1)}, bf16[256,1024]{1,0:T(8,128)(2,1)S(1)}, u32[]{:S(2)}, u32[]{:S(2)}) collective-permute-start(bf16[256,1024]{1,0:T(8,128)(2,1)} %early.1.u0), channel_id=1, source_target_pairs={{0,4},{4,8},{8,12},{12,0},{1,5},{5,9},{9,13},{13,1},{2,6},{6,10},{... | collective-permute-start | bytes 1572872 | tf_op jit(solution)/shard_map/ppermute | solution.py:23
  8.2 1.4 %collective-permute-start.1 = (bf16[256,1024]{1,0:T(8,128)(2,1)}, bf16[256,1024]{1,0:T(8,128)(2,1)S(1)}, u32[]{:S(2)}, u32[]{:S(2)}) collective-permute-start(bf16[256,1024]{1,0:T(8,128)(2,1)} %early.1.u0), channel_id=1, source_target_pairs={{0,12},{4,0},{8,4},{12,8},{1,13},{5,1},{9,5},{13,9},{2,14},{6,2},{... | collective-permute-start | bytes 1572872 | tf_op jit(solution)/shard_map/ppermute | solution.py:23
  9.6 1.6 %prepare.1 = (f32[2,128,512]{2,1,0:T(8,128)S(1)}, f32[2,1536,128]{2,1,0:T(8,128)S(1)}) custom-call(s32[1,2,16]{2,1,0:T(2,128)S(1)} %copy-done.4, s32[1,2,4]{2,1,0:T(2,128)S(1)} %copy-done.5, bf16[1,1536,1536]{2,1,0:T(8,128)(2,1)S(1)} %copy-done, bf16[1,512,512]{2,1,0:T(8,128)(2,1)S(1)} %copy-done.2), custom_call_target="tpu_custom_call" | custom-call | flops 1000 | bytes 1000 | tf_op jit(solution)/shard_map/prepare/pallas_call | solution.py:180
  11.2 1.6 %base.1._ = f32[1536,1536]{1,0:T(8,128)S(1)} custom-call(s32[1,2,16]{2,1,0:T(2,128)S(1)} %copy-done.4, bf16[1,1536,1536]{2,1,0:T(8,128)(2,1)S(1)} %copy-done, bf16[1,512,512]{2,1,0:T(8,128)(2,1)S(1)} %copy-done.2), custom_call_target="tpu_custom_call" | custom-call | flops 1000 | bytes 1000 | tf_op jit(solution)/shard_map/base/pallas_call | solution.py:273
  12.8 1.8 %collective-permute-done.arrived = bf16[1,512,512]{2,1,0:T(8,128)(2,1)S(1)} collective-permute-done((bf16[1,512,512]{2,1,0:T(8,128)(2,1)}, bf16[1,512,512]{2,1,0:T(8,128)(2,1)S(1)}, u32[]{:S(2)}, u32[]{:S(2)}) %collective-permute-start) | collective-permute-done | bytes 524320 | tf_op jit(solution)/shard_map/ppermute | solution.py:28
  14.6 1.0 %extract.1 = (bf16[256,640]{1,0:T(8,128)(2,1)S(1)}, bf16[1024,256]{1,0:T(8,128)(2,1)S(1)}, bf16[512,256]{1,0:T(8,128)(2,1)S(1)}, bf16[128,128]{1,0:T(8,128)(2,1)S(1)}) custom-call(s32[1,2,16]{2,1,0:T(2,128)S(1)} %copy-done.4, s32[1,2,4]{2,1,0:T(2,128)S(1)} %copy-done.5, f32[2,128,512]{2,1,0:T(8,128)S(1)} %get-tuple-element.46.rows32, ...), custom_call_target="tpu_custom_call" | custom-call | flops 1000 | bytes 1000 | tf_op jit(solution)/shard_map/extract/pallas_call | solution.py:231
  15.6 2.2 %collective-permute-start.7 = (bf16[1024,256]{1,0:T(8,128)(2,1)S(1)}, bf16[1024,256]{1,0:T(8,128)(2,1)S(1)}, u32[]{:S(2)}, u32[]{:S(2)}) collective-permute-start(bf16[1024,256]{1,0:T(8,128)(2,1)S(1)} %get-tuple-element.52.c0), channel_id=1, source_target_pairs={{0,1},{1,0},{2,3},{3,2},{4,5},{5,4},{6,7},{7,6},{8,9},{9,8},{10,11... | collective-permute-start | bytes 1572872 | tf_op jit(solution)/shard_map/ppermute | solution.py:28
  17.8 1.4 %collective-permute-start.6 = (bf16[1024,256]{1,0:T(8,128)(2,1)S(1)}, bf16[1024,256]{1,0:T(8,128)(2,1)S(1)}, u32[]{:S(2)}, u32[]{:S(2)}) collective-permute-start(bf16[1024,256]{1,0:T(8,128)(2,1)S(1)} %get-tuple-element.52.c0), channel_id=1, source_target_pairs={{0,2},{1,3},{2,0},{3,1},{4,6},{5,7},{6,4},{7,5},{8,10},{9,11},{10,... | collective-permute-start | bytes 1572872 | tf_op jit(solution)/shard_map/ppermute | solution.py:28
  19.2 1.3 %collective-permute-start.4 = (bf16[256,640]{1,0:T(8,128)(2,1)S(1)}, bf16[256,640]{1,0:T(8,128)(2,1)S(1)}, u32[]{:S(2)}, u32[]{:S(2)}) collective-permute-start(bf16[256,640]{1,0:T(8,128)(2,1)S(1)} %get-tuple-element.50.a0), channel_id=1, source_target_pairs={{0,4},{4,8},{8,12},{12,0},{1,5},{5,9},{9,13},{13,1},{2,6},{6,10},{... | collective-permute-start | bytes 983048 | tf_op jit(solution)/shard_map/ppermute | solution.py:23
  20.8 1.4 %collective-permute-start.3 = (bf16[256,640]{1,0:T(8,128)(2,1)S(1)}, bf16[256,640]{1,0:T(8,128)(2,1)S(1)}, u32[]{:S(2)}, u32[]{:S(2)}) collective-permute-start(bf16[256,640]{1,0:T(8,128)(2,1)S(1)} %get-tuple-element.50.a0), channel_id=1, source_target_pairs={{0,12},{4,0},{8,4},{12,8},{1,13},{5,1},{9,5},{13,9},{2,14},{6,2},{... | collective-permute-start | bytes 983048 | tf_op jit(solution)/shard_map/ppermute | solution.py:23
  22.2 1.4 %collective-permute-start.5 = (bf16[128,128]{1,0:T(8,128)(2,1)S(1)}, bf16[128,128]{1,0:T(8,128)(2,1)S(1)}, u32[]{:S(2)}, u32[]{:S(2)}) collective-permute-start(bf16[128,128]{1,0:T(8,128)(2,1)S(1)} %get-tuple-element.49), channel_id=1, source_target_pairs={{0,8},{4,12},{8,0},{12,4},{1,9},{5,13},{9,1},{13,5},{2,10},{6,14},... | collective-permute-start | bytes 98312 | tf_op jit(solution)/shard_map/ppermute | solution.py:23
  24.4 6.6 %collective-permute-done.5 = bf16[128,128]{1,0:T(8,128)(2,1)S(1)} collective-permute-done((bf16[128,128]{1,0:T(8,128)(2,1)S(1)}, bf16[128,128]{1,0:T(8,128)(2,1)S(1)}, u32[]{:S(2)}, u32[]{:S(2)}) %collective-permute-start.5) | collective-permute-done | bytes 32800 | tf_op jit(solution)/shard_map/ppermute | solution.py:23
  31.3 1.3 %collective-permute-start.9 = (bf16[4,128,128]{2,1,0:T(8,128)(2,1)S(1)}, bf16[4,128,128]{2,1,0:T(8,128)(2,1)S(1)}, u32[]{:S(2)}, u32[]{:S(2)}) collective-permute-start(bf16[4,128,128]{2,1,0:T(8,128)(2,1)S(1)} %pad_maximum_fusion.x0), channel_id=1, source_target_pairs={{0,1},{1,0},{2,3},{3,2},{4,5},{5,4},{6,7},{7,6},{8,9},{9,8},{10,11... | collective-permute-start | bytes 393224 | tf_op jit(solution)/shard_map/ppermute | solution.py:28
  32.7 1.0 %collective-permute-start.8 = (bf16[4,128,128]{2,1,0:T(8,128)(2,1)S(1)}, bf16[4,128,128]{2,1,0:T(8,128)(2,1)S(1)}, u32[]{:S(2)}, u32[]{:S(2)}) collective-permute-start(bf16[4,128,128]{2,1,0:T(8,128)(2,1)S(1)} %pad_maximum_fusion.x0), channel_id=1, source_target_pairs={{0,2},{1,3},{2,0},{3,1},{4,6},{5,7},{6,4},{7,5},{8,10},{9,11},{10,... | collective-permute-start | bytes 393224 | tf_op jit(solution)/shard_map/ppermute | solution.py:28
  34.6 2.8 %collective-permute-start.20 = (bf16[256,1536]{1,0:T(8,128)(2,1)S(1)}, bf16[256,1536]{1,0:T(8,128)(2,1)S(1)}, u32[]{:S(2)}, u32[]{:S(2)}) collective-permute-start(bf16[256,1536]{1,0:T(8,128)(2,1)S(1)} %get-tuple-element.77), channel_id=1, source_target_pairs={{0,4},{1,13},{2,6},{3,15},{4,8},{5,1},{6,10},{7,3},{8,12},{9,5},{1... | collective-permute-start | bytes 2359304 | tf_op jit(solution)/shard_map/ppermute | solution.py:340
  37.7 1.0 %collective-permute-start.16 = (bf16[512,256]{1,0:T(8,128)(2,1)S(1)}, bf16[512,256]{1,0:T(8,128)(2,1)S(1)}, u32[]{:S(2)}, u32[]{:S(2)}) collective-permute-start(bf16[512,256]{1,0:T(8,128)(2,1)S(1)} %get-tuple-element.71.c0), channel_id=1, source_target_pairs={{0,2},{1,3},{2,0},{3,1},{4,6},{5,7},{6,4},{7,5},{8,10},{9,11},{10,... | collective-permute-start | bytes 786440 | tf_op jit(solution)/shard_map/ppermute | solution.py:28
  38.7 1.2 %collective-permute-start.11 = (bf16[256,256]{1,0:T(8,128)(2,1)S(1)}, bf16[256,256]{1,0:T(8,128)(2,1)S(1)}, u32[]{:S(2)}, u32[]{:S(2)}) collective-permute-start(bf16[256,256]{1,0:T(8,128)(2,1)S(1)} %get-tuple-element.85), channel_id=1, source_target_pairs={{0,1},{1,0},{2,3},{3,2},{4,5},{5,4},{6,7},{7,6},{8,9},{9,8},{10,11... | collective-permute-start | bytes 393224 | tf_op jit(solution)/shard_map/ppermute | solution.py:28
  41.4 1.4 %begin.1 = (f32[1024,512]{1,0:T(8,128)S(1)}, bf16[1024,512]{1,0:T(8,128)(2,1)S(1)}) custom-call(bf16[1024,256]{1,0:T(8,128)(2,1)S(1)} %get-tuple-element.52.c0, bf16[1024,256]{1,0:T(8,128)(2,1)S(1)} %collective-permute-done.7.c1, bf16[1024,256]{1,0:T(8,128)(2,1)S(1)} %collective-permute-done.6.c2, bf16[256,256]{1,0:T(8,128)(2,1)S(1)} %collective-permute-done.10.rest_0_, ...), custom_call_target="tpu_custom_call" | custom-call | flops 1000 | bytes 1000 | tf_op jit(solution)/shard_map/begin/pallas_call | solution.py:359
  42.8 2.8 %multiply_top.1 = (bf16[1024,1024]{1,0:T(8,128)(2,1)S(1)}, bf16[512,512]{1,0:T(8,128)(2,1)S(1)}, bf16[512,512]{1,0:T(8,128)(2,1)S(1)}) custom-call(bf16[4,128,128]{2,1,0:T(8,128)(2,1)S(1)} %pad_maximum_fusion.x0, bf16[4,128,128]{2,1,0:T(8,128)(2,1)S(1)} %collective-permute-done.9.x1, bf16[4,128,128]{2,1,0:T(8,128)(2,1)S(1)} %collective-permute-done.8.x2, ...), custom_call_target="tpu_custom_call" | custom-call | flops 1000 | bytes 1000 | tf_op jit(solution)/shard_map/multiply_top/pallas_call | solution.py:403
  45.7 0.9 %collective-permute-start.19 = (bf16[256,256]{1,0:T(8,128)(2,1)S(1)}, bf16[256,256]{1,0:T(8,128)(2,1)S(1)}, u32[]{:S(2)}, u32[]{:S(2)}) collective-permute-start(bf16[256,256]{1,0:T(8,128)(2,1)S(1)} %get-tuple-element.87), channel_id=1, source_target_pairs={{0,1},{1,0},{2,3},{3,2},{4,5},{5,4},{6,7},{7,6},{8,9},{9,8},{10,11... | collective-permute-start | bytes 393224 | tf_op jit(solution)/shard_map/ppermute | solution.py:28
  47.9 1.6 %multiply_bottom.1.bottom = bf16[512,1024]{1,0:T(8,128)(2,1)S(1)} custom-call(bf16[512,256]{1,0:T(8,128)(2,1)S(1)} %get-tuple-element.71.c0, bf16[512,256]{1,0:T(8,128)(2,1)S(1)} %collective-permute-done.17.c1, bf16[512,256]{1,0:T(8,128)(2,1)S(1)} %collective-permute-done.16.c2, bf16[256,256]{1,0:T(8,128)(2,1)S(1)} %collective-permute-done.18.k0, ...), custom_call_target="tpu_custom_call" | custom-call | flops 1000 | bytes 1000 | tf_op jit(solution)/shard_map/multiply_bottom/pallas_call | solution.py:431
  49.5 7.1 %update.1 = (bf16[1,1536,1536]{2,1,0:T(8,128)(2,1)}, bf16[1024,1536]{1,0:T(8,128)(2,1)S(1)}) custom-call(s32[1,2,16]{2,1,0:T(2,128)S(1)} %copy-done.4, bf16[1024,1024]{1,0:T(8,128)(2,1)S(1)} %get-tuple-element.72.top, bf16[512,1024]{1,0:T(8,128)(2,1)S(1)} %multiply_bottom.1.bottom, ...), custom_call_target="tpu_custom_call", output_to_operand_aliasing={{1}: (3, {})} | custom-call | flops 1000 | bytes 1000 | tf_op jit(solution)/shard_map/update/pallas_call | solution.py:479
  (45 shorter events, 5.5 us)
Async XLA Ops:
  0.0 9.6 %copy-start.2 = (bf16[1,512,512]{2,1,0:T(8,128)(2,1)S(1)}, bf16[1,512,512]{2,1,0:T(8,128)(2,1)}, u32[]{:S(2)}) copy-start(bf16[1,512,512]{2,1,0:T(8,128)(2,1)} %kept.5) | copy-start | bytes 1572868
  0.0 14.6 %collective-permute-start = (bf16[1,512,512]{2,1,0:T(8,128)(2,1)}, bf16[1,512,512]{2,1,0:T(8,128)(2,1)S(1)}, u32[]{:S(2)}, u32[]{:S(2)}) collective-permute-start(bf16[1,512,512]{2,1,0:T(8,128)(2,1)} %param.8), channel_id=1, source_target_pairs={{0,16},{16,0},{32,48},{48,32},{64,80},{80,64},{96,112},{112,96},{1... | collective-permute-start | bytes 1572872 | tf_op jit(solution)/shard_map/ppermute | solution.py:28
  6.7 14.1 %collective-permute-start.2 = (bf16[256,1024]{1,0:T(8,128)(2,1)}, bf16[256,1024]{1,0:T(8,128)(2,1)S(1)}, u32[]{:S(2)}, u32[]{:S(2)}) collective-permute-start(bf16[256,1024]{1,0:T(8,128)(2,1)} %early.1.u0), channel_id=1, source_target_pairs={{0,4},{4,8},{8,12},{12,0},{1,5},{5,9},{9,13},{13,1},{2,6},{6,10},{... | collective-permute-start | bytes 1572872 | tf_op jit(solution)/shard_map/ppermute | solution.py:23
  8.2 14.0 %collective-permute-start.1 = (bf16[256,1024]{1,0:T(8,128)(2,1)}, bf16[256,1024]{1,0:T(8,128)(2,1)S(1)}, u32[]{:S(2)}, u32[]{:S(2)}) collective-permute-start(bf16[256,1024]{1,0:T(8,128)(2,1)} %early.1.u0), channel_id=1, source_target_pairs={{0,12},{4,0},{8,4},{12,8},{1,13},{5,1},{9,5},{13,9},{2,14},{6,2},{... | collective-permute-start | bytes 1572872 | tf_op jit(solution)/shard_map/ppermute | solution.py:23
  15.6 15.4 %collective-permute-start.7 = (bf16[1024,256]{1,0:T(8,128)(2,1)S(1)}, bf16[1024,256]{1,0:T(8,128)(2,1)S(1)}, u32[]{:S(2)}, u32[]{:S(2)}) collective-permute-start(bf16[1024,256]{1,0:T(8,128)(2,1)S(1)} %get-tuple-element.52.c0), channel_id=1, source_target_pairs={{0,1},{1,0},{2,3},{3,2},{4,5},{5,4},{6,7},{7,6},{8,9},{9,8},{10,11... | collective-permute-start | bytes 1572872 | tf_op jit(solution)/shard_map/ppermute | solution.py:28
  17.8 13.5 %collective-permute-start.6 = (bf16[1024,256]{1,0:T(8,128)(2,1)S(1)}, bf16[1024,256]{1,0:T(8,128)(2,1)S(1)}, u32[]{:S(2)}, u32[]{:S(2)}) collective-permute-start(bf16[1024,256]{1,0:T(8,128)(2,1)S(1)} %get-tuple-element.52.c0), channel_id=1, source_target_pairs={{0,2},{1,3},{2,0},{3,1},{4,6},{5,7},{6,4},{7,5},{8,10},{9,11},{10,... | collective-permute-start | bytes 1572872 | tf_op jit(solution)/shard_map/ppermute | solution.py:28
  19.2 11.8 %collective-permute-start.4 = (bf16[256,640]{1,0:T(8,128)(2,1)S(1)}, bf16[256,640]{1,0:T(8,128)(2,1)S(1)}, u32[]{:S(2)}, u32[]{:S(2)}) collective-permute-start(bf16[256,640]{1,0:T(8,128)(2,1)S(1)} %get-tuple-element.50.a0), channel_id=1, source_target_pairs={{0,4},{4,8},{8,12},{12,0},{1,5},{5,9},{9,13},{13,1},{2,6},{6,10},{... | collective-permute-start | bytes 983048 | tf_op jit(solution)/shard_map/ppermute | solution.py:23
  20.8 10.2 %collective-permute-start.3 = (bf16[256,640]{1,0:T(8,128)(2,1)S(1)}, bf16[256,640]{1,0:T(8,128)(2,1)S(1)}, u32[]{:S(2)}, u32[]{:S(2)}) collective-permute-start(bf16[256,640]{1,0:T(8,128)(2,1)S(1)} %get-tuple-element.50.a0), channel_id=1, source_target_pairs={{0,12},{4,0},{8,4},{12,8},{1,13},{5,1},{9,5},{13,9},{2,14},{6,2},{... | collective-permute-start | bytes 983048 | tf_op jit(solution)/shard_map/ppermute | solution.py:23
  22.2 12.2 %copy-start.3 = (bf16[256,1024]{1,0:T(8,128)(2,1)S(1)}, bf16[256,1024]{1,0:T(8,128)(2,1)}, u32[]{:S(2)}) copy-start(bf16[256,1024]{1,0:T(8,128)(2,1)} %early.1.u0) | copy-start | bytes 1572868
  22.2 8.8 %collective-permute-start.5 = (bf16[128,128]{1,0:T(8,128)(2,1)S(1)}, bf16[128,128]{1,0:T(8,128)(2,1)S(1)}, u32[]{:S(2)}, u32[]{:S(2)}) collective-permute-start(bf16[128,128]{1,0:T(8,128)(2,1)S(1)} %get-tuple-element.49), channel_id=1, source_target_pairs={{0,8},{4,12},{8,0},{12,4},{1,9},{5,13},{9,1},{13,5},{2,10},{6,14},... | collective-permute-start | bytes 98312 | tf_op jit(solution)/shard_map/ppermute | solution.py:23
  24.4 17.1 %copy-start.1 = (bf16[1,2,512,512]{3,2,1,0:T(8,128)(2,1)S(1)}, bf16[1,2,512,512]{3,2,1,0:T(8,128)(2,1)}, u32[]{:S(2)}) copy-start(bf16[1,2,512,512]{3,2,1,0:T(8,128)(2,1)} %inverse.3) | copy-start | bytes 3145732
  31.3 6.0 %collective-permute-start.9 = (bf16[4,128,128]{2,1,0:T(8,128)(2,1)S(1)}, bf16[4,128,128]{2,1,0:T(8,128)(2,1)S(1)}, u32[]{:S(2)}, u32[]{:S(2)}) collective-permute-start(bf16[4,128,128]{2,1,0:T(8,128)(2,1)S(1)} %pad_maximum_fusion.x0), channel_id=1, source_target_pairs={{0,1},{1,0},{2,3},{3,2},{4,5},{5,4},{6,7},{7,6},{8,9},{9,8},{10,11... | collective-permute-start | bytes 393224 | tf_op jit(solution)/shard_map/ppermute | solution.py:28
  32.7 5.1 %collective-permute-start.8 = (bf16[4,128,128]{2,1,0:T(8,128)(2,1)S(1)}, bf16[4,128,128]{2,1,0:T(8,128)(2,1)S(1)}, u32[]{:S(2)}, u32[]{:S(2)}) collective-permute-start(bf16[4,128,128]{2,1,0:T(8,128)(2,1)S(1)} %pad_maximum_fusion.x0), channel_id=1, source_target_pairs={{0,2},{1,3},{2,0},{3,1},{4,6},{5,7},{6,4},{7,5},{8,10},{9,11},{10,... | collective-permute-start | bytes 393224 | tf_op jit(solution)/shard_map/ppermute | solution.py:28
  33.7 5.0 %collective-permute-start.13 = (bf16[256,256]{1,0:T(8,128)(2,1)S(1)}, bf16[256,256]{1,0:T(8,128)(2,1)S(1)}, u32[]{:S(2)}, u32[]{:S(2)}) collective-permute-start(bf16[256,256]{1,0:T(8,128)(2,1)S(1)} %get-tuple-element.83), channel_id=1, source_target_pairs={{0,1},{1,0},{2,3},{3,2},{4,5},{5,4},{6,7},{7,6},{8,9},{9,8},{10,11... | collective-permute-start | bytes 393224 | tf_op jit(solution)/shard_map/ppermute | solution.py:28
  34.2 5.7 %collective-permute-start.12 = (bf16[256,256]{1,0:T(8,128)(2,1)S(1)}, bf16[256,256]{1,0:T(8,128)(2,1)S(1)}, u32[]{:S(2)}, u32[]{:S(2)}) collective-permute-start(bf16[256,256]{1,0:T(8,128)(2,1)S(1)} %get-tuple-element.84), channel_id=1, source_target_pairs={{0,1},{1,0},{2,3},{3,2},{4,5},{5,4},{6,7},{7,6},{8,9},{9,8},{10,11... | collective-permute-start | bytes 393224 | tf_op jit(solution)/shard_map/ppermute | solution.py:28
  34.6 15.0 %collective-permute-start.20 = (bf16[256,1536]{1,0:T(8,128)(2,1)S(1)}, bf16[256,1536]{1,0:T(8,128)(2,1)S(1)}, u32[]{:S(2)}, u32[]{:S(2)}) collective-permute-start(bf16[256,1536]{1,0:T(8,128)(2,1)S(1)} %get-tuple-element.77), channel_id=1, source_target_pairs={{0,4},{1,13},{2,6},{3,15},{4,8},{5,1},{6,10},{7,3},{8,12},{9,5},{1... | collective-permute-start | bytes 2359304 | tf_op jit(solution)/shard_map/ppermute | solution.py:340
  37.4 8.2 %collective-permute-start.17 = (bf16[512,256]{1,0:T(8,128)(2,1)S(1)}, bf16[512,256]{1,0:T(8,128)(2,1)S(1)}, u32[]{:S(2)}, u32[]{:S(2)}) collective-permute-start(bf16[512,256]{1,0:T(8,128)(2,1)S(1)} %get-tuple-element.71.c0), channel_id=1, source_target_pairs={{0,1},{1,0},{2,3},{3,2},{4,5},{5,4},{6,7},{7,6},{8,9},{9,8},{10,11... | collective-permute-start | bytes 786440 | tf_op jit(solution)/shard_map/ppermute | solution.py:28
  37.7 7.9 %collective-permute-start.16 = (bf16[512,256]{1,0:T(8,128)(2,1)S(1)}, bf16[512,256]{1,0:T(8,128)(2,1)S(1)}, u32[]{:S(2)}, u32[]{:S(2)}) collective-permute-start(bf16[512,256]{1,0:T(8,128)(2,1)S(1)} %get-tuple-element.71.c0), channel_id=1, source_target_pairs={{0,2},{1,3},{2,0},{3,1},{4,6},{5,7},{6,4},{7,5},{8,10},{9,11},{10,... | collective-permute-start | bytes 786440 | tf_op jit(solution)/shard_map/ppermute | solution.py:28
  38.7 2.1 %collective-permute-start.11 = (bf16[256,256]{1,0:T(8,128)(2,1)S(1)}, bf16[256,256]{1,0:T(8,128)(2,1)S(1)}, u32[]{:S(2)}, u32[]{:S(2)}) collective-permute-start(bf16[256,256]{1,0:T(8,128)(2,1)S(1)} %get-tuple-element.85), channel_id=1, source_target_pairs={{0,1},{1,0},{2,3},{3,2},{4,5},{5,4},{6,7},{7,6},{8,9},{9,8},{10,11... | collective-permute-start | bytes 393224 | tf_op jit(solution)/shard_map/ppermute | solution.py:28
  39.9 1.3 %collective-permute-start.10 = (bf16[256,256]{1,0:T(8,128)(2,1)S(1)}, bf16[256,256]{1,0:T(8,128)(2,1)S(1)}, u32[]{:S(2)}, u32[]{:S(2)}) collective-permute-start(bf16[256,256]{1,0:T(8,128)(2,1)S(1)} %get-tuple-element.86), channel_id=1, source_target_pairs={{0,1},{1,0},{2,3},{3,2},{4,5},{5,4},{6,7},{7,6},{8,9},{9,8},{10,11... | collective-permute-start | bytes 393224 | tf_op jit(solution)/shard_map/ppermute | solution.py:28
  40.9 1.9 %collective-permute-start.15 = (bf16[2,128,128]{2,1,0:T(8,128)(2,1)S(1)}, bf16[2,128,128]{2,1,0:T(8,128)(2,1)S(1)}, u32[]{:S(2)}, u32[]{:S(2)}) collective-permute-start(bf16[2,128,128]{2,1,0:T(8,128)(2,1)S(1)} %get-tuple-element.89), channel_id=1, source_target_pairs={{0,1},{1,0},{2,3},{3,2},{4,5},{5,4},{6,7},{7,6},{8,9},{9,8},{10,11... | collective-permute-start | bytes 196616 | tf_op jit(solution)/shard_map/ppermute | solution.py:28
  41.3 1.6 %collective-permute-start.14 = (bf16[2,128,128]{2,1,0:T(8,128)(2,1)S(1)}, bf16[2,128,128]{2,1,0:T(8,128)(2,1)S(1)}, u32[]{:S(2)}, u32[]{:S(2)}) collective-permute-start(bf16[2,128,128]{2,1,0:T(8,128)(2,1)S(1)} %get-tuple-element.90), channel_id=1, source_target_pairs={{0,1},{1,0},{2,3},{3,2},{4,5},{5,4},{6,7},{7,6},{8,9},{9,8},{10,11... | collective-permute-start | bytes 196616 | tf_op jit(solution)/shard_map/ppermute | solution.py:28
  45.7 1.9 %collective-permute-start.19 = (bf16[256,256]{1,0:T(8,128)(2,1)S(1)}, bf16[256,256]{1,0:T(8,128)(2,1)S(1)}, u32[]{:S(2)}, u32[]{:S(2)}) collective-permute-start(bf16[256,256]{1,0:T(8,128)(2,1)S(1)} %get-tuple-element.87), channel_id=1, source_target_pairs={{0,1},{1,0},{2,3},{3,2},{4,5},{5,4},{6,7},{7,6},{8,9},{9,8},{10,11... | collective-permute-start | bytes 393224 | tf_op jit(solution)/shard_map/ppermute | solution.py:28
  46.6 1.3 %collective-permute-start.18 = (bf16[256,256]{1,0:T(8,128)(2,1)S(1)}, bf16[256,256]{1,0:T(8,128)(2,1)S(1)}, u32[]{:S(2)}, u32[]{:S(2)}) collective-permute-start(bf16[256,256]{1,0:T(8,128)(2,1)S(1)} %get-tuple-element.88), channel_id=1, source_target_pairs={{0,1},{1,0},{2,3},{3,2},{4,5},{5,4},{6,7},{7,6},{8,9},{9,8},{10,11... | collective-permute-start | bytes 393224 | tf_op jit(solution)/shard_map/ppermute | solution.py:28
  (3 other events, 28.8 us)

commit v4 on v3

--- a/solution.py
+++ b/solution.py
@@ -414,15 +414,16 @@
 def multiply_bottom(pieces, corners, x, k, inverse):
     span = pieces[0].shape[0]
 
-    def kernel(c0, c1, c2, k0, k1, x, k, inverse, mult, p1, i2):
+    def kernel(c0, c1, c2, *rest):
+        *corners, x, k, inverse, mult, p1, i2 = rest
         row, col = places()
         for q, c in enumerate((c0, c1, c2)):
             j = lax.bitwise_xor(col, q)
             p1[:, at(j)] = c[:, :BLK]
             i2[:, at(j)] = c[:, BLK:]
         j = lax.bitwise_xor(col, 3)
-        for n, corner in enumerate((k0, k1)):
-            rows = slice(n * PAIR, (n + 1) * PAIR)
+        for n, corner in enumerate(corners):
+            rows = slice(n * BLK, (n + 1) * BLK)
             p1[rows, at(j)] = corner[:, :BLK]
             i2[rows, at(j)] = corner[:, BLK:]
         m1 = dot(p1[...], inverse[0, 0])
@@ -431,7 +432,7 @@
     return pl.pallas_call(
         kernel,
         out_shape=out(span, 2 * P_SIZE),
-        in_specs=[VMEM] * 8,
+        in_specs=[VMEM] * (6 + len(corners)),
         out_specs=VMEM,
         scratch_shapes=[pltpu.VMEM((span, P_SIZE), BF16)] * 2,
         compiler_params=params(8),
@@ -507,22 +508,20 @@
     an, ap = shift(a, "row", -1), shift(a, "row", 1)
     cross2 = shift(cross, "row", 2)
     base = add_child(child_map, base, arrived)
-    un, up, an, ap, cross2, base, tfar, tnear, bottom = hold(
-        (un, up, an, ap, cross2, base, tfar, tnear, bottom)
-    )
+    bfar, bnear = flip(bottom, "col", 2), flip(bottom, "col", 1)
+    un, up, an, ap, cross2, base, tfar, tnear = hold((un, up, an, ap, cross2, base, tfar, tnear))
     panel, onward = stage((u, un, up), (a, an, ap))
     far = hand_on(onward)
     crosses = jnp.stack([cross, an[:BLK, kid:], cross2, ap[:BLK, kid:]])
     xfar, xnear = flip(crosses, "col", 2), flip(crosses, "col", 1)
-    bfar, bnear = flip(bottom, "col", 2), flip(bottom, "col", 1)
     tcorners = [flip(tfar[n : n + PAIR], "col", 1) for n in range(0, top.shape[0], PAIR)]
-    xfar, xnear, panel = hold((xfar, xnear, panel))
+    xfar, xnear, panel, tcorners, bfar, bnear = hold((xfar, xnear, panel, tcorners, bfar, bnear))
     xcorners = [flip(xfar[n : n + 2], "col", 1) for n in (0, 2)]
     first, second = begin((top, tnear, tfar), tcorners, pivot_inverse)
     first, second, xcorners = hold((first, second, xcorners))
     upper, x, k = multiply_top((crosses, xnear, xfar, *xcorners), first, second, pivot_inverse)
-    upper, bfar, bnear = hold((upper, bfar, bnear))
-    bcorners = [flip(bfar[n : n + PAIR], "col", 1) for n in range(0, bottom.shape[0], PAIR)]
+    bcorners = [flip(bfar[n : n + BLK], "col", 1) for n in range(0, bottom.shape[0], BLK)]
+    upper, bcorners = hold((upper, bcorners))
     lower = multiply_bottom((bottom, bnear, bfar), bcorners, x, k, pivot_inverse)
     lower, far = hold((lower, far))
     return update(child_map, (upper, lower), panel, far, base)

time: 56.9 us -> 60.2 us (1.058)
  waiting for transfers between devices: 11.3 us -> 14.8 us
    ppermute x15 -> x17, waiting for transfers between devices: 4.38 us -> 7.99 us  [flip(): return lax.ppermute(x, axis, [(i, i ^ bit) for i in range(n)])]
    ppermute x1, starting transfers between devices: 2.81 us -> 2.11 us  [hand_on(): return lax.ppermute(x, ('row', 'col'), route)]
    ppermute x15 -> x17, starting transfers between devices: 14.3 us -> 14.7 us  [flip(): return lax.ppermute(x, axis, [(i, i ^ bit) for i in range(n)])]
  transfers between devices with their start and end apart: 21 -> 23, of which waited for: 8 -> 7; matrix products, arithmetic and copies ran while one was open for 0% -> 0% of each run, Pallas kernels for 24% -> 23%
where the time goes in v4:
time: 60.2 us; the launch traced here: 60.1 us
  starting transfers between devices  23.7 us (39%)
  Pallas kernels  21.1 us (35%)
  waiting for transfers between devices  14.8 us (25%)
    ppermute x17, starting transfers between devices, flip(): return lax.ppermute(x, axis, [(i, i ^ bit) for i in range(n)])  14.7 us
    ppermute x17, waiting for transfers between devices, flip(): return lax.ppermute(x, axis, [(i, i ^ bit) for i in range(n)])  7.99 us
    pallas_call x1, Pallas kernels, update(): pl.pallas_call(kernel, out_shape=(out(1, span, span), out(*panel.shape)),...  7.07 us
    ppermute x5, starting transfers between devices, shift(): return lax.ppermute(x, axis, [(i, (i + step) % n) for i in range(n)])  6.92 us
    ppermute x5, waiting for transfers between devices, shift(): return lax.ppermute(x, axis, [(i, (i + step) % n) for i in range(n)])  6.81 us
    pallas_call x1, Pallas kernels, early(): pl.pallas_call(early_kernel, out_shape=out(PAIR, span - kept.shape[1]), i...  3.14 us
    pallas_call x1, Pallas kernels, multiply_top(): pl.pallas_call(kernel, out_shape=(out(span, 2 * P_SIZE), out(P_SIZE, P_SI...  2.77 us
    ppermute x1, starting transfers between devices, hand_on(): return lax.ppermute(x, ('row', 'col'), route)  2.11 us
  transfers between devices with their start and end apart: 23, of which 7 were waited for; matrix products, arithmetic and copies ran while one was open for 0% of the time, Pallas kernels for 23%

profile of v4, /device:TPU:1, one launch (start us, length us, event | category | flops | bytes accessed | tf_op | source)
XLA Modules:
  0.0 60.1 jit_solution(10971362130391028900)
XLA Ops:
  0.0 3.7 %collective-permute-start = (bf16[1,512,512]{2,1,0:T(8,128)(2,1)}, bf16[1,512,512]{2,1,0:T(8,128)(2,1)S(1)}, u32[]{:S(2)}, u32[]{:S(2)}) collective-permute-start(bf16[1,512,512]{2,1,0:T(8,128)(2,1)} %param.8), channel_id=1, source_target_pairs={{0,16},{16,0},{32,48},{48,32},{64,80},{80,64},{96,112},{112,96},{1... | collective-permute-start | bytes 1572872 | tf_op jit(solution)/shard_map/ppermute | solution.py:28
  3.7 3.1 %early.1.u0 = bf16[256,1024]{1,0:T(8,128)(2,1)} custom-call(s32[1,2,16]{2,1,0:T(2,128)} %map_s.7, s32[1,2,4]{2,1,0:T(2,128)} %piv_s.1, bf16[1,1536,1536]{2,1,0:T(8,128)(2,1)} %front.5, bf16[1,512,512]{2,1,0:T(8,128)(2,1)} %kept.5), custom_call_target="tpu_custom_call" | custom-call | flops 1000 | bytes 1000 | tf_op jit(solution)/shard_map/early/pallas_call | solution.py:133
  6.8 1.2 %collective-permute-start.2 = (bf16[256,1024]{1,0:T(8,128)(2,1)}, bf16[256,1024]{1,0:T(8,128)(2,1)S(1)}, u32[]{:S(2)}, u32[]{:S(2)}) collective-permute-start(bf16[256,1024]{1,0:T(8,128)(2,1)} %early.1.u0), channel_id=1, source_target_pairs={{0,4},{4,8},{8,12},{12,0},{1,5},{5,9},{9,13},{13,1},{2,6},{6,10},{... | collective-permute-start | bytes 1572872 | tf_op jit(solution)/shard_map/ppermute | solution.py:23
  8.1 1.5 %collective-permute-start.1 = (bf16[256,1024]{1,0:T(8,128)(2,1)}, bf16[256,1024]{1,0:T(8,128)(2,1)S(1)}, u32[]{:S(2)}, u32[]{:S(2)}) collective-permute-start(bf16[256,1024]{1,0:T(8,128)(2,1)} %early.1.u0), channel_id=1, source_target_pairs={{0,12},{4,0},{8,4},{12,8},{1,13},{5,1},{9,5},{13,9},{2,14},{6,2},{... | collective-permute-start | bytes 1572872 | tf_op jit(solution)/shard_map/ppermute | solution.py:23
  9.6 1.6 %prepare.1 = (f32[2,128,512]{2,1,0:T(8,128)S(1)}, f32[2,1536,128]{2,1,0:T(8,128)S(1)}) custom-call(s32[1,2,16]{2,1,0:T(2,128)S(1)} %copy-done.4, s32[1,2,4]{2,1,0:T(2,128)S(1)} %copy-done.5, bf16[1,1536,1536]{2,1,0:T(8,128)(2,1)S(1)} %copy-done, bf16[1,512,512]{2,1,0:T(8,128)(2,1)S(1)} %copy-done.2), custom_call_target="tpu_custom_call" | custom-call | flops 1000 | bytes 1000 | tf_op jit(solution)/shard_map/prepare/pallas_call | solution.py:180
  11.2 1.6 %base.1._ = f32[1536,1536]{1,0:T(8,128)S(1)} custom-call(s32[1,2,16]{2,1,0:T(2,128)S(1)} %copy-done.4, bf16[1,1536,1536]{2,1,0:T(8,128)(2,1)S(1)} %copy-done, bf16[1,512,512]{2,1,0:T(8,128)(2,1)S(1)} %copy-done.2), custom_call_target="tpu_custom_call" | custom-call | flops 1000 | bytes 1000 | tf_op jit(solution)/shard_map/base/pallas_call | solution.py:273
  12.8 1.8 %collective-permute-done.arrived = bf16[1,512,512]{2,1,0:T(8,128)(2,1)S(1)} collective-permute-done((bf16[1,512,512]{2,1,0:T(8,128)(2,1)}, bf16[1,512,512]{2,1,0:T(8,128)(2,1)S(1)}, u32[]{:S(2)}, u32[]{:S(2)}) %collective-permute-start) | collective-permute-done | bytes 524320 | tf_op jit(solution)/shard_map/ppermute | solution.py:28
  15.6 2.3 %collective-permute-start.7 = (bf16[1024,256]{1,0:T(8,128)(2,1)S(1)}, bf16[1024,256]{1,0:T(8,128)(2,1)S(1)}, u32[]{:S(2)}, u32[]{:S(2)}) collective-permute-start(bf16[1024,256]{1,0:T(8,128)(2,1)S(1)} %get-tuple-element.59.c0), channel_id=1, source_target_pairs={{0,1},{1,0},{2,3},{3,2},{4,5},{5,4},{6,7},{7,6},{8,9},{9,8},{10,11... | collective-permute-start | bytes 1572872 | tf_op jit(solution)/shard_map/ppermute | solution.py:28
  17.8 1.5 %collective-permute-start.6 = (bf16[1024,256]{1,0:T(8,128)(2,1)S(1)}, bf16[1024,256]{1,0:T(8,128)(2,1)S(1)}, u32[]{:S(2)}, u32[]{:S(2)}) collective-permute-start(bf16[1024,256]{1,0:T(8,128)(2,1)S(1)} %get-tuple-element.59.c0), channel_id=1, source_target_pairs={{0,2},{1,3},{2,0},{3,1},{4,6},{5,7},{6,4},{7,5},{8,10},{9,11},{10,... | collective-permute-start | bytes 1572872 | tf_op jit(solution)/shard_map/ppermute | solution.py:28
  19.3 1.3 %collective-permute-start.4 = (bf16[256,640]{1,0:T(8,128)(2,1)S(1)}, bf16[256,640]{1,0:T(8,128)(2,1)S(1)}, u32[]{:S(2)}, u32[]{:S(2)}) collective-permute-start(bf16[256,640]{1,0:T(8,128)(2,1)S(1)} %get-tuple-element.57.a0), channel_id=1, source_target_pairs={{0,4},{4,8},{8,12},{12,0},{1,5},{5,9},{9,13},{13,1},{2,6},{6,10},{... | collective-permute-start | bytes 983048 | tf_op jit(solution)/shard_map/ppermute | solution.py:23
  20.8 1.4 %collective-permute-start.3 = (bf16[256,640]{1,0:T(8,128)(2,1)S(1)}, bf16[256,640]{1,0:T(8,128)(2,1)S(1)}, u32[]{:S(2)}, u32[]{:S(2)}) collective-permute-start(bf16[256,640]{1,0:T(8,128)(2,1)S(1)} %get-tuple-element.57.a0), channel_id=1, source_target_pairs={{0,12},{4,0},{8,4},{12,8},{1,13},{5,1},{9,5},{13,9},{2,14},{6,2},{... | collective-permute-start | bytes 983048 | tf_op jit(solution)/shard_map/ppermute | solution.py:23
  22.2 1.5 %collective-permute-start.5 = (bf16[128,128]{1,0:T(8,128)(2,1)S(1)}, bf16[128,128]{1,0:T(8,128)(2,1)S(1)}, u32[]{:S(2)}, u32[]{:S(2)}) collective-permute-start(bf16[128,128]{1,0:T(8,128)(2,1)S(1)} %get-tuple-element.56), channel_id=1, source_target_pairs={{0,8},{4,12},{8,0},{12,4},{1,9},{5,13},{9,1},{13,5},{2,10},{6,14},... | collective-permute-start | bytes 98312 | tf_op jit(solution)/shard_map/ppermute | solution.py:23
  24.5 6.6 %collective-permute-done.5 = bf16[128,128]{1,0:T(8,128)(2,1)S(1)} collective-permute-done((bf16[128,128]{1,0:T(8,128)(2,1)S(1)}, bf16[128,128]{1,0:T(8,128)(2,1)S(1)}, u32[]{:S(2)}, u32[]{:S(2)}) %collective-permute-start.5) | collective-permute-done | bytes 32800 | tf_op jit(solution)/shard_map/ppermute | solution.py:23
  31.0 1.5 %collective-permute-start.15 = (bf16[512,256]{1,0:T(8,128)(2,1)S(1)}, bf16[512,256]{1,0:T(8,128)(2,1)S(1)}, u32[]{:S(2)}, u32[]{:S(2)}) collective-permute-start(bf16[512,256]{1,0:T(8,128)(2,1)S(1)} %get-tuple-element.67.c0), channel_id=1, source_target_pairs={{0,1},{1,0},{2,3},{3,2},{4,5},{5,4},{6,7},{7,6},{8,9},{9,8},{10,11... | collective-permute-start | bytes 786440 | tf_op jit(solution)/shard_map/ppermute | solution.py:28
  33.2 1.2 %collective-permute-start.8 = (bf16[4,128,128]{2,1,0:T(8,128)(2,1)S(1)}, bf16[4,128,128]{2,1,0:T(8,128)(2,1)S(1)}, u32[]{:S(2)}, u32[]{:S(2)}) collective-permute-start(bf16[4,128,128]{2,1,0:T(8,128)(2,1)S(1)} %pad_maximum_fusion.x0), channel_id=1, source_target_pairs={{0,2},{1,3},{2,0},{3,1},{4,6},{5,7},{6,4},{7,5},{8,10},{9,11},{10,... | collective-permute-start | bytes 393224 | tf_op jit(solution)/shard_map/ppermute | solution.py:28
  34.6 2.1 %collective-permute-start.22 = (bf16[256,1536]{1,0:T(8,128)(2,1)S(1)}, bf16[256,1536]{1,0:T(8,128)(2,1)S(1)}, u32[]{:S(2)}, u32[]{:S(2)}) collective-permute-start(bf16[256,1536]{1,0:T(8,128)(2,1)S(1)} %get-tuple-element.91), channel_id=1, source_target_pairs={{0,4},{1,13},{2,6},{3,15},{4,8},{5,1},{6,10},{7,3},{8,12},{9,5},{1... | collective-permute-start | bytes 2359304 | tf_op jit(solution)/shard_map/ppermute | solution.py:340
  37.1 3.4 %collective-permute-done.14.c2 = bf16[512,256]{1,0:T(8,128)(2,1)S(1)} collective-permute-done((bf16[512,256]{1,0:T(8,128)(2,1)S(1)}, bf16[512,256]{1,0:T(8,128)(2,1)S(1)}, u32[]{:S(2)}, u32[]{:S(2)}) %collective-permute-start.14) | collective-permute-done | bytes 262176 | tf_op jit(solution)/shard_map/ppermute | solution.py:28
  40.5 1.2 %collective-permute-start.12 = (bf16[256,256]{1,0:T(8,128)(2,1)S(1)}, bf16[256,256]{1,0:T(8,128)(2,1)S(1)}, u32[]{:S(2)}, u32[]{:S(2)}) collective-permute-start(bf16[256,256]{1,0:T(8,128)(2,1)S(1)} %get-tuple-element.98), channel_id=1, source_target_pairs={{0,1},{1,0},{2,3},{3,2},{4,5},{5,4},{6,7},{7,6},{8,9},{9,8},{10,11... | collective-permute-start | bytes 393224 | tf_op jit(solution)/shard_map/ppermute | solution.py:28
  41.6 1.6 %collective-permute-done.8.x2 = bf16[4,128,128]{2,1,0:T(8,128)(2,1)S(1)} collective-permute-done((bf16[4,128,128]{2,1,0:T(8,128)(2,1)S(1)}, bf16[4,128,128]{2,1,0:T(8,128)(2,1)S(1)}, u32[]{:S(2)}, u32[]{:S(2)}) %collective-permute-start.8) | collective-permute-done | bytes 131104 | tf_op jit(solution)/shard_map/ppermute | solution.py:28
  44.1 1.0 %collective-permute-done.10.rest_0_ = bf16[256,256]{1,0:T(8,128)(2,1)S(1)} collective-permute-done((bf16[256,256]{1,0:T(8,128)(2,1)S(1)}, bf16[256,256]{1,0:T(8,128)(2,1)S(1)}, u32[]{:S(2)}, u32[]{:S(2)}) %collective-permute-start.10) | collective-permute-done | bytes 131104 | tf_op jit(solution)/shard_map/ppermute | solution.py:28
  47.0 1.4 %begin.1 = (f32[1024,512]{1,0:T(8,128)S(1)}, bf16[1024,512]{1,0:T(8,128)(2,1)S(1)}) custom-call(bf16[1024,256]{1,0:T(8,128)(2,1)S(1)} %get-tuple-element.59.c0, bf16[1024,256]{1,0:T(8,128)(2,1)S(1)} %collective-permute-done.7.c1, bf16[1024,256]{1,0:T(8,128)(2,1)S(1)} %collective-permute-done.6.c2, bf16[256,256]{1,0:T(8,128)(2,1)S(1)} %collective-permute-done.10.rest_0_, ...), custom_call_target="tpu_custom_call" | custom-call | flops 1000 | bytes 1000 | tf_op jit(solution)/shard_map/begin/pallas_call | solution.py:359
  48.4 2.8 %multiply_top.1 = (bf16[1024,1024]{1,0:T(8,128)(2,1)S(1)}, bf16[512,512]{1,0:T(8,128)(2,1)S(1)}, bf16[512,512]{1,0:T(8,128)(2,1)S(1)}) custom-call(bf16[4,128,128]{2,1,0:T(8,128)(2,1)S(1)} %pad_maximum_fusion.x0, bf16[4,128,128]{2,1,0:T(8,128)(2,1)S(1)} %collective-permute-done.9.x1, bf16[4,128,128]{2,1,0:T(8,128)(2,1)S(1)} %collective-permute-done.8.x2, ...), custom_call_target="tpu_custom_call" | custom-call | flops 1000 | bytes 1000 | tf_op jit(solution)/shard_map/multiply_top/pallas_call | solution.py:403
  51.2 1.6 %multiply_bottom.1.bottom = bf16[512,1024]{1,0:T(8,128)(2,1)S(1)} custom-call(bf16[512,256]{1,0:T(8,128)(2,1)S(1)} %get-tuple-element.67.c0, bf16[512,256]{1,0:T(8,128)(2,1)S(1)} %collective-permute-done.15.c1, bf16[512,256]{1,0:T(8,128)(2,1)S(1)} %collective-permute-done.14.c2, bf16[128,256]{1,0:T(8,128)(2,1)S(1)} %collective-permute-done.18.rest_0_, ...), custom_call_target="tpu_custom_call" | custom-call | flops 1000 | bytes 1000 | tf_op jit(solution)/shard_map/multiply_bottom/pallas_call | solution.py:432
  52.9 7.1 %update.1 = (bf16[1,1536,1536]{2,1,0:T(8,128)(2,1)}, bf16[1024,1536]{1,0:T(8,128)(2,1)S(1)}) custom-call(s32[1,2,16]{2,1,0:T(2,128)S(1)} %copy-done.4, bf16[1024,1024]{1,0:T(8,128)(2,1)S(1)} %get-tuple-element.83.top, bf16[512,1024]{1,0:T(8,128)(2,1)S(1)} %multiply_bottom.1.bottom, ...), custom_call_target="tpu_custom_call", output_to_operand_aliasing={{1}: (3, {})} | custom-call | flops 1000 | bytes 1000 | tf_op jit(solution)/shard_map/update/pallas_call | solution.py:480
  (49 shorter events, 6.0 us)
Async XLA Ops:
  0.0 14.6 %collective-permute-start = (bf16[1,512,512]{2,1,0:T(8,128)(2,1)}, bf16[1,512,512]{2,1,0:T(8,128)(2,1)S(1)}, u32[]{:S(2)}, u32[]{:S(2)}) collective-permute-start(bf16[1,512,512]{2,1,0:T(8,128)(2,1)} %param.8), channel_id=1, source_target_pairs={{0,16},{16,0},{32,48},{48,32},{64,80},{80,64},{96,112},{112,96},{1... | collective-permute-start | bytes 1572872 | tf_op jit(solution)/shard_map/ppermute | solution.py:28
  6.8 14.0 %collective-permute-start.2 = (bf16[256,1024]{1,0:T(8,128)(2,1)}, bf16[256,1024]{1,0:T(8,128)(2,1)S(1)}, u32[]{:S(2)}, u32[]{:S(2)}) collective-permute-start(bf16[256,1024]{1,0:T(8,128)(2,1)} %early.1.u0), channel_id=1, source_target_pairs={{0,4},{4,8},{8,12},{12,0},{1,5},{5,9},{9,13},{13,1},{2,6},{6,10},{... | collective-permute-start | bytes 1572872 | tf_op jit(solution)/shard_map/ppermute | solution.py:23
  8.1 14.1 %collective-permute-start.1 = (bf16[256,1024]{1,0:T(8,128)(2,1)}, bf16[256,1024]{1,0:T(8,128)(2,1)S(1)}, u32[]{:S(2)}, u32[]{:S(2)}) collective-permute-start(bf16[256,1024]{1,0:T(8,128)(2,1)} %early.1.u0), channel_id=1, source_target_pairs={{0,12},{4,0},{8,4},{12,8},{1,13},{5,1},{9,5},{13,9},{2,14},{6,2},{... | collective-permute-start | bytes 1572872 | tf_op jit(solution)/shard_map/ppermute | solution.py:23
  15.6 17.2 %collective-permute-start.7 = (bf16[1024,256]{1,0:T(8,128)(2,1)S(1)}, bf16[1024,256]{1,0:T(8,128)(2,1)S(1)}, u32[]{:S(2)}, u32[]{:S(2)}) collective-permute-start(bf16[1024,256]{1,0:T(8,128)(2,1)S(1)} %get-tuple-element.59.c0), channel_id=1, source_target_pairs={{0,1},{1,0},{2,3},{3,2},{4,5},{5,4},{6,7},{7,6},{8,9},{9,8},{10,11... | collective-permute-start | bytes 1572872 | tf_op jit(solution)/shard_map/ppermute | solution.py:28
  17.8 15.0 %collective-permute-start.6 = (bf16[1024,256]{1,0:T(8,128)(2,1)S(1)}, bf16[1024,256]{1,0:T(8,128)(2,1)S(1)}, u32[]{:S(2)}, u32[]{:S(2)}) collective-permute-start(bf16[1024,256]{1,0:T(8,128)(2,1)S(1)} %get-tuple-element.59.c0), channel_id=1, source_target_pairs={{0,2},{1,3},{2,0},{3,1},{4,6},{5,7},{6,4},{7,5},{8,10},{9,11},{10,... | collective-permute-start | bytes 1572872 | tf_op jit(solution)/shard_map/ppermute | solution.py:28
  19.3 13.3 %collective-permute-start.4 = (bf16[256,640]{1,0:T(8,128)(2,1)S(1)}, bf16[256,640]{1,0:T(8,128)(2,1)S(1)}, u32[]{:S(2)}, u32[]{:S(2)}) collective-permute-start(bf16[256,640]{1,0:T(8,128)(2,1)S(1)} %get-tuple-element.57.a0), channel_id=1, source_target_pairs={{0,4},{4,8},{8,12},{12,0},{1,5},{5,9},{9,13},{13,1},{2,6},{6,10},{... | collective-permute-start | bytes 983048 | tf_op jit(solution)/shard_map/ppermute | solution.py:23
  20.8 12.0 %collective-permute-start.3 = (bf16[256,640]{1,0:T(8,128)(2,1)S(1)}, bf16[256,640]{1,0:T(8,128)(2,1)S(1)}, u32[]{:S(2)}, u32[]{:S(2)}) collective-permute-start(bf16[256,640]{1,0:T(8,128)(2,1)S(1)} %get-tuple-element.57.a0), channel_id=1, source_target_pairs={{0,12},{4,0},{8,4},{12,8},{1,13},{5,1},{9,5},{13,9},{2,14},{6,2},{... | collective-permute-start | bytes 983048 | tf_op jit(solution)/shard_map/ppermute | solution.py:23
  22.2 8.8 %collective-permute-start.5 = (bf16[128,128]{1,0:T(8,128)(2,1)S(1)}, bf16[128,128]{1,0:T(8,128)(2,1)S(1)}, u32[]{:S(2)}, u32[]{:S(2)}) collective-permute-start(bf16[128,128]{1,0:T(8,128)(2,1)S(1)} %get-tuple-element.56), channel_id=1, source_target_pairs={{0,8},{4,12},{8,0},{12,4},{1,9},{5,13},{9,1},{13,5},{2,10},{6,14},... | collective-permute-start | bytes 98312 | tf_op jit(solution)/shard_map/ppermute | solution.py:23
  24.5 22.6 %copy-start.1 = (bf16[1,2,512,512]{3,2,1,0:T(8,128)(2,1)S(1)}, bf16[1,2,512,512]{3,2,1,0:T(8,128)(2,1)}, u32[]{:S(2)}) copy-start(bf16[1,2,512,512]{3,2,1,0:T(8,128)(2,1)} %rest_6_.1) | copy-start | bytes 3145732
  31.0 5.7 %collective-permute-start.15 = (bf16[512,256]{1,0:T(8,128)(2,1)S(1)}, bf16[512,256]{1,0:T(8,128)(2,1)S(1)}, u32[]{:S(2)}, u32[]{:S(2)}) collective-permute-start(bf16[512,256]{1,0:T(8,128)(2,1)S(1)} %get-tuple-element.67.c0), channel_id=1, source_target_pairs={{0,1},{1,0},{2,3},{3,2},{4,5},{5,4},{6,7},{7,6},{8,9},{9,8},{10,11... | collective-permute-start | bytes 786440 | tf_op jit(solution)/shard_map/ppermute | solution.py:28
  32.5 7.9 %collective-permute-start.14 = (bf16[512,256]{1,0:T(8,128)(2,1)S(1)}, bf16[512,256]{1,0:T(8,128)(2,1)S(1)}, u32[]{:S(2)}, u32[]{:S(2)}) collective-permute-start(bf16[512,256]{1,0:T(8,128)(2,1)S(1)} %get-tuple-element.67.c0), channel_id=1, source_target_pairs={{0,2},{1,3},{2,0},{3,1},{4,6},{5,7},{6,4},{7,5},{8,10},{9,11},{10,... | collective-permute-start | bytes 786440 | tf_op jit(solution)/shard_map/ppermute | solution.py:28
  32.8 8.8 %collective-permute-start.9 = (bf16[4,128,128]{2,1,0:T(8,128)(2,1)S(1)}, bf16[4,128,128]{2,1,0:T(8,128)(2,1)S(1)}, u32[]{:S(2)}, u32[]{:S(2)}) collective-permute-start(bf16[4,128,128]{2,1,0:T(8,128)(2,1)S(1)} %pad_maximum_fusion.x0), channel_id=1, source_target_pairs={{0,1},{1,0},{2,3},{3,2},{4,5},{5,4},{6,7},{7,6},{8,9},{9,8},{10,11... | collective-permute-start | bytes 393224 | tf_op jit(solution)/shard_map/ppermute | solution.py:28
  33.2 10.1 %collective-permute-start.8 = (bf16[4,128,128]{2,1,0:T(8,128)(2,1)S(1)}, bf16[4,128,128]{2,1,0:T(8,128)(2,1)S(1)}, u32[]{:S(2)}, u32[]{:S(2)}) collective-permute-start(bf16[4,128,128]{2,1,0:T(8,128)(2,1)S(1)} %pad_maximum_fusion.x0), channel_id=1, source_target_pairs={{0,2},{1,3},{2,0},{3,1},{4,6},{5,7},{6,4},{7,5},{8,10},{9,11},{10,... | collective-permute-start | bytes 393224 | tf_op jit(solution)/shard_map/ppermute | solution.py:28
  34.6 18.2 %collective-permute-start.22 = (bf16[256,1536]{1,0:T(8,128)(2,1)S(1)}, bf16[256,1536]{1,0:T(8,128)(2,1)S(1)}, u32[]{:S(2)}, u32[]{:S(2)}) collective-permute-start(bf16[256,1536]{1,0:T(8,128)(2,1)S(1)} %get-tuple-element.91), channel_id=1, source_target_pairs={{0,4},{1,13},{2,6},{3,15},{4,8},{5,1},{6,10},{7,3},{8,12},{9,5},{1... | collective-permute-start | bytes 2359304 | tf_op jit(solution)/shard_map/ppermute | solution.py:340
  36.8 7.3 %collective-permute-start.13 = (bf16[256,256]{1,0:T(8,128)(2,1)S(1)}, bf16[256,256]{1,0:T(8,128)(2,1)S(1)}, u32[]{:S(2)}, u32[]{:S(2)}) collective-permute-start(bf16[256,256]{1,0:T(8,128)(2,1)S(1)} %get-tuple-element.97), channel_id=1, source_target_pairs={{0,1},{1,0},{2,3},{3,2},{4,5},{5,4},{6,7},{7,6},{8,9},{9,8},{10,11... | collective-permute-start | bytes 393224 | tf_op jit(solution)/shard_map/ppermute | solution.py:28
  40.5 3.6 %collective-permute-start.12 = (bf16[256,256]{1,0:T(8,128)(2,1)S(1)}, bf16[256,256]{1,0:T(8,128)(2,1)S(1)}, u32[]{:S(2)}, u32[]{:S(2)}) collective-permute-start(bf16[256,256]{1,0:T(8,128)(2,1)S(1)} %get-tuple-element.98), channel_id=1, source_target_pairs={{0,1},{1,0},{2,3},{3,2},{4,5},{5,4},{6,7},{7,6},{8,9},{9,8},{10,11... | collective-permute-start | bytes 393224 | tf_op jit(solution)/shard_map/ppermute | solution.py:28
  41.6 2.4 %collective-permute-start.11 = (bf16[256,256]{1,0:T(8,128)(2,1)S(1)}, bf16[256,256]{1,0:T(8,128)(2,1)S(1)}, u32[]{:S(2)}, u32[]{:S(2)}) collective-permute-start(bf16[256,256]{1,0:T(8,128)(2,1)S(1)} %get-tuple-element.99), channel_id=1, source_target_pairs={{0,1},{1,0},{2,3},{3,2},{4,5},{5,4},{6,7},{7,6},{8,9},{9,8},{10,11... | collective-permute-start | bytes 393224 | tf_op jit(solution)/shard_map/ppermute | solution.py:28
  43.3 1.8 %collective-permute-start.10 = (bf16[256,256]{1,0:T(8,128)(2,1)S(1)}, bf16[256,256]{1,0:T(8,128)(2,1)S(1)}, u32[]{:S(2)}, u32[]{:S(2)}) collective-permute-start(bf16[256,256]{1,0:T(8,128)(2,1)S(1)} %get-tuple-element.100), channel_id=1, source_target_pairs={{0,1},{1,0},{2,3},{3,2},{4,5},{5,4},{6,7},{7,6},{8,9},{9,8},{10,11... | collective-permute-start | bytes 393224 | tf_op jit(solution)/shard_map/ppermute | solution.py:28
  45.1 1.4 %collective-permute-start.17 = (bf16[2,128,128]{2,1,0:T(8,128)(2,1)S(1)}, bf16[2,128,128]{2,1,0:T(8,128)(2,1)S(1)}, u32[]{:S(2)}, u32[]{:S(2)}) collective-permute-start(bf16[2,128,128]{2,1,0:T(8,128)(2,1)S(1)} %get-tuple-element.105), channel_id=1, source_target_pairs={{0,1},{1,0},{2,3},{3,2},{4,5},{5,4},{6,7},{7,6},{8,9},{9,8},{10,11... | collective-permute-start | bytes 196616 | tf_op jit(solution)/shard_map/ppermute | solution.py:28
  45.5 1.3 %collective-permute-start.16 = (bf16[2,128,128]{2,1,0:T(8,128)(2,1)S(1)}, bf16[2,128,128]{2,1,0:T(8,128)(2,1)S(1)}, u32[]{:S(2)}, u32[]{:S(2)}) collective-permute-start(bf16[2,128,128]{2,1,0:T(8,128)(2,1)S(1)} %get-tuple-element.106), channel_id=1, source_target_pairs={{0,1},{1,0},{2,3},{3,2},{4,5},{5,4},{6,7},{7,6},{8,9},{9,8},{10,11... | collective-permute-start | bytes 196616 | tf_op jit(solution)/shard_map/ppermute | solution.py:28
  45.7 5.5 %collective-permute-start.21 = (bf16[128,256]{1,0:T(8,128)(2,1)S(1)}, bf16[128,256]{1,0:T(8,128)(2,1)S(1)}, u32[]{:S(2)}, u32[]{:S(2)}) collective-permute-start(bf16[128,256]{1,0:T(8,128)(2,1)S(1)} %get-tuple-element.101), channel_id=1, source_target_pairs={{0,1},{1,0},{2,3},{3,2},{4,5},{5,4},{6,7},{7,6},{8,9},{9,8},{10,11... | collective-permute-start | bytes 196616 | tf_op jit(solution)/shard_map/ppermute | solution.py:28
  46.1 5.1 %collective-permute-start.20 = (bf16[128,256]{1,0:T(8,128)(2,1)S(1)}, bf16[128,256]{1,0:T(8,128)(2,1)S(1)}, u32[]{:S(2)}, u32[]{:S(2)}) collective-permute-start(bf16[128,256]{1,0:T(8,128)(2,1)S(1)} %get-tuple-element.102), channel_id=1, source_target_pairs={{0,1},{1,0},{2,3},{3,2},{4,5},{5,4},{6,7},{7,6},{8,9},{9,8},{10,11... | collective-permute-start | bytes 196616 | tf_op jit(solution)/shard_map/ppermute | solution.py:28
  46.4 4.8 %collective-permute-start.19 = (bf16[128,256]{1,0:T(8,128)(2,1)S(1)}, bf16[128,256]{1,0:T(8,128)(2,1)S(1)}, u32[]{:S(2)}, u32[]{:S(2)}) collective-permute-start(bf16[128,256]{1,0:T(8,128)(2,1)S(1)} %get-tuple-element.103), channel_id=1, source_target_pairs={{0,1},{1,0},{2,3},{3,2},{4,5},{5,4},{6,7},{7,6},{8,9},{9,8},{10,11... | collective-permute-start | bytes 196616 | tf_op jit(solution)/shard_map/ppermute | solution.py:28
  46.8 4.4 %collective-permute-start.18 = (bf16[128,256]{1,0:T(8,128)(2,1)S(1)}, bf16[128,256]{1,0:T(8,128)(2,1)S(1)}, u32[]{:S(2)}, u32[]{:S(2)}) collective-permute-start(bf16[128,256]{1,0:T(8,128)(2,1)S(1)} %get-tuple-element.104), channel_id=1, source_target_pairs={{0,1},{1,0},{2,3},{3,2},{4,5},{5,4},{6,7},{7,6},{8,9},{9,8},{10,11... | collective-permute-start | bytes 196616 | tf_op jit(solution)/shard_map/ppermute | solution.py:28
  (5 other events, 50.6 us)

commit v5 on v3

--- a/solution.py
+++ b/solution.py
@@ -516,7 +516,7 @@
     xfar, xnear = flip(crosses, "col", 2), flip(crosses, "col", 1)
     bfar, bnear = flip(bottom, "col", 2), flip(bottom, "col", 1)
     tcorners = [flip(tfar[n : n + PAIR], "col", 1) for n in range(0, top.shape[0], PAIR)]
-    xfar, xnear, panel = hold((xfar, xnear, panel))
+    xfar, xnear, panel, tcorners = hold((xfar, xnear, panel, tcorners))
     xcorners = [flip(xfar[n : n + 2], "col", 1) for n in (0, 2)]
     first, second = begin((top, tnear, tfar), tcorners, pivot_inverse)
     first, second, xcorners = hold((first, second, xcorners))

time: 56.9 us -> 59.5 us (1.046)
  waiting for transfers between devices: 11.3 us -> 13.9 us
    ppermute x15, waiting for transfers between devices: 4.38 us -> 6.97 us  [flip(): return lax.ppermute(x, axis, [(i, i ^ bit) for i in range(n)])]
  transfers between devices with their start and end apart: 21 -> 21, of which waited for: 8 -> 8; matrix products, arithmetic and copies ran while one was open for 0% -> 0% of each run, Pallas kernels for 24% -> 23%
where the time goes in v5:
time: 59.5 us; the launch traced here: 59.4 us
  starting transfers between devices  24.2 us (41%)
  Pallas kernels  20.9 us (35%)
  waiting for transfers between devices  13.9 us (23%)
    ppermute x15, starting transfers between devices, flip(): return lax.ppermute(x, axis, [(i, i ^ bit) for i in range(n)])  14.7 us
    pallas_call x1, Pallas kernels, update(): pl.pallas_call(kernel, out_shape=(out(1, span, span), out(*panel.shape)),...  7.03 us
    ppermute x15, waiting for transfers between devices, flip(): return lax.ppermute(x, axis, [(i, i ^ bit) for i in range(n)])  6.97 us
    ppermute x5, starting transfers between devices, shift(): return lax.ppermute(x, axis, [(i, (i + step) % n) for i in range(n)])  6.93 us
    ppermute x5, waiting for transfers between devices, shift(): return lax.ppermute(x, axis, [(i, (i + step) % n) for i in range(n)])  6.93 us
    pallas_call x1, Pallas kernels, early(): pl.pallas_call(early_kernel, out_shape=out(PAIR, span - kept.shape[1]), i...  3.02 us
    pallas_call x1, Pallas kernels, multiply_top(): pl.pallas_call(kernel, out_shape=(out(span, 2 * P_SIZE), out(P_SIZE, P_SI...  2.76 us
    ppermute x1, starting transfers between devices, hand_on(): return lax.ppermute(x, ('row', 'col'), route)  2.59 us
  transfers between devices with their start and end apart: 21, of which 8 were waited for; matrix products, arithmetic and copies ran while one was open for 0% of the time, Pallas kernels for 23%

profile of v5, /device:TPU:1, one launch (start us, length us, event | category | flops | bytes accessed | tf_op | source)
XLA Modules:
  0.0 59.4 jit_solution(13446223486095547625)
XLA Ops:
  0.0 3.7 %collective-permute-start = (bf16[1,512,512]{2,1,0:T(8,128)(2,1)}, bf16[1,512,512]{2,1,0:T(8,128)(2,1)S(1)}, u32[]{:S(2)}, u32[]{:S(2)}) collective-permute-start(bf16[1,512,512]{2,1,0:T(8,128)(2,1)} %param.8), channel_id=1, source_target_pairs={{0,16},{16,0},{32,48},{48,32},{64,80},{80,64},{96,112},{112,96},{1... | collective-permute-start | bytes 1572872 | tf_op jit(solution)/shard_map/ppermute | solution.py:28
  3.7 3.0 %early.1.u0 = bf16[256,1024]{1,0:T(8,128)(2,1)} custom-call(s32[1,2,16]{2,1,0:T(2,128)} %map_s.7, s32[1,2,4]{2,1,0:T(2,128)} %piv_s.1, bf16[1,1536,1536]{2,1,0:T(8,128)(2,1)} %front.5, bf16[1,512,512]{2,1,0:T(8,128)(2,1)} %kept.5), custom_call_target="tpu_custom_call" | custom-call | flops 1000 | bytes 1000 | tf_op jit(solution)/shard_map/early/pallas_call | solution.py:133
  6.7 1.5 %collective-permute-start.2 = (bf16[256,1024]{1,0:T(8,128)(2,1)}, bf16[256,1024]{1,0:T(8,128)(2,1)S(1)}, u32[]{:S(2)}, u32[]{:S(2)}) collective-permute-start(bf16[256,1024]{1,0:T(8,128)(2,1)} %early.1.u0), channel_id=1, source_target_pairs={{0,4},{4,8},{8,12},{12,0},{1,5},{5,9},{9,13},{13,1},{2,6},{6,10},{... | collective-permute-start | bytes 1572872 | tf_op jit(solution)/shard_map/ppermute | solution.py:23
  8.2 1.4 %collective-permute-start.1 = (bf16[256,1024]{1,0:T(8,128)(2,1)}, bf16[256,1024]{1,0:T(8,128)(2,1)S(1)}, u32[]{:S(2)}, u32[]{:S(2)}) collective-permute-start(bf16[256,1024]{1,0:T(8,128)(2,1)} %early.1.u0), channel_id=1, source_target_pairs={{0,12},{4,0},{8,4},{12,8},{1,13},{5,1},{9,5},{13,9},{2,14},{6,2},{... | collective-permute-start | bytes 1572872 | tf_op jit(solution)/shard_map/ppermute | solution.py:23
  9.6 1.6 %prepare.1 = (f32[2,128,512]{2,1,0:T(8,128)S(1)}, f32[2,1536,128]{2,1,0:T(8,128)S(1)}) custom-call(s32[1,2,16]{2,1,0:T(2,128)S(1)} %copy-done.4, s32[1,2,4]{2,1,0:T(2,128)S(1)} %copy-done.5, bf16[1,1536,1536]{2,1,0:T(8,128)(2,1)S(1)} %copy-done, bf16[1,512,512]{2,1,0:T(8,128)(2,1)S(1)} %copy-done.2), custom_call_target="tpu_custom_call" | custom-call | flops 1000 | bytes 1000 | tf_op jit(solution)/shard_map/prepare/pallas_call | solution.py:180
  11.2 1.6 %base.1._ = f32[1536,1536]{1,0:T(8,128)S(1)} custom-call(s32[1,2,16]{2,1,0:T(2,128)S(1)} %copy-done.4, bf16[1,1536,1536]{2,1,0:T(8,128)(2,1)S(1)} %copy-done, bf16[1,512,512]{2,1,0:T(8,128)(2,1)S(1)} %copy-done.2), custom_call_target="tpu_custom_call" | custom-call | flops 1000 | bytes 1000 | tf_op jit(solution)/shard_map/base/pallas_call | solution.py:273
  12.8 1.8 %collective-permute-done.arrived = bf16[1,512,512]{2,1,0:T(8,128)(2,1)S(1)} collective-permute-done((bf16[1,512,512]{2,1,0:T(8,128)(2,1)}, bf16[1,512,512]{2,1,0:T(8,128)(2,1)S(1)}, u32[]{:S(2)}, u32[]{:S(2)}) %collective-permute-start) | collective-permute-done | bytes 524320 | tf_op jit(solution)/shard_map/ppermute | solution.py:28
  15.5 2.3 %collective-permute-start.7 = (bf16[1024,256]{1,0:T(8,128)(2,1)S(1)}, bf16[1024,256]{1,0:T(8,128)(2,1)S(1)}, u32[]{:S(2)}, u32[]{:S(2)}) collective-permute-start(bf16[1024,256]{1,0:T(8,128)(2,1)S(1)} %get-tuple-element.56.c0), channel_id=1, source_target_pairs={{0,1},{1,0},{2,3},{3,2},{4,5},{5,4},{6,7},{7,6},{8,9},{9,8},{10,11... | collective-permute-start | bytes 1572872 | tf_op jit(solution)/shard_map/ppermute | solution.py:28
  17.8 1.4 %collective-permute-start.6 = (bf16[1024,256]{1,0:T(8,128)(2,1)S(1)}, bf16[1024,256]{1,0:T(8,128)(2,1)S(1)}, u32[]{:S(2)}, u32[]{:S(2)}) collective-permute-start(bf16[1024,256]{1,0:T(8,128)(2,1)S(1)} %get-tuple-element.56.c0), channel_id=1, source_target_pairs={{0,2},{1,3},{2,0},{3,1},{4,6},{5,7},{6,4},{7,5},{8,10},{9,11},{10,... | collective-permute-start | bytes 1572872 | tf_op jit(solution)/shard_map/ppermute | solution.py:28
  19.2 1.3 %collective-permute-start.4 = (bf16[256,640]{1,0:T(8,128)(2,1)S(1)}, bf16[256,640]{1,0:T(8,128)(2,1)S(1)}, u32[]{:S(2)}, u32[]{:S(2)}) collective-permute-start(bf16[256,640]{1,0:T(8,128)(2,1)S(1)} %get-tuple-element.54.a0), channel_id=1, source_target_pairs={{0,4},{4,8},{8,12},{12,0},{1,5},{5,9},{9,13},{13,1},{2,6},{6,10},{... | collective-permute-start | bytes 983048 | tf_op jit(solution)/shard_map/ppermute | solution.py:23
  20.8 1.4 %collective-permute-start.3 = (bf16[256,640]{1,0:T(8,128)(2,1)S(1)}, bf16[256,640]{1,0:T(8,128)(2,1)S(1)}, u32[]{:S(2)}, u32[]{:S(2)}) collective-permute-start(bf16[256,640]{1,0:T(8,128)(2,1)S(1)} %get-tuple-element.54.a0), channel_id=1, source_target_pairs={{0,12},{4,0},{8,4},{12,8},{1,13},{5,1},{9,5},{13,9},{2,14},{6,2},{... | collective-permute-start | bytes 983048 | tf_op jit(solution)/shard_map/ppermute | solution.py:23
  22.2 1.4 %collective-permute-start.5 = (bf16[128,128]{1,0:T(8,128)(2,1)S(1)}, bf16[128,128]{1,0:T(8,128)(2,1)S(1)}, u32[]{:S(2)}, u32[]{:S(2)}) collective-permute-start(bf16[128,128]{1,0:T(8,128)(2,1)S(1)} %get-tuple-element.53), channel_id=1, source_target_pairs={{0,8},{4,12},{8,0},{12,4},{1,9},{5,13},{9,1},{13,5},{2,10},{6,14},... | collective-permute-start | bytes 98312 | tf_op jit(solution)/shard_map/ppermute | solution.py:23
  24.4 6.6 %collective-permute-done.5 = bf16[128,128]{1,0:T(8,128)(2,1)S(1)} collective-permute-done((bf16[128,128]{1,0:T(8,128)(2,1)S(1)}, bf16[128,128]{1,0:T(8,128)(2,1)S(1)}, u32[]{:S(2)}, u32[]{:S(2)}) %collective-permute-start.5) | collective-permute-done | bytes 32800 | tf_op jit(solution)/shard_map/ppermute | solution.py:23
  31.3 1.3 %collective-permute-start.9 = (bf16[4,128,128]{2,1,0:T(8,128)(2,1)S(1)}, bf16[4,128,128]{2,1,0:T(8,128)(2,1)S(1)}, u32[]{:S(2)}, u32[]{:S(2)}) collective-permute-start(bf16[4,128,128]{2,1,0:T(8,128)(2,1)S(1)} %pad_maximum_fusion.x0), channel_id=1, source_target_pairs={{0,1},{1,0},{2,3},{3,2},{4,5},{5,4},{6,7},{7,6},{8,9},{9,8},{10,11... | collective-permute-start | bytes 393224 | tf_op jit(solution)/shard_map/ppermute | solution.py:28
  32.6 1.1 %collective-permute-start.8 = (bf16[4,128,128]{2,1,0:T(8,128)(2,1)S(1)}, bf16[4,128,128]{2,1,0:T(8,128)(2,1)S(1)}, u32[]{:S(2)}, u32[]{:S(2)}) collective-permute-start(bf16[4,128,128]{2,1,0:T(8,128)(2,1)S(1)} %pad_maximum_fusion.x0), channel_id=1, source_target_pairs={{0,2},{1,3},{2,0},{3,1},{4,6},{5,7},{6,4},{7,5},{8,10},{9,11},{10,... | collective-permute-start | bytes 393224 | tf_op jit(solution)/shard_map/ppermute | solution.py:28
  35.1 2.6 %collective-permute-done.8.x2 = bf16[4,128,128]{2,1,0:T(8,128)(2,1)S(1)} collective-permute-done((bf16[4,128,128]{2,1,0:T(8,128)(2,1)S(1)}, bf16[4,128,128]{2,1,0:T(8,128)(2,1)S(1)}, u32[]{:S(2)}, u32[]{:S(2)}) %collective-permute-start.8) | collective-permute-done | bytes 131104 | tf_op jit(solution)/shard_map/ppermute | solution.py:28
  37.7 2.6 %collective-permute-start.20 = (bf16[256,1536]{1,0:T(8,128)(2,1)S(1)}, bf16[256,1536]{1,0:T(8,128)(2,1)S(1)}, u32[]{:S(2)}, u32[]{:S(2)}) collective-permute-start(bf16[256,1536]{1,0:T(8,128)(2,1)S(1)} %get-tuple-element.85), channel_id=1, source_target_pairs={{0,4},{1,13},{2,6},{3,15},{4,8},{5,1},{6,10},{7,3},{8,12},{9,5},{1... | collective-permute-start | bytes 2359304 | tf_op jit(solution)/shard_map/ppermute | solution.py:340
  40.3 1.3 %collective-permute-start.16 = (bf16[512,256]{1,0:T(8,128)(2,1)S(1)}, bf16[512,256]{1,0:T(8,128)(2,1)S(1)}, u32[]{:S(2)}, u32[]{:S(2)}) collective-permute-start(bf16[512,256]{1,0:T(8,128)(2,1)S(1)} %get-tuple-element.79.c0), channel_id=1, source_target_pairs={{0,2},{1,3},{2,0},{3,1},{4,6},{5,7},{6,4},{7,5},{8,10},{9,11},{10,... | collective-permute-start | bytes 786440 | tf_op jit(solution)/shard_map/ppermute | solution.py:28
  42.5 1.4 %begin.1 = (f32[1024,512]{1,0:T(8,128)S(1)}, bf16[1024,512]{1,0:T(8,128)(2,1)S(1)}) custom-call(bf16[1024,256]{1,0:T(8,128)(2,1)S(1)} %get-tuple-element.56.c0, bf16[1024,256]{1,0:T(8,128)(2,1)S(1)} %collective-permute-done.7.c1, bf16[1024,256]{1,0:T(8,128)(2,1)S(1)} %collective-permute-done.6.c2, bf16[256,256]{1,0:T(8,128)(2,1)S(1)} %collective-permute-done.10.rest_0_, ...), custom_call_target="tpu_custom_call" | custom-call | flops 1000 | bytes 1000 | tf_op jit(solution)/shard_map/begin/pallas_call | solution.py:359
  43.9 2.8 %multiply_top.1 = (bf16[1024,1024]{1,0:T(8,128)(2,1)S(1)}, bf16[512,512]{1,0:T(8,128)(2,1)S(1)}, bf16[512,512]{1,0:T(8,128)(2,1)S(1)}) custom-call(bf16[4,128,128]{2,1,0:T(8,128)(2,1)S(1)} %pad_maximum_fusion.x0, bf16[4,128,128]{2,1,0:T(8,128)(2,1)S(1)} %collective-permute-done.9.x1, bf16[4,128,128]{2,1,0:T(8,128)(2,1)S(1)} %collective-permute-done.8.x2, ...), custom_call_target="tpu_custom_call" | custom-call | flops 1000 | bytes 1000 | tf_op jit(solution)/shard_map/multiply_top/pallas_call | solution.py:403
  46.6 1.2 %collective-permute-done.16.c2 = bf16[512,256]{1,0:T(8,128)(2,1)S(1)} collective-permute-done((bf16[512,256]{1,0:T(8,128)(2,1)S(1)}, bf16[512,256]{1,0:T(8,128)(2,1)S(1)}, u32[]{:S(2)}, u32[]{:S(2)}) %collective-permute-start.16) | collective-permute-done | bytes 262176 | tf_op jit(solution)/shard_map/ppermute | solution.py:28
  47.9 1.3 %collective-permute-start.19 = (bf16[256,256]{1,0:T(8,128)(2,1)S(1)}, bf16[256,256]{1,0:T(8,128)(2,1)S(1)}, u32[]{:S(2)}, u32[]{:S(2)}) collective-permute-start(bf16[256,256]{1,0:T(8,128)(2,1)S(1)} %get-tuple-element.95), channel_id=1, source_target_pairs={{0,1},{1,0},{2,3},{3,2},{4,5},{5,4},{6,7},{7,6},{8,9},{9,8},{10,11... | collective-permute-start | bytes 393224 | tf_op jit(solution)/shard_map/ppermute | solution.py:28
  50.6 1.6 %multiply_bottom.1.bottom = bf16[512,1024]{1,0:T(8,128)(2,1)S(1)} custom-call(bf16[512,256]{1,0:T(8,128)(2,1)S(1)} %get-tuple-element.79.c0, bf16[512,256]{1,0:T(8,128)(2,1)S(1)} %collective-permute-done.17.c1, bf16[512,256]{1,0:T(8,128)(2,1)S(1)} %collective-permute-done.16.c2, bf16[256,256]{1,0:T(8,128)(2,1)S(1)} %collective-permute-done.18.k0, ...), custom_call_target="tpu_custom_call" | custom-call | flops 1000 | bytes 1000 | tf_op jit(solution)/shard_map/multiply_bottom/pallas_call | solution.py:431
  52.2 7.0 %update.1 = (bf16[1,1536,1536]{2,1,0:T(8,128)(2,1)}, bf16[1024,1536]{1,0:T(8,128)(2,1)S(1)}) custom-call(s32[1,2,16]{2,1,0:T(2,128)S(1)} %copy-done.4, bf16[1024,1024]{1,0:T(8,128)(2,1)S(1)} %get-tuple-element.80.top, bf16[512,1024]{1,0:T(8,128)(2,1)S(1)} %multiply_bottom.1.bottom, ...), custom_call_target="tpu_custom_call", output_to_operand_aliasing={{1}: (3, {})} | custom-call | flops 1000 | bytes 1000 | tf_op jit(solution)/shard_map/update/pallas_call | solution.py:479
  (45 shorter events, 6.0 us)
Async XLA Ops:
  0.0 9.6 %copy-start.2 = (bf16[1,512,512]{2,1,0:T(8,128)(2,1)S(1)}, bf16[1,512,512]{2,1,0:T(8,128)(2,1)}, u32[]{:S(2)}) copy-start(bf16[1,512,512]{2,1,0:T(8,128)(2,1)} %kept.5) | copy-start | bytes 1572868
  0.0 14.6 %collective-permute-start = (bf16[1,512,512]{2,1,0:T(8,128)(2,1)}, bf16[1,512,512]{2,1,0:T(8,128)(2,1)S(1)}, u32[]{:S(2)}, u32[]{:S(2)}) collective-permute-start(bf16[1,512,512]{2,1,0:T(8,128)(2,1)} %param.8), channel_id=1, source_target_pairs={{0,16},{16,0},{32,48},{48,32},{64,80},{80,64},{96,112},{112,96},{1... | collective-permute-start | bytes 1572872 | tf_op jit(solution)/shard_map/ppermute | solution.py:28
  6.7 14.1 %collective-permute-start.2 = (bf16[256,1024]{1,0:T(8,128)(2,1)}, bf16[256,1024]{1,0:T(8,128)(2,1)S(1)}, u32[]{:S(2)}, u32[]{:S(2)}) collective-permute-start(bf16[256,1024]{1,0:T(8,128)(2,1)} %early.1.u0), channel_id=1, source_target_pairs={{0,4},{4,8},{8,12},{12,0},{1,5},{5,9},{9,13},{13,1},{2,6},{6,10},{... | collective-permute-start | bytes 1572872 | tf_op jit(solution)/shard_map/ppermute | solution.py:23
  8.2 14.0 %collective-permute-start.1 = (bf16[256,1024]{1,0:T(8,128)(2,1)}, bf16[256,1024]{1,0:T(8,128)(2,1)S(1)}, u32[]{:S(2)}, u32[]{:S(2)}) collective-permute-start(bf16[256,1024]{1,0:T(8,128)(2,1)} %early.1.u0), channel_id=1, source_target_pairs={{0,12},{4,0},{8,4},{12,8},{1,13},{5,1},{9,5},{13,9},{2,14},{6,2},{... | collective-permute-start | bytes 1572872 | tf_op jit(solution)/shard_map/ppermute | solution.py:23
  15.5 15.5 %collective-permute-start.7 = (bf16[1024,256]{1,0:T(8,128)(2,1)S(1)}, bf16[1024,256]{1,0:T(8,128)(2,1)S(1)}, u32[]{:S(2)}, u32[]{:S(2)}) collective-permute-start(bf16[1024,256]{1,0:T(8,128)(2,1)S(1)} %get-tuple-element.56.c0), channel_id=1, source_target_pairs={{0,1},{1,0},{2,3},{3,2},{4,5},{5,4},{6,7},{7,6},{8,9},{9,8},{10,11... | collective-permute-start | bytes 1572872 | tf_op jit(solution)/shard_map/ppermute | solution.py:28
  17.8 13.5 %collective-permute-start.6 = (bf16[1024,256]{1,0:T(8,128)(2,1)S(1)}, bf16[1024,256]{1,0:T(8,128)(2,1)S(1)}, u32[]{:S(2)}, u32[]{:S(2)}) collective-permute-start(bf16[1024,256]{1,0:T(8,128)(2,1)S(1)} %get-tuple-element.56.c0), channel_id=1, source_target_pairs={{0,2},{1,3},{2,0},{3,1},{4,6},{5,7},{6,4},{7,5},{8,10},{9,11},{10,... | collective-permute-start | bytes 1572872 | tf_op jit(solution)/shard_map/ppermute | solution.py:28
  19.2 11.8 %collective-permute-start.4 = (bf16[256,640]{1,0:T(8,128)(2,1)S(1)}, bf16[256,640]{1,0:T(8,128)(2,1)S(1)}, u32[]{:S(2)}, u32[]{:S(2)}) collective-permute-start(bf16[256,640]{1,0:T(8,128)(2,1)S(1)} %get-tuple-element.54.a0), channel_id=1, source_target_pairs={{0,4},{4,8},{8,12},{12,0},{1,5},{5,9},{9,13},{13,1},{2,6},{6,10},{... | collective-permute-start | bytes 983048 | tf_op jit(solution)/shard_map/ppermute | solution.py:23
  20.8 10.2 %collective-permute-start.3 = (bf16[256,640]{1,0:T(8,128)(2,1)S(1)}, bf16[256,640]{1,0:T(8,128)(2,1)S(1)}, u32[]{:S(2)}, u32[]{:S(2)}) collective-permute-start(bf16[256,640]{1,0:T(8,128)(2,1)S(1)} %get-tuple-element.54.a0), channel_id=1, source_target_pairs={{0,12},{4,0},{8,4},{12,8},{1,13},{5,1},{9,5},{13,9},{2,14},{6,2},{... | collective-permute-start | bytes 983048 | tf_op jit(solution)/shard_map/ppermute | solution.py:23
  22.2 12.6 %copy-start.3 = (bf16[256,1024]{1,0:T(8,128)(2,1)S(1)}, bf16[256,1024]{1,0:T(8,128)(2,1)}, u32[]{:S(2)}) copy-start(bf16[256,1024]{1,0:T(8,128)(2,1)} %early.1.u0) | copy-start | bytes 1572868
  22.2 8.8 %collective-permute-start.5 = (bf16[128,128]{1,0:T(8,128)(2,1)S(1)}, bf16[128,128]{1,0:T(8,128)(2,1)S(1)}, u32[]{:S(2)}, u32[]{:S(2)}) collective-permute-start(bf16[128,128]{1,0:T(8,128)(2,1)S(1)} %get-tuple-element.53), channel_id=1, source_target_pairs={{0,8},{4,12},{8,0},{12,4},{1,9},{5,13},{9,1},{13,5},{2,10},{6,14},... | collective-permute-start | bytes 98312 | tf_op jit(solution)/shard_map/ppermute | solution.py:23
  24.4 18.1 %copy-start.1 = (bf16[1,2,512,512]{3,2,1,0:T(8,128)(2,1)S(1)}, bf16[1,2,512,512]{3,2,1,0:T(8,128)(2,1)}, u32[]{:S(2)}) copy-start(bf16[1,2,512,512]{3,2,1,0:T(8,128)(2,1)} %inverse.3) | copy-start | bytes 3145732
  31.3 3.4 %collective-permute-start.9 = (bf16[4,128,128]{2,1,0:T(8,128)(2,1)S(1)}, bf16[4,128,128]{2,1,0:T(8,128)(2,1)S(1)}, u32[]{:S(2)}, u32[]{:S(2)}) collective-permute-start(bf16[4,128,128]{2,1,0:T(8,128)(2,1)S(1)} %pad_maximum_fusion.x0), channel_id=1, source_target_pairs={{0,1},{1,0},{2,3},{3,2},{4,5},{5,4},{6,7},{7,6},{8,9},{9,8},{10,11... | collective-permute-start | bytes 393224 | tf_op jit(solution)/shard_map/ppermute | solution.py:28
  32.6 5.1 %collective-permute-start.8 = (bf16[4,128,128]{2,1,0:T(8,128)(2,1)S(1)}, bf16[4,128,128]{2,1,0:T(8,128)(2,1)S(1)}, u32[]{:S(2)}, u32[]{:S(2)}) collective-permute-start(bf16[4,128,128]{2,1,0:T(8,128)(2,1)S(1)} %pad_maximum_fusion.x0), channel_id=1, source_target_pairs={{0,2},{1,3},{2,0},{3,1},{4,6},{5,7},{6,4},{7,5},{8,10},{9,11},{10,... | collective-permute-start | bytes 393224 | tf_op jit(solution)/shard_map/ppermute | solution.py:28
  33.7 6.5 %collective-permute-start.13 = (bf16[256,256]{1,0:T(8,128)(2,1)S(1)}, bf16[256,256]{1,0:T(8,128)(2,1)S(1)}, u32[]{:S(2)}, u32[]{:S(2)}) collective-permute-start(bf16[256,256]{1,0:T(8,128)(2,1)S(1)} %get-tuple-element.91), channel_id=1, source_target_pairs={{0,1},{1,0},{2,3},{3,2},{4,5},{5,4},{6,7},{7,6},{8,9},{9,8},{10,11... | collective-permute-start | bytes 393224 | tf_op jit(solution)/shard_map/ppermute | solution.py:28
  34.2 6.1 %collective-permute-start.12 = (bf16[256,256]{1,0:T(8,128)(2,1)S(1)}, bf16[256,256]{1,0:T(8,128)(2,1)S(1)}, u32[]{:S(2)}, u32[]{:S(2)}) collective-permute-start(bf16[256,256]{1,0:T(8,128)(2,1)S(1)} %get-tuple-element.92), channel_id=1, source_target_pairs={{0,1},{1,0},{2,3},{3,2},{4,5},{5,4},{6,7},{7,6},{8,9},{9,8},{10,11... | collective-permute-start | bytes 393224 | tf_op jit(solution)/shard_map/ppermute | solution.py:28
  34.3 7.2 %collective-permute-start.11 = (bf16[256,256]{1,0:T(8,128)(2,1)S(1)}, bf16[256,256]{1,0:T(8,128)(2,1)S(1)}, u32[]{:S(2)}, u32[]{:S(2)}) collective-permute-start(bf16[256,256]{1,0:T(8,128)(2,1)S(1)} %get-tuple-element.93), channel_id=1, source_target_pairs={{0,1},{1,0},{2,3},{3,2},{4,5},{5,4},{6,7},{7,6},{8,9},{9,8},{10,11... | collective-permute-start | bytes 393224 | tf_op jit(solution)/shard_map/ppermute | solution.py:28
  34.7 6.9 %collective-permute-start.10 = (bf16[256,256]{1,0:T(8,128)(2,1)S(1)}, bf16[256,256]{1,0:T(8,128)(2,1)S(1)}, u32[]{:S(2)}, u32[]{:S(2)}) collective-permute-start(bf16[256,256]{1,0:T(8,128)(2,1)S(1)} %get-tuple-element.94), channel_id=1, source_target_pairs={{0,1},{1,0},{2,3},{3,2},{4,5},{5,4},{6,7},{7,6},{8,9},{9,8},{10,11... | collective-permute-start | bytes 393224 | tf_op jit(solution)/shard_map/ppermute | solution.py:28
  37.7 14.5 %collective-permute-start.20 = (bf16[256,1536]{1,0:T(8,128)(2,1)S(1)}, bf16[256,1536]{1,0:T(8,128)(2,1)S(1)}, u32[]{:S(2)}, u32[]{:S(2)}) collective-permute-start(bf16[256,1536]{1,0:T(8,128)(2,1)S(1)} %get-tuple-element.85), channel_id=1, source_target_pairs={{0,4},{1,13},{2,6},{3,15},{4,8},{5,1},{6,10},{7,3},{8,12},{9,5},{1... | collective-permute-start | bytes 2359304 | tf_op jit(solution)/shard_map/ppermute | solution.py:340
  40.3 6.3 %collective-permute-start.17 = (bf16[512,256]{1,0:T(8,128)(2,1)S(1)}, bf16[512,256]{1,0:T(8,128)(2,1)S(1)}, u32[]{:S(2)}, u32[]{:S(2)}) collective-permute-start(bf16[512,256]{1,0:T(8,128)(2,1)S(1)} %get-tuple-element.79.c0), channel_id=1, source_target_pairs={{0,1},{1,0},{2,3},{3,2},{4,5},{5,4},{6,7},{7,6},{8,9},{9,8},{10,11... | collective-permute-start | bytes 786440 | tf_op jit(solution)/shard_map/ppermute | solution.py:28
  40.3 7.6 %collective-permute-start.16 = (bf16[512,256]{1,0:T(8,128)(2,1)S(1)}, bf16[512,256]{1,0:T(8,128)(2,1)S(1)}, u32[]{:S(2)}, u32[]{:S(2)}) collective-permute-start(bf16[512,256]{1,0:T(8,128)(2,1)S(1)} %get-tuple-element.79.c0), channel_id=1, source_target_pairs={{0,2},{1,3},{2,0},{3,1},{4,6},{5,7},{6,4},{7,5},{8,10},{9,11},{10,... | collective-permute-start | bytes 786440 | tf_op jit(solution)/shard_map/ppermute | solution.py:28
  41.6 2.3 %collective-permute-start.15 = (bf16[2,128,128]{2,1,0:T(8,128)(2,1)S(1)}, bf16[2,128,128]{2,1,0:T(8,128)(2,1)S(1)}, u32[]{:S(2)}, u32[]{:S(2)}) collective-permute-start(bf16[2,128,128]{2,1,0:T(8,128)(2,1)S(1)} %get-tuple-element.97), channel_id=1, source_target_pairs={{0,1},{1,0},{2,3},{3,2},{4,5},{5,4},{6,7},{7,6},{8,9},{9,8},{10,11... | collective-permute-start | bytes 196616 | tf_op jit(solution)/shard_map/ppermute | solution.py:28
  42.4 1.5 %collective-permute-start.14 = (bf16[2,128,128]{2,1,0:T(8,128)(2,1)S(1)}, bf16[2,128,128]{2,1,0:T(8,128)(2,1)S(1)}, u32[]{:S(2)}, u32[]{:S(2)}) collective-permute-start(bf16[2,128,128]{2,1,0:T(8,128)(2,1)S(1)} %get-tuple-element.98), channel_id=1, source_target_pairs={{0,1},{1,0},{2,3},{3,2},{4,5},{5,4},{6,7},{7,6},{8,9},{9,8},{10,11... | collective-permute-start | bytes 196616 | tf_op jit(solution)/shard_map/ppermute | solution.py:28
  47.9 2.3 %collective-permute-start.19 = (bf16[256,256]{1,0:T(8,128)(2,1)S(1)}, bf16[256,256]{1,0:T(8,128)(2,1)S(1)}, u32[]{:S(2)}, u32[]{:S(2)}) collective-permute-start(bf16[256,256]{1,0:T(8,128)(2,1)S(1)} %get-tuple-element.95), channel_id=1, source_target_pairs={{0,1},{1,0},{2,3},{3,2},{4,5},{5,4},{6,7},{7,6},{8,9},{9,8},{10,11... | collective-permute-start | bytes 393224 | tf_op jit(solution)/shard_map/ppermute | solution.py:28
  49.2 1.3 %collective-permute-start.18 = (bf16[256,256]{1,0:T(8,128)(2,1)S(1)}, bf16[256,256]{1,0:T(8,128)(2,1)S(1)}, u32[]{:S(2)}, u32[]{:S(2)}) collective-permute-start(bf16[256,256]{1,0:T(8,128)(2,1)S(1)} %get-tuple-element.96), channel_id=1, source_target_pairs={{0,1},{1,0},{2,3},{3,2},{4,5},{5,4},{6,7},{7,6},{8,9},{9,8},{10,11... | collective-permute-start | bytes 393224 | tf_op jit(solution)/shard_map/ppermute | solution.py:28
  (3 other events, 28.8 us)
